TPU v7x, 256 devices: a whole 4x4x8 slice. The times are simulated.
256 devices in a mesh: section: 8 (over z_hi, x), dp: 32 (over z_lo, y, core).
Axes of the slice: x: 4, y: 4, z: 8 (z_hi: 2, z_lo: 4; z = z_hi * 4 + z_lo), core: 2. Of those that a mesh axis runs over, the one named last changes fastest.
Arguments:
- hidden: bfloat16 [8, 8192, 8192], P('section', 'dp'), may hold values from -64 to 64
- norm_gain: bfloat16 [8, 8192], P('section', 'dp'), may hold values from 0.099609375 to 1.8984375
- key_weight: bfloat16 [8, 8192, 512], P('section', 'dp'), may hold values from -0.0625 to 0.0625
- key_cotangent: bfloat16 [8, 8192, 512], P('section', 'dp'), may hold values from -24 to 24
- token_logratio: float32 [8, 8192], P('section', 'dp'), may hold values from -4 to 4
- lengths: int32 [8, 4], P('section'), may hold values from 512 to 2048
- pair_of_row: int32 [8, 4], P('section'), may hold values from 0 to 1, as said below
Outputs:
- upstream_cotangent: bfloat16 [8, 8192, 8192], P('section', 'dp')
- key_weight_grad: bfloat16 [8, 8192, 512], P('section', 'dp')
- gain_grad: bfloat16 [8, 8192], P('section', 'dp')
Inputs may be any that keep to these rules, and one draw needn't show every extreme that they name: `pair_of_row`: in each section every pair number appears once among the first 2 rows and once among the last 2 rows.
All inputs are finite; a program needn't handle non-finite values.
Results may differ from a plain program's by a relative error of at most 0.029.
Values may be sent and summed in bfloat16 or wider, within the bound.
No kernel may reach another device: no remote copies, remote signals or barrier semaphores. Data moves between devices by JAX's collectives and lax.ppermute only.
A program may use at most 128 MiB of HBM per device.

v0:
```python
import jax
import jax.numpy as jnp
from jax import lax
from jax.sharding import PartitionSpec as P

ROW_LEN = 2048


DPO_BETA = 0.1


def passed_along(value, axis, steps):
    count = lax.axis_size(axis)
    first, last = (max(0, -steps), min(count, count - steps))
    return lax.ppermute(value, axis, [(source, source + steps) for source in range(first, last)])


def pair_coefficients(row_ratio, pairing, pair_count):
    row_total = row_ratio.shape[0]
    signs = jnp.where(jnp.arange(row_total) < pair_count, 1.0, -1.0).astype(jnp.float32)
    pair_hot = (pairing[:, None] == jnp.arange(pair_count, dtype=jnp.int32)[None, :]).astype(
        jnp.float32
    )
    margin = jnp.sum(pair_hot * (signs * row_ratio)[:, None], axis=0)
    row_margin = jnp.sum(pair_hot * margin[None, :], axis=1)
    return -DPO_BETA * signs * jax.nn.sigmoid(-DPO_BETA * row_margin)


def on_device(hidden, norm_gain, key_weight, key_cotangent, token_logratio, lengths, pair_of_row):
    states = hidden[0]
    gains = norm_gain[0]
    weights = key_weight[0]
    key_in = key_cotangent[0]
    ratios = token_logratio[0]
    limits = lengths[0]
    pairing = pair_of_row[0]
    local_tokens = states.shape[0]
    row_total = limits.shape[0]
    first_token = lax.axis_index("dp") * local_tokens
    places = first_token + jnp.arange(local_tokens, dtype=jnp.int32)
    row_ids = places // ROW_LEN
    offsets = places % ROW_LEN
    member = row_ids[:, None] == jnp.arange(row_total, dtype=jnp.int32)[None, :]
    limit_tok = jnp.sum(jnp.where(member, limits[None, :], 0), axis=1)
    valid = (offsets < limit_tok).astype(jnp.float32)
    partial_ratio = jnp.sum(jnp.where(member, (valid * ratios)[:, None], 0.0), axis=0)
    row_ratio = lax.psum(partial_ratio, "dp")
    coef_rows = pair_coefficients(row_ratio, pairing, row_total // 2)
    token_weight = valid * jnp.sum(jnp.where(member, coef_rows[None, :], 0.0), axis=1)
    hidden32 = states.astype(jnp.float32)
    inv_rms = lax.rsqrt(jnp.mean(hidden32 * hidden32, axis=1, keepdims=True) + 1e-06)
    unit = hidden32 * inv_rms
    key_grad = (key_in.astype(jnp.float32) * token_weight[:, None]).astype(jnp.bfloat16)
    full_weight, full_gain = (
        lax.all_gather(weights, "dp", axis=0, tiled=True),
        lax.all_gather(gains, "dp", axis=0, tiled=True),
    )
    gain32 = full_gain.astype(jnp.float32)
    normed = (unit * gain32[None, :]).astype(jnp.bfloat16)
    normed_grad = lax.dot_general(
        key_grad, full_weight, (((1,), (1,)), ((), ())), preferred_element_type=jnp.float32
    ).astype(jnp.bfloat16)
    weight_term = lax.dot_general(
        normed, key_grad, (((0,), (0,)), ((), ())), preferred_element_type=jnp.float32
    )
    gain_term = jnp.sum(normed_grad.astype(jnp.float32) * unit, axis=0)
    weight_share, gain_share = (
        lax.psum_scatter(
            weight_term.astype(jnp.bfloat16), "dp", scatter_dimension=0, tiled=True
        ).astype(jnp.float32),
        lax.psum_scatter(
            gain_term.astype(jnp.bfloat16), "dp", scatter_dimension=0, tiled=True
        ).astype(jnp.float32),
    )
    unit_grad = normed_grad.astype(jnp.float32) * gain32[None, :]
    inner = jnp.mean(unit_grad * unit, axis=1, keepdims=True)
    section_grad = (inv_rms * (unit_grad - unit * inner)).astype(jnp.bfloat16)
    arriving = passed_along(section_grad, "section", -1)
    return (
        arriving[None],
        weight_share.astype(jnp.bfloat16)[None],
        gain_share.astype(jnp.bfloat16)[None],
    )


def solution(mesh):
    in_specs = (
        P("section", "dp", None),
        P("section", "dp"),
        P("section", "dp", None),
        P("section", "dp", None),
        P("section", "dp"),
        P("section", None),
        P("section", None),
    )
    out_specs = (P("section", "dp", None), P("section", "dp", None), P("section", "dp"))
    return jax.shard_map(
        on_device, mesh=mesh, in_specs=in_specs, out_specs=out_specs, check_vma=False
    )
```

profile of v0, /device:TPU:128, one launch (start us, length us, event | category | flops | bytes accessed | tf_op | source)
XLA Modules:
  0.0 492.2 jit_solution(4584231819467687664)
XLA Ops:
  7.2 0.0 all-gather.4.cloned.1.call-start
  7.2 0.7 all-gather.4.cloned.1.call-update
  7.9 0.0 reduce-scatter.2.cloned.1.call-start
  8.0 0.7 select_reduce_fusion.2
  8.7 0.7 broadcast_select_fusion.1
  9.4 0.1 select_reduce_fusion.1
  9.5 72.3 %psum.7 = f32[4]{0:T(128)S(1)} all-reduce(f32[4]{0:T(128)S(1)} %select_reduce_fusion.1), channel_id=1, replica_groups=mesh['section'=8,'dp'=32] {'dp'}, use_global_device_ids=true, to_apply=%region_3.4 | all-reduce | flops 4 | bytes 32 | tf_op jit(solution)/shard_map/psum | solution.py:47
  81.8 37.9 %all-gather.1 = bf16[1,8192]{1,0:T(2,128)(2,1)S(1)} all-gather(bf16[1,256]{1,0:T(2,128)(2,1)} %param.8), channel_id=3, replica_groups=mesh['section'=8,'dp'=32] {'dp'}, dimensions={1}, use_global_device_ids=true | all-gather | bytes 16896 | tf_op jit(solution)/shard_map/all_gather | solution.py:56
  119.8 0.8 select_reduce_fusion.4
  120.6 0.7 select_reduce_fusion.3
  121.3 0.1 select_reduce_fusion
  121.4 3.1 fusion.10
  124.5 8.2 %convolution_convert_fusion = bf16[8192,512]{1,0:T(8,128)(2,1)} fusion(bf16[1,256,8192]{2,1,0:T(8,128)(2,1)} %param.7, f32[8192]{0:T(1024)S(1)} %bitcast.47, f32[256]{0:T(256)S(1)} %get-tuple-element.6, bf16[1,256,512]{2,1,0:T(8,128)(2,1)} %param.10, f32[256]{0:T(256)S(1)} %get-tuple-element.7), kind=kOutput, calls=%fused_computation | convolution fusion | flops 2160459776 | bytes 12879872 | tf_op jit(solution)/shard_map/dot_general | solution.py:63
  132.7 0.0 reduce-scatter.2.cloned.1.call-update
  132.7 0.0 all-gather.4.cloned.1.call-done
  132.8 0.9 copy-done.1
  133.7 10.3 %fusion.9 = (bf16[8192]{0:T(1024)(128)(2,1)S(1)}, f32[256]{0:T(256)S(1)}, bf16[256,8192]{1,0:T(8,128)(2,1)S(1)}) fusion(bf16[1,256,8192]{2,1,0:T(8,128)(2,1)} %param.7, f32[256]{0:T(256)S(1)} %get-tuple-element.6, f32[8192]{0:T(1024)S(1)} %bitcast.48, bf16[1,8192,512]{2,1,0:T(8,128)(2,1)} %all-gather.4.cloned.1.call-done, ...), kind=kOutput, calls=%fused_computation.14 | convolution fusion | flops 2166742784 | bytes 17091584 | tf_op jit(solution)/shard_map/dot_general | solution.py:60
  144.0 3.6 fusion.7
  147.6 5.6 %collective-permute-start = (bf16[256,8192]{1,0:T(8,128)(2,1)}, bf16[256,8192]{1,0:T(8,128)(2,1)}, u32[]{:S(2)}, u32[]{:S(2)}) collective-permute-start(bf16[256,8192]{1,0:T(8,128)(2,1)} %fusion.7), channel_id=1, source_target_pairs={{32,0},{64,32},{96,64},{128,96},{160,128},{192,160},{224,192},{33,... | collective-permute-start | bytes 12582920 | tf_op jit(solution)/shard_map/ppermute | solution.py:15
  153.2 0.6 dynamic-slice
  154.4 325.6 %all-reduce = bf16[8192]{0:T(1024)(128)(2,1)S(1)} all-reduce(bf16[8192]{0:T(1024)(128)(2,1)S(1)} %get-tuple-element.3), channel_id=5, replica_groups=mesh['section'=8,'dp'=32] {'dp'}, use_global_device_ids=true, to_apply=%region_10.11.clone | all-reduce | flops 8192 | bytes 32768
  480.1 0.1 dynamic-slice.1
  480.2 0.6 broadcast_in_dim.75
  480.7 4.6 copy.11
  (13 shorter events, 0.1 us)
Async XLA Ops:
  7.2 125.6 %all-gather.4.cloned.1.call-start = ((), (), s32[]{:S(2)}) async-start(), calls=%async_computation.2 | async-start | bytes 8650752 | tf_op jit(solution)/shard_map/all_gather | solution.py:55
  7.9 472.8 %reduce-scatter.2.cloned.1.call-start = ((), (), s32[]{:S(2)}) async-start(), calls=%async_computation.1 | async-start | bytes 8650752 | tf_op jit(solution)/shard_map/reduce_scatter | solution.py:68
  132.7 0.9 copy-start.1
  133.7 10.3 %copy-start = (bf16[1,256,8192]{2,1,0:T(8,128)(2,1)S(1)}, bf16[1,256,8192]{2,1,0:T(8,128)(2,1)}, u32[]{:S(2)}) copy-start(bf16[1,256,8192]{2,1,0:T(8,128)(2,1)} %param.7) | copy-start | bytes 12582916
  144.0 9.2 %copy-start.2 = (u32[256]{0:T(256)S(1)}, u32[256]{0:T(256)}, u32[]{:S(2)}) copy-start(u32[256]{0:T(256)} %constant.65) | copy-start | bytes 3076
  147.6 333.1 %collective-permute-start = (bf16[256,8192]{1,0:T(8,128)(2,1)}, bf16[256,8192]{1,0:T(8,128)(2,1)}, u32[]{:S(2)}, u32[]{:S(2)}) collective-permute-start(bf16[256,8192]{1,0:T(8,128)(2,1)} %fusion.7), channel_id=1, source_target_pairs={{32,0},{64,32},{96,64},{128,96},{160,128},{192,160},{224,192},{33,... | collective-permute-start | bytes 12582920 | tf_op jit(solution)/shard_map/ppermute | solution.py:15
Sparse Core Ops, SparseCore 0:
  9.9 69.2 all-gather.3
  132.8 227.5 reduce-scatter.1
where the time goes:
time: 493 us; the launch traced here: 492 us
  blocking collectives  436 us (88%)
  matrix products  18.5 us (4%)
  between operations  14.8 us (3%)
  other arithmetic  9.95 us (2%)
  local copies, waits for them, and re-layouts  6.78 us (1%)
  starting transfers between devices  5.65 us (1%)
    unnamed x1, blocking collectives  326 us
    psum x1, blocking collectives, on_device(): row_ratio = lax.psum(partial_ratio, 'dp')  72.3 us
    all_gather x1, blocking collectives, on_device(): lax.all_gather(gains, 'dp', axis=0, tiled=True)  37.9 us
    dot_general x1, matrix products, on_device(): lax.dot_general(key_grad, full_weight, (((1,), (1,)), ((), ())), preferre...  10.3 us
  transfers between devices with their start and end apart: 3, of which 0 were waited for; matrix products, arithmetic and copies ran while one was open for 6% of the time, Pallas kernels for 0%

commit v1 on v0

v1 whole, which is shorter than its diff:
```python
import functools
import jax
import jax.numpy as jnp
from jax import lax
from jax.experimental import pallas as pl
from jax.experimental.pallas import tpu as pltpu
from jax.sharding import PartitionSpec as P

ROW_LEN = 2048
DPO_BETA = 0.1
EPS = 1e-06
AXES = ("section", "dp")
BF, F32 = jnp.bfloat16, jnp.float32
BLK = 256
PIECE = 16
FREE = pl.CostEstimate(flops=0, bytes_accessed=0, transcendentals=0)
EXTRA = 16
OWN = 16
VMEM_LIMIT = 56 * 1024 * 1024


def index_of(z_hi, x, z_lo, y, core):
    return ((z_hi * 4 + x) * 4 + z_lo) * 8 + y * 2 + core


def moved(value, target):
    pairs = []
    for z_hi in range(2):
        for x in range(4):
            for z_lo in range(4):
                for y in range(4):
                    for core in range(2):
                        goal = target(z_hi, x, z_lo, y, core)
                        if goal is not None:
                            pairs.append((index_of(z_hi, x, z_lo, y, core), index_of(*goal)))
    return lax.ppermute(value, AXES, pairs)


def to_previous(value):
    def target(z_hi, x, z_lo, y, core):
        section = z_hi * 4 + x - 1
        return None if section < 0 else (section // 4, section % 4, z_lo, y, core)

    return moved(value, target)


ANYWHERE = pl.BlockSpec(memory_space=pl.ANY)


def gated(values, events):
    count = len(values)
    return pl.pallas_call(
        lambda *refs: None,
        in_specs=[ANYWHERE] * (count + len(events)),
        out_specs=[ANYWHERE] * count,
        out_shape=[jax.ShapeDtypeStruct(v.shape, v.dtype) for v in values],
        input_output_aliases={i: i for i in range(count)},
        cost_estimate=FREE,
    )(*values, *events)


def stepped(value, source, goal):
    return moved(
        value,
        lambda z_hi, x, z_lo, y, core: (*goal, z_lo, y, core) if (z_hi, x) == source else None,
    )


def lowered_part(value, event):
    return moved(
        gated([value], [event])[0],
        lambda z_hi, x, z_lo, y, core: (z_hi, x - 1, z_lo, y, core) if x else None,
    )


def prepare_kernel(place, limits, pairs, weights, gains, keys, ratios, out, mark):
    tokens, kw = keys.shape
    out[:tokens, :] = (weights[...].astype(F32) * gains[...].astype(F32)).astype(BF)
    limit = limits[place[2]] - place[3]
    valid = lax.broadcasted_iota(jnp.int32, (tokens, kw), 0) < limit
    out[tokens + EXTRA :, :] = jnp.where(valid, keys[...], jnp.zeros_like(keys))
    kept = lax.broadcasted_iota(jnp.int32, ratios.shape, 1) < limit
    partial = jnp.sum(jnp.where(kept, ratios[...], 0.0), axis=1, keepdims=True)
    high = partial.astype(BF).astype(F32)
    middle = (partial - high).astype(BF).astype(F32)
    terms = [high, middle, partial - high - middle]
    lane = lax.broadcasted_iota(jnp.int32, (EXTRA, kw), 1)
    line = lax.broadcasted_iota(jnp.int32, (EXTRA, kw), 0)
    sums = jnp.zeros((EXTRA, kw), F32)
    own = jnp.zeros((EXTRA, kw), F32)
    for i, term in enumerate(terms):
        sums = jnp.where(lane == i, term, sums)
        own = jnp.where(lane == OWN + i, term, own)
    for i in range(4):
        sums = jnp.where(lane == 3 + i, pairs[i].astype(F32), sums)
    out[tokens : tokens + EXTRA, :] = jnp.where(line == 0, sums, 0.0).astype(BF)
    mark[...] = jnp.where(line == 0, own, 0.0).astype(BF)


def prepared(place, limits, pairs, weights, gains, keys, ratios):
    tokens, kw = keys.shape
    scalar = pl.BlockSpec(memory_space=pltpu.SMEM)
    whole = pl.BlockSpec(memory_space=pltpu.VMEM)
    return pl.pallas_call(
        prepare_kernel,
        in_specs=[scalar] * 3 + [whole] * 4,
        out_specs=[whole] * 2,
        out_shape=[
            jax.ShapeDtypeStruct((2 * tokens + EXTRA, kw), BF),
            jax.ShapeDtypeStruct((EXTRA, kw), BF),
        ],
    )(place, limits, pairs, weights, gains, keys, ratios)


def join_kernel(payload, mark, out):
    rows = out.shape[0]
    out[: rows - EXTRA, :] = payload[: rows - EXTRA, :]
    out[rows - EXTRA :, :] = payload[rows - EXTRA : rows, :] + mark[...]


def joined(payload, mark):
    rows, kw = (payload.shape[0] + EXTRA) // 2, payload.shape[1]
    whole = pl.BlockSpec(memory_space=pltpu.VMEM)
    return pl.pallas_call(
        join_kernel,
        in_specs=[whole] * 2,
        out_specs=whole,
        out_shape=jax.ShapeDtypeStruct((rows, kw), BF),
        cost_estimate=FREE,
    )(payload, mark)


def coefficients(ratios, pairs):
    signs = [1.0, 1.0, -1.0, -1.0]
    out = []
    for row in range(4):
        margin = jnp.zeros_like(ratios[0])
        for other in range(4):
            margin += jnp.where(pairs[other] == pairs[row], signs[other] * ratios[other], 0.0)
        out.append(-DPO_BETA * signs[row] / (1.0 + jnp.exp(DPO_BETA * margin)))
    return out


def coef_kernel(place, pairs, gathered, out, notes, sem):
    copy = pltpu.make_async_copy(
        gathered.at[:, pl.ds(gathered.shape[1] - EXTRA, EXTRA)], notes, sem
    )
    copy.start()
    copy.wait()
    row = place[2]
    values = jnp.sum(notes[...].astype(F32).reshape(4, -1, EXTRA, notes.shape[2]), axis=1)

    def ratios(first):
        picked = values[:, :1, first : first + 3]
        return [jnp.sum(picked[r], axis=1, keepdims=True) for r in range(4)]

    first = notes[0, :1, :16].astype(F32)
    own = coefficients(ratios(OWN), [pairs[i].astype(F32) for i in range(4)])
    following = coefficients(ratios(0), [first[:, 3 + i : 4 + i] for i in range(4)])
    lane = lax.broadcasted_iota(jnp.int32, out.shape, 1)
    result = jnp.zeros(out.shape, F32)
    for r in range(4):
        result = jnp.where(lane == lax.rem(row - r + 4, 4), own[r], result)
        result = jnp.where((lane == 4) & (row == r), following[r], result)
    out[...] = result


def coef_table(place, pairs, gathered):
    scalar = pl.BlockSpec(memory_space=pltpu.SMEM)
    return pl.pallas_call(
        coef_kernel,
        in_specs=[scalar, scalar, ANYWHERE],
        out_specs=pl.BlockSpec(memory_space=pltpu.VMEM),
        out_shape=jax.ShapeDtypeStruct((8, 128), F32),
        scratch_shapes=[
            pltpu.VMEM((gathered.shape[0], EXTRA, gathered.shape[2]), BF),
            pltpu.SemaphoreType.DMA,
        ],
        cost_estimate=FREE,
    )(place, pairs, gathered)


def finish_kernel(coefs, first, second, third, fourth, gains, weights, out, sums):
    total = first[...] * coefs[:1, :1]
    for i, wave in enumerate((second, third, fourth)):
        total += wave[...].astype(F32) * coefs[:1, i + 1 : i + 2]
    out[...] = (total * gains[...].astype(F32)).astype(BF)
    sums[...] = jnp.sum(total * weights[...].astype(F32), axis=1, keepdims=True)


def finished(coefs, waves, gains, weights):
    whole = pl.BlockSpec(memory_space=pltpu.VMEM)
    rows, kw = weights.shape
    return pl.pallas_call(
        finish_kernel,
        in_specs=[whole] * 7,
        out_specs=[whole] * 2,
        out_shape=[jax.ShapeDtypeStruct((rows, kw), BF), jax.ShapeDtypeStruct((rows, 1), F32)],
        cost_estimate=FREE,
    )(coefs, *waves, gains, weights)


ORDER = (2, 1, 3, 0)


def block_products(spot, other, hidden, keys, terms, out, sem):
    y, z = spot[1], spot[2]
    core = 1 - spot[0] if other else spot[0]
    for r in ORDER:

        def block(q, carry):
            at = lax.rem(z + q, 4) * 8 + lax.rem(y + r, 4) * 2 + core
            columns = hidden[:, pl.ds(pl.multiple_of(at * BLK, BLK), BLK)]
            terms[r, q] = lax.dot_general(
                columns, keys[...], (((0,), (0,)), ((), ())), preferred_element_type=F32
            ).astype(BF)
            return carry

        lax.fori_loop(0, 4, block, 0)
        pltpu.make_async_copy(terms.at[r], out.at[r], sem.at[r]).start()
    for r in ORDER:
        pltpu.make_async_copy(terms.at[r], out.at[r], sem.at[r]).wait()


def load(source, target, sem, parts):
    rows = source.shape[0] // parts
    copies = []
    for i in range(parts):
        at = pl.ds(i * rows, rows)
        copies.append(pltpu.make_async_copy(source.at[at], target.at[at], sem.at[i]))
        copies[-1].start()
    return copies


def send_kernel(spot, payload, hidden, *refs):
    out, keys, states, terms, in_sem, out_sem = refs
    parts = 4
    rows = states.shape[0] // parts
    for i, copy in enumerate(load(hidden, states, in_sem, parts)):
        copy.wait()

        def line(j, carry):
            at = pl.ds(pl.multiple_of(i * rows + j * 16, 16), 16)
            square = jnp.zeros((16, 512), F32)
            for c in range(0, states.shape[1], 512):
                part = states[at, c : c + 512].astype(F32)
                square = square + part * part
            inv = lax.rsqrt(jnp.sum(square, axis=1, keepdims=True) / states.shape[1] + EPS)
            from_key = pl.ds(pl.multiple_of(states.shape[0] + EXTRA + i * rows + j * 16, 16), 16)
            keys[at, :] = (payload[from_key, :].astype(F32) * inv).astype(BF)
            return carry

        lax.fori_loop(0, rows // 16, line, 0)
    block_products(spot, True, states, keys, terms, out, out_sem)


def keep_kernel(spot, keys, hidden, *refs):
    out, states, terms, in_sem, out_sem = refs
    for copy in load(hidden, states, in_sem, 4):
        copy.wait()
    block_products(spot, False, states, keys, terms, out, out_sem)


def term_call(kernel, states, kw, more):
    tokens, width = states.shape
    whole = pl.BlockSpec(memory_space=pltpu.VMEM)
    return pl.pallas_call(
        kernel,
        in_specs=[pl.BlockSpec(memory_space=pltpu.SMEM), whole, ANYWHERE],
        out_specs=[ANYWHERE] + [whole] * len(more),
        out_shape=[jax.ShapeDtypeStruct((4, 4, BLK, kw), BF)] + more,
        scratch_shapes=[
            pltpu.VMEM((tokens, width), BF),
            pltpu.VMEM((4, 4, BLK, kw), BF),
            pltpu.SemaphoreType.DMA((4,)),
            pltpu.SemaphoreType.DMA((4,)),
        ],
        compiler_params=pltpu.CompilerParams(vmem_limit_bytes=VMEM_LIMIT),
        cost_estimate=pl.CostEstimate(
            flops=tokens * width * kw, bytes_accessed=width * (tokens + kw) * 2, transcendentals=0
        ),
    )


def around(value, steps):
    return moved(value, lambda z_hi, x, z_lo, y, core: (z_hi, x, z_lo, (y + steps) % 4, core))


def along(value, steps):
    return moved(value, lambda z_hi, x, z_lo, y, core: (z_hi, x, (z_lo + steps) % 4, y, core))


def added(*parts):
    return sum(part.astype(F32) for part in parts)


def grad_kernel(payload, weights, out):
    keys = payload[payload.shape[0] - out.shape[0] :, :]
    for i in range(weights.shape[0]):
        out[:, i * BLK : (i + 1) * BLK] = lax.dot_general(
            keys, weights[i, :BLK], (((1,), (1,)), ((), ())), preferred_element_type=F32
        ).astype(BF)


def unit_grads(payload, gathered, tokens):
    count, rows, kw = gathered.shape
    step = 4
    return pl.pallas_call(
        grad_kernel,
        grid=(count // step,),
        in_specs=[
            pl.BlockSpec(payload.shape, lambda i: (0, 0)),
            pl.BlockSpec((step, rows, kw), lambda i: (i, 0, 0)),
        ],
        out_specs=pl.BlockSpec((tokens, step * BLK), lambda i: (0, i)),
        out_shape=jax.ShapeDtypeStruct((tokens, count * BLK), BF),
        compiler_params=pltpu.CompilerParams(vmem_limit_bytes=VMEM_LIMIT),
        cost_estimate=FREE,
    )(payload, gathered)


def section_kernel(near_rows, far_rows, scale, is_far, slopes, *refs):
    count = len(near_rows)
    near, far = refs[:count], refs[count : count + len(far_rows)]
    out, rows, grads, done, row_sem, grad_sem, out_sem = refs[count + len(far_rows) :]
    tokens, width = rows.shape
    group, span = 16, 512
    parts = tokens // PIECE

    def fetched(sources, sizes):
        first = 0
        for source, size in zip(sources, sizes):
            for at in range(0, size, PIECE):
                spot = (first + at) // PIECE
                pltpu.make_async_copy(
                    source.at[pl.ds(at, PIECE)], rows.at[pl.ds(first + at, PIECE)], row_sem.at[spot]
                ).start()
            first += size

    def whole(i):
        return pl.ds(pl.multiple_of(i * PIECE, PIECE), PIECE)

    for i in range(parts):
        at = pl.ds(i * PIECE, PIECE)
        pltpu.make_async_copy(slopes.at[at], grads.at[at], grad_sem.at[i]).start()

    @pl.when(is_far[0] == 1)
    def _():
        fetched(far, far_rows)

    @pl.when(is_far[0] != 1)
    def _():
        fetched(near, near_rows)

    factor = scale[:1, 4:5]

    def part(i, carry):
        at = whole(i)
        pltpu.make_async_copy(slopes.at[at], grads.at[at], grad_sem.at[i]).wait()
        pltpu.make_async_copy(slopes.at[at], rows.at[at], row_sem.at[i]).wait()
        for g in range(PIECE // group):
            line = pl.ds(pl.multiple_of(i * PIECE + g * group, group), group)
            square = jnp.zeros((group, span), F32)
            cross = jnp.zeros((group, span), F32)
            for c in range(0, width, span):
                h = rows[line, c : c + span].astype(F32)
                square = square + h * h
                cross = cross + h * grads[line, c : c + span].astype(F32)
            inv = lax.rsqrt(jnp.sum(square, axis=1, keepdims=True) / width + EPS)
            inner = jnp.sum(cross, axis=1, keepdims=True) / width * inv * factor
            ahead, back = inv * factor, inv * inv * inner
            for c in range(0, width, span):
                h = rows[line, c : c + span].astype(F32)
                u = grads[line, c : c + span].astype(F32)
                done[line, c : c + span] = (ahead * u - back * h).astype(BF)
        pltpu.make_async_copy(done.at[at], out.at[at], out_sem.at[i]).start()
        return carry

    lax.fori_loop(0, parts, part, 0)
    for i in range(parts):
        at = pl.ds(i * PIECE, PIECE)
        pltpu.make_async_copy(done.at[at], out.at[at], out_sem.at[i]).wait()


def section_grads(scale, is_far, slopes, near, far):
    tokens, width = slopes.shape
    scalar = pl.BlockSpec(memory_space=pltpu.SMEM)
    near_rows, far_rows = [v.shape[0] for v in near], [v.shape[0] for v in far]
    parts = tokens // PIECE
    return pl.pallas_call(
        functools.partial(section_kernel, near_rows, far_rows),
        in_specs=[pl.BlockSpec(memory_space=pltpu.VMEM), scalar] + [ANYWHERE] * (1 + len(near) + len(far)),
        out_specs=ANYWHERE,
        out_shape=jax.ShapeDtypeStruct((tokens, width), BF),
        scratch_shapes=[pltpu.VMEM((tokens, width), BF)] * 3
        + [pltpu.SemaphoreType.DMA((parts,))] * 3,
        compiler_params=pltpu.CompilerParams(vmem_limit_bytes=VMEM_LIMIT),
        cost_estimate=FREE,
    )(scale, is_far, slopes, *near, *far)


def on_device(hidden, norm_gain, key_weight, key_cotangent, token_logratio, lengths, pair_of_row):
    states = hidden[0]
    weights = key_weight[0]
    tokens, width = states.shape
    kw = weights.shape[1]
    section, dp = lax.axis_index("section"), lax.axis_index("dp")
    core, y, z = dp % 2, (dp // 2) % 4, dp // 8
    place = jnp.stack([core, y, z, (dp * tokens) % ROW_LEN]).astype(jnp.int32)
    gains = norm_gain[0][:, None]

    payload, mark = prepared(
        place, lengths[0], pair_of_row[0], weights, gains, key_cotangent[0], token_logratio
    )
    following = to_previous(payload)
    up, low = (1, 0), (0, 3)
    early = stepped(states[:48], up, (1, 3))
    near_last = to_previous(states[128:])
    late = stepped(states[48:128], up, (1, 3))

    send, keys = term_call(send_kernel, states, kw, [jax.ShapeDtypeStruct((tokens, kw), BF)])(
        place, payload, states
    )
    following, early = gated([following, early], [keys])
    joint = joined(following, mark)
    gathered = lax.all_gather(joint, "dp", axis=0, tiled=True)
    gathered = gathered.reshape(-1, tokens + EXTRA, kw)
    last = [stepped(early, (1, 3), low)]

    def over_cores(operands):
        states, keys, place, send, _ = operands
        swapped = moved(send, lambda z_hi, x, z_lo, y, core: (z_hi, x, z_lo, y, 1 - core))
        keep = term_call(keep_kernel, states, kw, [])(place, keys, states)[0]
        far = added(keep[2], swapped[2]).astype(BF)
        far_up, far_down = around(far[:2], 1), around(far[2:], -1)
        sums = added(keep, swapped).astype(BF)
        up_terms = jnp.concatenate([added(sums[1, :2], far_up).astype(BF), sums[1, 2:]])
        down_terms = jnp.concatenate([sums[3, :2], added(sums[3, 2:], far_down).astype(BF)])
        return sums[0], up_terms, down_terms

    def over_chips(operands):
        here, up_terms, down_terms = operands
        plane = added(here, around(up_terms, 1), around(down_terms, -1))
        first, second = along(plane[1].astype(BF), 1), along(plane[2].astype(BF), 2)
        third = gated([plane[3].astype(BF)], [first])[0]
        return plane[0], first, second, along(third, 3)

    def staged(step, operands):
        shapes = jax.eval_shape(step, operands)
        blank = lambda _: jax.tree.map(lambda v: jnp.zeros(v.shape, v.dtype), shapes)
        return lax.cond(dp < tokens, step, blank, operands)

    sums = staged(over_cores, (states, keys, place, send, joint))
    late = gated([late], [sums[0]])[0]
    last.append(stepped(late, (1, 3), low))
    near_first = lowered_part(states[:128], sums[0])
    waves = staged(over_chips, sums)

    coefs = coef_table(place, pair_of_row[0], gathered)
    weight_grad, gain_grad = finished(coefs, waves, gains, weights)

    slopes = unit_grads(following, gathered, tokens)
    is_far = (section == 3).astype(jnp.int32)[None]
    out = section_grads(coefs, is_far, slopes, [near_first, near_last], [*last, near_last])
    return out[None], weight_grad[None], gain_grad.astype(BF).reshape(1, -1)


def solution(mesh):
    in_specs = (
        P("section", "dp", None),
        P("section", "dp"),
        P("section", "dp", None),
        P("section", "dp", None),
        P("section", "dp"),
        P("section", None),
        P("section", None),
    )
    out_specs = (P("section", "dp", None), P("section", "dp", None), P("section", "dp"))
    return jax.shard_map(
        on_device, mesh=mesh, in_specs=in_specs, out_specs=out_specs, check_vma=False
    )
```

time: 493 us -> 263 us (0.53)
  the two profiles are of different devices: /device:TPU:128 before, /device:TPU:224 now
where the time goes in v1:
time: 263 us; the launch traced here: 262 us
  waiting for transfers between devices  147 us (56%)
  Pallas kernels  43.1 us (16%)
  starting transfers between devices  33.8 us (13%)
  local copies, waits for them, and re-layouts  15.8 us (6%)
  between operations  14.2 us (5%)
  other arithmetic  7.81 us (3%)
    ppermute x15, waiting for transfers between devices, moved(): return lax.ppermute(value, AXES, pairs)  147 us
    ppermute x15, starting transfers between devices, moved(): return lax.ppermute(value, AXES, pairs)  33.7 us
    pallas_call x1, Pallas kernels, on_device(): term_call(send_kernel, states, kw, [jax.ShapeDtypeStruct((tokens, kw), BF)])  9.35 us
    pallas_call x1, Pallas kernels, unit_grads(): pl.pallas_call(grad_kernel, grid=(count // step,), in_specs=[pl.BlockSpec...  9.31 us
    pallas_call x1, Pallas kernels, over_cores(): keep = term_call(keep_kernel, states, kw, [])(place, keys, states)[0]  7.92 us
    pallas_call x1, Pallas kernels, section_grads(): pl.pallas_call(functools.partial(section_kernel, near_rows, far_rows), in...  7.68 us
  transfers between devices with their start and end apart: 16, of which 7 were waited for; matrix products, arithmetic and copies ran while one was open for 8% of the time, Pallas kernels for 13%

profile of v1, /device:TPU:224, one launch (start us, length us, event | category | flops | bytes accessed | tf_op | source)
XLA Modules:
  0.0 262.1 jit_solution(17983008883327516056)
XLA Ops:
  8.4 4.7 %collective-permute-start.9 = (bf16[48,8192]{1,0:T(8,128)(2,1)S(1)}, bf16[48,8192]{1,0:T(8,128)(2,1)S(1)}, u32[]{:S(2)}, u32[]{:S(2)}) collective-permute-start(bf16[48,8192]{1,0:T(8,128)(2,1)S(1)} %slice_bitcast_fusion.14), channel_id=1, source_target_pairs={{128,224},{129,225},{130,226},{131,227},{132,228},{133,229},{134,2... | collective-permute-start | bytes 2359304 | tf_op jit(solution)/shard_map/ppermute | solution.py:36
  14.7 2.0 shard_map.94
  16.7 1.9 collective-permute-start.8
  18.6 9.3 %shard_map.95 = (bf16[4,4,256,512]{3,2,1,0:T(8,128)(2,1)}, bf16[256,512]{1,0:T(8,128)(2,1)S(1)}) custom-call(s32[4]{0:T(128)S(1)} %pad_add_fusion.place.spot, bf16[528,512]{1,0:T(8,128)(2,1)} %get-tuple-element.37.payload, bf16[256,8192]{1,0:T(8,128)(2,1)} %bitcast.50), custom_call_target="tpu_custom_call" | custom-call | flops 1073741824 | bytes 12582912 | tf_op jit(solution)/shard_map/pallas_call | solution.py:421
  27.9 4.6 %collective-permute-done.8.refs_0_ = bf16[528,512]{1,0:T(8,128)(2,1)S(1)} collective-permute-done((bf16[528,512]{1,0:T(8,128)(2,1)}, bf16[528,512]{1,0:T(8,128)(2,1)S(1)}, u32[]{:S(2)}, u32[]{:S(2)}) %collective-permute-start.8) | collective-permute-done | bytes 540704 | tf_op jit(solution)/shard_map/ppermute | solution.py:36
  35.4 2.5 slice_bitcast_fusion.13
  37.9 3.9 %collective-permute-start.13 = (bf16[80,8192]{1,0:T(8,128)(2,1)}, bf16[80,8192]{1,0:T(8,128)(2,1)}, u32[]{:S(2)}, u32[]{:S(2)}) collective-permute-start(bf16[80,8192]{1,0:T(8,128)(2,1)} %slice_bitcast_fusion.13), channel_id=1, source_target_pairs={{128,224},{129,225},{130,226},{131,227},{132,228},{133,229},{134,2... | collective-permute-start | bytes 3932168 | tf_op jit(solution)/shard_map/ppermute | solution.py:36
  41.7 4.7 %slice_bitcast_fusion.11 = (bf16[128,8192]{1,0:T(8,128)(2,1)}, bf16[128,8192]{1,0:T(8,128)(2,1)}) fusion(bf16[1,256,8192]{2,1,0:T(8,128)(2,1)} %param.11), kind=kLoop, calls=%fused_computation.20 | loop fusion | bytes 8388608 | tf_op jit(solution)/shard_map/slice | solution.py:418
  46.4 38.6 %conditional.2 = (bf16[4,256,512]{2,1,0:T(8,128)(2,1)S(1)}, bf16[4,256,512]{2,1,0:T(8,128)(2,1)}, bf16[4,256,512]{2,1,0:T(8,128)(2,1)}) conditional(s32[]{:T(128)} %convert_element_type.73, () %tuple.23, (s32[4]{0:T(128)S(1)}, bf16[256,512]{1,0:T(8,128)(2,1)S(1)}, bf16[256,8192]{1,0:T(8,128)(2,1)}, bf16[4,4,256,512]{3,2,1,0:T(8,128)(2,1)}) %tuple.41), branch_computations={%region_0.1_spmd, %region_1.2_spmd} | conditional | flops 1087373312 | bytes 79691944 | solution.py:451
  46.4 7.9 %branch_1_fun.2 = bf16[4,4,256,512]{3,2,1,0:T(8,128)(2,1)} custom-call(s32[4]{0:T(128)S(1)} %get-tuple-element.14.spot, bf16[256,512]{1,0:T(8,128)(2,1)S(1)} %get-tuple-element.15.keys, bf16[256,8192]{1,0:T(8,128)(2,1)} %get-tuple-element.16.hidden), custom_call_target="tpu_custom_call" | custom-call | flops 1073741824 | bytes 12582912 | tf_op jit(solution)/shard_map/cond/branch_1_fun/pallas_call | solution.py:433
  61.0 20.0 %collective-permute-done.1 = bf16[2,256,512]{2,1,0:T(8,128)(2,1)S(1)} collective-permute-done((bf16[2,256,512]{2,1,0:T(8,128)(2,1)S(1)}, bf16[2,256,512]{2,1,0:T(8,128)(2,1)S(1)}, u32[]{:S(2)}, u32[]{:S(2)}) %collective-permute-start.1) | collective-permute-done | bytes 524320 | tf_op jit(solution)/shard_map/cond/branch_1_fun/ppermute | solution.py:36
  81.0 2.2 collective-permute-done.2
  86.3 7.5 %collective-permute-start.11 = (bf16[128,8192]{1,0:T(8,128)(2,1)}, bf16[128,8192]{1,0:T(8,128)(2,1)S(1)}, u32[]{:S(2)}, u32[]{:S(2)}) collective-permute-start(bf16[128,8192]{1,0:T(8,128)(2,1)} %get-tuple-element.63), channel_id=1, source_target_pairs={{32,0},{33,1},{34,2},{35,3},{36,4},{37,5},{38,6},{39,7},{40,8},{41... | collective-permute-start | bytes 6291464 | tf_op jit(solution)/shard_map/ppermute | solution.py:36
  95.6 133.7 %conditional.3 = (f32[256,512]{1,0:T(8,128)}, bf16[256,512]{1,0:T(8,128)(2,1)}, bf16[256,512]{1,0:T(8,128)(2,1)}, bf16[256,512]{1,0:T(8,128)(2,1)}) conditional(s32[]{:T(128)} %convert_element_type.73, () %tuple.25, (bf16[4,256,512]{2,1,0:T(8,128)(2,1)S(1)}, bf16[4,256,512]{2,1,0:T(8,128)(2,1)}, bf16[4,256,512]{2,1,0:T(8,128)(2,1)}) %conditional.2), branch_computations={%region_2.3_spmd, %region_3.4_spmd} | conditional | flops 3145728 | bytes 20447464 | solution.py:451
  98.8 25.2 %collective-permute-done.3 = bf16[4,256,512]{2,1,0:T(8,128)(2,1)S(1)} collective-permute-done((bf16[4,256,512]{2,1,0:T(8,128)(2,1)}, bf16[4,256,512]{2,1,0:T(8,128)(2,1)S(1)}, u32[]{:S(2)}, u32[]{:S(2)}) %collective-permute-start.3) | collective-permute-done | bytes 1048608 | tf_op jit(solution)/shard_map/cond/branch_1_fun/ppermute | solution.py:36
  124.0 4.8 %collective-permute-done.4 = bf16[4,256,512]{2,1,0:T(8,128)(2,1)S(1)} collective-permute-done((bf16[4,256,512]{2,1,0:T(8,128)(2,1)}, bf16[4,256,512]{2,1,0:T(8,128)(2,1)S(1)}, u32[]{:S(2)}, u32[]{:S(2)}) %collective-permute-start.4) | collective-permute-done | bytes 1048608 | tf_op jit(solution)/shard_map/cond/branch_1_fun/ppermute | solution.py:36
  132.8 4.1 %collective-permute-start.6 = (bf16[256,512]{1,0:T(8,128)(2,1)S(1)}, bf16[256,512]{1,0:T(8,128)(2,1)}, u32[]{:S(2)}, u32[]{:S(2)}) collective-permute-start(bf16[256,512]{1,0:T(8,128)(2,1)S(1)} %get-tuple-element.61), channel_id=1, source_target_pairs={{0,16},{1,17},{2,18},{3,19},{4,20},{5,21},{6,22},{7,23},{8,24},{9,... | collective-permute-start | bytes 786440 | tf_op jit(solution)/shard_map/cond/branch_1_fun/ppermute | solution.py:36
  136.9 82.3 %collective-permute-done.5.refs_1_ = bf16[256,512]{1,0:T(8,128)(2,1)} collective-permute-done((bf16[256,512]{1,0:T(8,128)(2,1)S(1)}, bf16[256,512]{1,0:T(8,128)(2,1)}, u32[]{:S(2)}, u32[]{:S(2)}) %collective-permute-start.5) | collective-permute-done | bytes 262176 | tf_op jit(solution)/shard_map/cond/branch_1_fun/ppermute | solution.py:36
  219.2 1.9 slice_bitcast_fusion.7
  221.1 8.2 %collective-permute-done.7 = bf16[256,512]{1,0:T(8,128)(2,1)} collective-permute-done((bf16[256,512]{1,0:T(8,128)(2,1)}, bf16[256,512]{1,0:T(8,128)(2,1)}, u32[]{:S(2)}, u32[]{:S(2)}) %collective-permute-start.7) | collective-permute-done | bytes 262176 | tf_op jit(solution)/shard_map/cond/branch_1_fun/ppermute | solution.py:36
  230.0 2.6 %shard_map.98.scale.coefs = f32[8,128]{1,0:T(8,128)} custom-call(s32[4]{0:T(128)S(1)} %pad_add_fusion.place.spot, s32[4]{0:T(128)} %bitcast.59, bf16[32,272,512]{2,1,0:T(8,128)(2,1)} %bitcast.52), custom_call_target="tpu_custom_call" | custom-call | tf_op jit(solution)/shard_map/pallas_call | solution.py:170
  232.7 9.3 %shard_map.99.slopes = bf16[256,8192]{1,0:T(8,128)(2,1)} custom-call(bf16[528,512]{1,0:T(8,128)(2,1)} %get-tuple-element.39.payload, bf16[32,272,512]{2,1,0:T(8,128)(2,1)} %bitcast.53), custom_call_target="tpu_custom_call" | custom-call | tf_op jit(solution)/shard_map/pallas_call | solution.py:308
  242.0 2.4 shard_map.103
  247.6 7.7 %shard_map.102 = bf16[256,8192]{1,0:T(8,128)(2,1)} custom-call(f32[8,128]{1,0:T(8,128)} %shard_map.98.scale.coefs, s32[1]{0:T(128)} %bitcast.25.is_far, bf16[256,8192]{1,0:T(8,128)(2,1)} %shard_map.99.slopes, bf16[128,8192]{1,0:T(8,128)(2,1)} %collective-permute-done.10.refs_0_, bf16[128,8192]{1,0:T(8,128)(2,1)} %copy-done.1, bf16[48,8192]{1,0:T(8,128)(2,1)} %copy-done.3, ...), custom_call_target="tpu_custom_call" | custom-call | tf_op jit(solution)/shard_map/pallas_call | solution.py:390
  (50 shorter events, 28.1 us)
Async XLA Ops:
  7.2 222.8 %all-gather.2.cloned.1.call-start = ((), (), s32[]{:S(2)}) async-start(), calls=%async_computation | async-start | bytes 9191424 | tf_op jit(solution)/shard_map/all_gather | solution.py:426
  8.4 24.1 %collective-permute-start.9 = (bf16[48,8192]{1,0:T(8,128)(2,1)S(1)}, bf16[48,8192]{1,0:T(8,128)(2,1)S(1)}, u32[]{:S(2)}, u32[]{:S(2)}) collective-permute-start(bf16[48,8192]{1,0:T(8,128)(2,1)S(1)} %slice_bitcast_fusion.14), channel_id=1, source_target_pairs={{128,224},{129,225},{130,226},{131,227},{132,228},{133,229},{134,2... | collective-permute-start | bytes 2359304 | tf_op jit(solution)/shard_map/ppermute | solution.py:36
  16.7 15.8 %collective-permute-start.8 = (bf16[528,512]{1,0:T(8,128)(2,1)}, bf16[528,512]{1,0:T(8,128)(2,1)S(1)}, u32[]{:S(2)}, u32[]{:S(2)}) collective-permute-start(bf16[528,512]{1,0:T(8,128)(2,1)} %get-tuple-element.37.payload), channel_id=1, source_target_pairs={{32,0},{33,1},{34,2},{35,3},{36,4},{37,5},{38,6},{39,7},{40,8},{41... | collective-permute-start | bytes 1622024 | tf_op jit(solution)/shard_map/ppermute | solution.py:36
  32.5 0.8 copy-start.2
  32.5 1.1 copy-start.4
  37.9 55.9 %collective-permute-start.13 = (bf16[80,8192]{1,0:T(8,128)(2,1)}, bf16[80,8192]{1,0:T(8,128)(2,1)}, u32[]{:S(2)}, u32[]{:S(2)}) collective-permute-start(bf16[80,8192]{1,0:T(8,128)(2,1)} %slice_bitcast_fusion.13), channel_id=1, source_target_pairs={{128,224},{129,225},{130,226},{131,227},{132,228},{133,229},{134,2... | collective-permute-start | bytes 3932168 | tf_op jit(solution)/shard_map/ppermute | solution.py:36
  46.4 7.9 %collective-permute-start = (bf16[4,4,256,512]{3,2,1,0:T(8,128)(2,1)}, bf16[4,4,256,512]{3,2,1,0:T(8,128)(2,1)S(1)}, u32[]{:S(2)}, u32[]{:S(2)}) collective-permute-start(bf16[4,4,256,512]{3,2,1,0:T(8,128)(2,1)} %get-tuple-element.17), channel_id=1, source_target_pairs={{0,1},{1,0},{2,3},{3,2},{4,5},{5,4},{6,7},{7,6},{8,9},{9,8},{10,11... | collective-permute-start | bytes 12582920 | tf_op jit(solution)/shard_map/cond/branch_1_fun/ppermute | solution.py:36
  54.3 5.1 %copy-start = (bf16[4,4,256,512]{3,2,1,0:T(8,128)(2,1)S(1)}, bf16[4,4,256,512]{3,2,1,0:T(8,128)(2,1)}, u32[]{:S(2)}) copy-start(bf16[4,4,256,512]{3,2,1,0:T(8,128)(2,1)} %branch_1_fun.2) | copy-start | bytes 12582916 | tf_op jit(solution)/shard_map/cond
  56.1 24.9 %collective-permute-start.1 = (bf16[2,256,512]{2,1,0:T(8,128)(2,1)S(1)}, bf16[2,256,512]{2,1,0:T(8,128)(2,1)S(1)}, u32[]{:S(2)}, u32[]{:S(2)}) collective-permute-start(bf16[2,256,512]{2,1,0:T(8,128)(2,1)S(1)} %get-tuple-element.57), channel_id=1, source_target_pairs={{0,2},{1,3},{2,4},{3,5},{4,6},{5,7},{6,0},{7,1},{8,10},{9,11},{10,... | collective-permute-start | bytes 1572872 | tf_op jit(solution)/shard_map/cond/branch_1_fun/ppermute | solution.py:36
  57.7 25.4 %collective-permute-start.2 = (bf16[2,256,512]{2,1,0:T(8,128)(2,1)S(1)}, bf16[2,256,512]{2,1,0:T(8,128)(2,1)S(1)}, u32[]{:S(2)}, u32[]{:S(2)}) collective-permute-start(bf16[2,256,512]{2,1,0:T(8,128)(2,1)S(1)} %get-tuple-element.56), channel_id=1, source_target_pairs={{0,6},{1,7},{2,0},{3,1},{4,2},{5,3},{6,4},{7,5},{8,14},{9,15},{10,... | collective-permute-start | bytes 1572872 | tf_op jit(solution)/shard_map/cond/branch_1_fun/ppermute | solution.py:36
  85.0 161.0 %collective-permute-start.10 = (bf16[128,8192]{1,0:T(8,128)(2,1)}, bf16[128,8192]{1,0:T(8,128)(2,1)}, u32[]{:S(2)}, u32[]{:S(2)}) collective-permute-start(bf16[128,8192]{1,0:T(8,128)(2,1)} %shard_map.100), channel_id=1, source_target_pairs={{32,0},{33,1},{34,2},{35,3},{36,4},{37,5},{38,6},{39,7},{40,8},{41... | collective-permute-start | bytes 6291464 | tf_op jit(solution)/shard_map/ppermute | solution.py:36
  86.3 159.8 %collective-permute-start.11 = (bf16[128,8192]{1,0:T(8,128)(2,1)}, bf16[128,8192]{1,0:T(8,128)(2,1)S(1)}, u32[]{:S(2)}, u32[]{:S(2)}) collective-permute-start(bf16[128,8192]{1,0:T(8,128)(2,1)} %get-tuple-element.63), channel_id=1, source_target_pairs={{32,0},{33,1},{34,2},{35,3},{36,4},{37,5},{38,6},{39,7},{40,8},{41... | collective-permute-start | bytes 6291464 | tf_op jit(solution)/shard_map/ppermute | solution.py:36
  93.8 152.2 %collective-permute-start.14 = (bf16[80,8192]{1,0:T(8,128)(2,1)}, bf16[80,8192]{1,0:T(8,128)(2,1)}, u32[]{:S(2)}, u32[]{:S(2)}) collective-permute-start(bf16[80,8192]{1,0:T(8,128)(2,1)} %shard_map.101), channel_id=1, source_target_pairs={{224,96},{225,97},{226,98},{227,99},{228,100},{229,101},{230,102},... | collective-permute-start | bytes 3932168 | tf_op jit(solution)/shard_map/ppermute | solution.py:36
  95.6 28.5 %collective-permute-start.3 = (bf16[4,256,512]{2,1,0:T(8,128)(2,1)}, bf16[4,256,512]{2,1,0:T(8,128)(2,1)S(1)}, u32[]{:S(2)}, u32[]{:S(2)}) collective-permute-start(bf16[4,256,512]{2,1,0:T(8,128)(2,1)} %get-tuple-element.19), channel_id=1, source_target_pairs={{0,2},{1,3},{2,4},{3,5},{4,6},{5,7},{6,0},{7,1},{8,10},{9,11},{10,... | collective-permute-start | bytes 3145736 | tf_op jit(solution)/shard_map/cond/branch_1_fun/ppermute | solution.py:36
  97.1 31.7 %collective-permute-start.4 = (bf16[4,256,512]{2,1,0:T(8,128)(2,1)}, bf16[4,256,512]{2,1,0:T(8,128)(2,1)S(1)}, u32[]{:S(2)}, u32[]{:S(2)}) collective-permute-start(bf16[4,256,512]{2,1,0:T(8,128)(2,1)} %get-tuple-element.20), channel_id=1, source_target_pairs={{0,6},{1,7},{2,0},{3,1},{4,2},{5,3},{6,4},{7,5},{8,14},{9,15},{10,... | collective-permute-start | bytes 3145736 | tf_op jit(solution)/shard_map/cond/branch_1_fun/ppermute | solution.py:36
  131.5 87.7 %collective-permute-start.5 = (bf16[256,512]{1,0:T(8,128)(2,1)S(1)}, bf16[256,512]{1,0:T(8,128)(2,1)}, u32[]{:S(2)}, u32[]{:S(2)}) collective-permute-start(bf16[256,512]{1,0:T(8,128)(2,1)S(1)} %get-tuple-element.62), channel_id=1, source_target_pairs={{0,8},{1,9},{2,10},{3,11},{4,12},{5,13},{6,14},{7,15},{8,16},{9,17... | collective-permute-start | bytes 786440 | tf_op jit(solution)/shard_map/cond/branch_1_fun/ppermute | solution.py:36
  132.8 88.3 %collective-permute-start.6 = (bf16[256,512]{1,0:T(8,128)(2,1)S(1)}, bf16[256,512]{1,0:T(8,128)(2,1)}, u32[]{:S(2)}, u32[]{:S(2)}) collective-permute-start(bf16[256,512]{1,0:T(8,128)(2,1)S(1)} %get-tuple-element.61), channel_id=1, source_target_pairs={{0,16},{1,17},{2,18},{3,19},{4,20},{5,21},{6,22},{7,23},{8,24},{9,... | collective-permute-start | bytes 786440 | tf_op jit(solution)/shard_map/cond/branch_1_fun/ppermute | solution.py:36
  219.2 10.1 %collective-permute-start.7 = (bf16[256,512]{1,0:T(8,128)(2,1)}, bf16[256,512]{1,0:T(8,128)(2,1)}, u32[]{:S(2)}, u32[]{:S(2)}) collective-permute-start(bf16[256,512]{1,0:T(8,128)(2,1)} %branch_1_fun.3), channel_id=1, source_target_pairs={{0,24},{1,25},{2,26},{3,27},{4,28},{5,29},{6,30},{7,31},{8,0},{9,1... | collective-permute-start | bytes 786440 | tf_op jit(solution)/shard_map/cond/branch_1_fun/ppermute | solution.py:36
  229.3 16.7 %collective-permute-start.12 = (bf16[48,8192]{1,0:T(8,128)(2,1)}, bf16[48,8192]{1,0:T(8,128)(2,1)S(1)}, u32[]{:S(2)}, u32[]{:S(2)}) collective-permute-start(bf16[48,8192]{1,0:T(8,128)(2,1)} %get-tuple-element.43), channel_id=1, source_target_pairs={{224,96},{225,97},{226,98},{227,99},{228,100},{229,101},{230,102},... | collective-permute-start | bytes 2359304 | tf_op jit(solution)/shard_map/ppermute | solution.py:36
  246.0 0.9 copy-start.3
  246.0 1.5 copy-start.1
Sparse Core Ops, SparseCore 0:
  35.5 158.1 all-gather.1

commit v2 on v1

--- a/solution.py
+++ b/solution.py
@@ -15,6 +15,7 @@
 PIECE = 16
 FREE = pl.CostEstimate(flops=0, bytes_accessed=0, transcendentals=0)
 EXTRA = 16
+QUARTER = 64
 OWN = 16
 VMEM_LIMIT = 56 * 1024 * 1024
 
@@ -66,10 +67,9 @@
     )
 
 
-def lowered_part(value, event):
+def lowered(value):
     return moved(
-        gated([value], [event])[0],
-        lambda z_hi, x, z_lo, y, core: (z_hi, x - 1, z_lo, y, core) if x else None,
+        value, lambda z_hi, x, z_lo, y, core: (z_hi, x - 1, z_lo, y, core) if x else None
     )
 
 
@@ -233,7 +233,7 @@
 
 
 def send_kernel(spot, payload, hidden, *refs):
-    out, keys, states, terms, in_sem, out_sem = refs
+    out, *quarters, keys, states, terms, in_sem, out_sem, row_sem = refs
     parts = 4
     rows = states.shape[0] // parts
     for i, copy in enumerate(load(hidden, states, in_sem, parts)):
@@ -251,7 +251,15 @@
             return carry
 
         lax.fori_loop(0, rows // 16, line, 0)
+    copies = [
+        pltpu.make_async_copy(states.at[pl.ds(i * QUARTER, QUARTER)], quarter, row_sem.at[i])
+        for i, quarter in enumerate(quarters)
+    ]
+    for copy in copies:
+        copy.start()
     block_products(spot, True, states, keys, terms, out, out_sem)
+    for copy in copies:
+        copy.wait()
 
 
 def keep_kernel(spot, keys, hidden, *refs):
@@ -261,25 +269,27 @@
     block_products(spot, False, states, keys, terms, out, out_sem)
 
 
-def term_call(kernel, states, kw, more):
-    tokens, width = states.shape
+def term_call(kernel, operands, more):
+    tokens, width = operands[2].shape
+    kw = operands[1].shape[1]
     whole = pl.BlockSpec(memory_space=pltpu.VMEM)
+    rows = [jax.ShapeDtypeStruct((QUARTER, width), BF)] * 4
+    keys = jax.ShapeDtypeStruct((tokens, kw), BF)
     return pl.pallas_call(
         kernel,
         in_specs=[pl.BlockSpec(memory_space=pltpu.SMEM), whole, ANYWHERE],
-        out_specs=[ANYWHERE] + [whole] * len(more),
-        out_shape=[jax.ShapeDtypeStruct((4, 4, BLK, kw), BF)] + more,
+        out_specs=[ANYWHERE] + ([ANYWHERE] * 4 + [whole] if more else []),
+        out_shape=[jax.ShapeDtypeStruct((4, 4, BLK, kw), BF)] + ([*rows, keys] if more else []),
         scratch_shapes=[
             pltpu.VMEM((tokens, width), BF),
             pltpu.VMEM((4, 4, BLK, kw), BF),
             pltpu.SemaphoreType.DMA((4,)),
             pltpu.SemaphoreType.DMA((4,)),
-        ],
+        ]
+        + ([pltpu.SemaphoreType.DMA((4,))] if more else []),
         compiler_params=pltpu.CompilerParams(vmem_limit_bytes=VMEM_LIMIT),
-        cost_estimate=pl.CostEstimate(
-            flops=tokens * width * kw, bytes_accessed=width * (tokens + kw) * 2, transcendentals=0
-        ),
-    )
+        cost_estimate=FREE,
+    )(*operands)
 
 
 def around(value, steps):
@@ -413,27 +423,26 @@
         place, lengths[0], pair_of_row[0], weights, gains, key_cotangent[0], token_logratio
     )
     following = to_previous(payload)
-    up, low = (1, 0), (0, 3)
-    early = stepped(states[:48], up, (1, 3))
-    near_last = to_previous(states[128:])
-    late = stepped(states[48:128], up, (1, 3))
-
-    send, keys = term_call(send_kernel, states, kw, [jax.ShapeDtypeStruct((tokens, kw), BF)])(
-        place, payload, states
-    )
-    following, early = gated([following, early], [keys])
+
+    send, *quarters, keys = term_call(send_kernel, (place, payload, states), True)
+    following = gated([following], [keys])[0]
     joint = joined(following, mark)
+    send = gated([send], [joint])[0]
     gathered = lax.all_gather(joint, "dp", axis=0, tiled=True)
     gathered = gathered.reshape(-1, tokens + EXTRA, kw)
-    last = [stepped(early, (1, 3), low)]
+    near = lowered(states)
+    up = (1, 0)
+    spread = [stepped(quarter, up, (1, x + 1)) for x, quarter in enumerate(quarters[1:])]
 
     def over_cores(operands):
-        states, keys, place, send, _ = operands
+        states, keys, place, send = operands
         swapped = moved(send, lambda z_hi, x, z_lo, y, core: (z_hi, x, z_lo, y, 1 - core))
-        keep = term_call(keep_kernel, states, kw, [])(place, keys, states)[0]
-        far = added(keep[2], swapped[2]).astype(BF)
-        far_up, far_down = around(far[:2], 1), around(far[2:], -1)
-        sums = added(keep, swapped).astype(BF)
+        keep = term_call(keep_kernel, (place, keys, states), False)[0]
+        return added(keep, swapped).astype(BF)
+
+    def over_far_chips(operands):
+        sums = operands
+        far_up, far_down = around(sums[2, :2], 1), around(sums[2, 2:], -1)
         up_terms = jnp.concatenate([added(sums[1, :2], far_up).astype(BF), sums[1, 2:]])
         down_terms = jnp.concatenate([sums[3, :2], added(sums[3, 2:], far_down).astype(BF)])
         return sums[0], up_terms, down_terms
@@ -441,27 +450,31 @@
     def over_chips(operands):
         here, up_terms, down_terms = operands
         plane = added(here, around(up_terms, 1), around(down_terms, -1))
-        first, second = along(plane[1].astype(BF), 1), along(plane[2].astype(BF), 2)
-        third = gated([plane[3].astype(BF)], [first])[0]
-        return plane[0], first, second, along(third, 3)
+        return plane[0], plane[1].astype(BF), plane[2].astype(BF), plane[3].astype(BF)
 
     def staged(step, operands):
         shapes = jax.eval_shape(step, operands)
         blank = lambda _: jax.tree.map(lambda v: jnp.zeros(v.shape, v.dtype), shapes)
         return lax.cond(dp < tokens, step, blank, operands)
 
-    sums = staged(over_cores, (states, keys, place, send, joint))
-    late = gated([late], [sums[0]])[0]
-    last.append(stepped(late, (1, 3), low))
-    near_first = lowered_part(states[:128], sums[0])
-    waves = staged(over_chips, sums)
+    sums = staged(over_cores, (states, keys, place, send))
+    spread = gated(spread, [sums])
+    crossing = jnp.where(section == 4, quarters[0], sum(spread))
+    crossed = moved(
+        crossing, lambda z_hi, x, z_lo, y, core: (0, x, z_lo, y, core) if z_hi else None
+    )
+    plane = staged(over_chips, staged(over_far_chips, sums))
+    waves = [plane[0], *[along(wave, i + 1) for i, wave in enumerate(plane[1:])]]
+
+    crossed = gated([crossed], plane[:1])[0]
+    far = [stepped(crossed, (0, x), (0, 3)) for x in range(3)] + [crossed]
 
     coefs = coef_table(place, pair_of_row[0], gathered)
     weight_grad, gain_grad = finished(coefs, waves, gains, weights)
 
     slopes = unit_grads(following, gathered, tokens)
     is_far = (section == 3).astype(jnp.int32)[None]
-    out = section_grads(coefs, is_far, slopes, [near_first, near_last], [*last, near_last])
+    out = section_grads(coefs, is_far, slopes, [near], far)
     return out[None], weight_grad[None], gain_grad.astype(BF).reshape(1, -1)
 
 

time: 263 us -> 221 us (0.84)
  the two profiles are of different devices: /device:TPU:224 before, /device:TPU:38 now
where the time goes in v2:
time: 221 us; the launch traced here: 220 us
  waiting for transfers between devices  110 us (50%)
  Pallas kernels  44.3 us (20%)
  starting transfers between devices  32.1 us (15%)
  between operations  14.3 us (6%)
  other arithmetic  11 us (5%)
  local copies, waits for them, and re-layouts  8.45 us (4%)
    ppermute x17, waiting for transfers between devices, moved(): return lax.ppermute(value, AXES, pairs)  110 us
    ppermute x17, starting transfers between devices, moved(): return lax.ppermute(value, AXES, pairs)  32 us
    pallas_call x2, Pallas kernels, term_call(): pl.pallas_call(kernel, in_specs=[pl.BlockSpec(memory_space=pltpu.SMEM), w...  17.3 us
    pallas_call x1, Pallas kernels, unit_grads(): pl.pallas_call(grad_kernel, grid=(count // step,), in_specs=[pl.BlockSpec...  9.35 us
    pallas_call x1, Pallas kernels, section_grads(): pl.pallas_call(functools.partial(section_kernel, near_rows, far_rows), in...  8.86 us
    unnamed x24, local copies, waits for them, and re-layouts  6.13 us
    convert_element_type x1, other arithmetic, over_cores(): return added(keep, swapped).astype(BF)  5.64 us
  transfers between devices with their start and end apart: 18, of which 8 were waited for; matrix products, arithmetic and copies ran while one was open for 5% of the time, Pallas kernels for 14%

profile of v2, /device:TPU:38, one launch (start us, length us, event | category | flops | bytes accessed | tf_op | source)
XLA Modules:
  0.0 220.3 jit_solution(2928063977383316298)
XLA Ops:
  8.8 2.0 shard_map.94
  10.8 2.7 %collective-permute-start.5 = (bf16[528,512]{1,0:T(8,128)(2,1)}, bf16[528,512]{1,0:T(8,128)(2,1)S(1)}, u32[]{:S(2)}, u32[]{:S(2)}) collective-permute-start(bf16[528,512]{1,0:T(8,128)(2,1)} %get-tuple-element.45.payload), channel_id=1, source_target_pairs={{32,0},{33,1},{34,2},{35,3},{36,4},{37,5},{38,6},{39,7},{40,8},{41... | collective-permute-start | bytes 1622024 | tf_op jit(solution)/shard_map/ppermute | solution.py:37
  13.5 9.4 %shard_map.95 = (bf16[4,4,256,512]{3,2,1,0:T(8,128)(2,1)}, bf16[64,8192]{1,0:T(8,128)(2,1)}, bf16[64,8192]{1,0:T(8,128)(2,1)}, bf16[64,8192]{1,0:T(8,128)(2,1)},...) custom-call(s32[4]{0:T(128)S(1)} %pad_add_fusion.place.spot, bf16[528,512]{1,0:T(8,128)(2,1)} %get-tuple-element.45.payload, ...), custom_call_target="tpu_custom_call" | custom-call | tf_op jit(solution)/shard_map/pallas_call | solution.py:278
  22.9 21.6 %collective-permute-done.5.refs_0_ = bf16[528,512]{1,0:T(8,128)(2,1)S(1)} collective-permute-done((bf16[528,512]{1,0:T(8,128)(2,1)}, bf16[528,512]{1,0:T(8,128)(2,1)S(1)}, u32[]{:S(2)}, u32[]{:S(2)}) %collective-permute-start.5) | collective-permute-done | bytes 540704 | tf_op jit(solution)/shard_map/ppermute | solution.py:37
  45.3 1.8 shard_map.97.refs_1_
  49.3 3.4 %collective-permute-start.6 = (bf16[256,8192]{1,0:T(8,128)(2,1)}, bf16[256,8192]{1,0:T(8,128)(2,1)}, u32[]{:S(2)}, u32[]{:S(2)}) collective-permute-start(bf16[256,8192]{1,0:T(8,128)(2,1)} %bitcast.41), channel_id=1, source_target_pairs={{32,0},{33,1},{34,2},{35,3},{36,4},{37,5},{38,6},{39,7},{40,8},{41... | collective-permute-start | bytes 12582920 | tf_op jit(solution)/shard_map/ppermute | solution.py:37
  52.7 13.6 %conditional.3 = (bf16[4,4,256,512]{3,2,1,0:T(8,128)(2,1)}) conditional(s32[]{:T(128)} %convert_element_type.63, () %tuple.29, (s32[4]{0:T(128)S(1)}, bf16[256,512]{1,0:T(8,128)(2,1)S(1)}, bf16[256,8192]{1,0:T(8,128)(2,1)}, bf16[4,4,256,512]{3,2,1,0:T(8,128)(2,1)}) %tuple.50), branch_computations={%region_0.1_spmd, %region_1.2_spmd} | conditional | flops 8388608 | bytes 29360176 | solution.py:458
  52.7 7.9 %branch_1_fun.1 = bf16[4,4,256,512]{3,2,1,0:T(8,128)(2,1)} custom-call(s32[4]{0:T(128)S(1)} %get-tuple-element.18.spot, bf16[256,512]{1,0:T(8,128)(2,1)S(1)} %get-tuple-element.19.keys, bf16[256,8192]{1,0:T(8,128)(2,1)} %get-tuple-element.20.hidden), custom_call_target="tpu_custom_call" | custom-call | tf_op jit(solution)/shard_map/cond/branch_1_fun/pallas_call | solution.py:278
  60.6 5.6 %add_convert_fusion = bf16[4,4,256,512]{3,2,1,0:T(8,128)(2,1)} fusion(bf16[4,4,256,512]{3,2,1,0:T(8,128)(2,1)S(1)} %collective-permute-done, bf16[4,4,256,512]{3,2,1,0:T(8,128)(2,1)} %branch_1_fun.1), kind=kLoop, calls=%fused_computation | loop fusion | flops 8388608 | bytes 12582912 | tf_op jit(solution)/shard_map/cond/branch_1_fun/convert_element_type | solution.py:441
  68.6 3.2 %add_select_fusion = bf16[64,8192]{1,0:T(8,128)(2,1)} fusion(bf16[64,8192]{1,0:T(8,128)(2,1)} %get-tuple-element.48, bf16[64,8192]{1,0:T(8,128)(2,1)} %get-tuple-element.55, bf16[64,8192]{1,0:T(8,128)(2,1)} %get-tuple-element.53, bf16[64,8192]{1,0:T(8,128)(2,1)} %get-tuple-element.54, pred[]{:T(512)S(6)} %eq.11), kind=kLoop, calls=%fused_computation.17 | loop fusion | flops 1572864 | bytes 5242881 | tf_op jit(solution)/shard_map/jit(_where)/select_n | solution.py:462
  73.1 16.5 %conditional.4 = (bf16[4,256,512]{2,1,0:T(8,128)(2,1)S(1)}, bf16[4,256,512]{2,1,0:T(8,128)(2,1)S(1)}, bf16[4,256,512]{2,1,0:T(8,128)(2,1)S(1)}) conditional(s32[]{:T(128)} %convert_element_type.63, () %tuple.32, bf16[4,4,256,512]{3,2,1,0:T(8,128)(2,1)S(1)} %copy-done), branch_computations={%region_2.3_spmd, %region_3.4_spmd} | conditional | flops 3145728 | bytes 17825896 | solution.py:458
  76.7 12.4 %collective-permute-done.1 = bf16[2,256,512]{2,1,0:T(8,128)(2,1)S(1)} collective-permute-done((bf16[2,256,512]{2,1,0:T(8,128)(2,1)S(1)}, bf16[2,256,512]{2,1,0:T(8,128)(2,1)S(1)}, u32[]{:S(2)}, u32[]{:S(2)}) %collective-permute-start.1) | collective-permute-done | bytes 524320 | tf_op jit(solution)/shard_map/cond/branch_1_fun/ppermute | solution.py:37
  89.6 36.6 %conditional.5 = (f32[256,512]{1,0:T(8,128)S(1)}, bf16[256,512]{1,0:T(8,128)(2,1)S(1)}, bf16[256,512]{1,0:T(8,128)(2,1)S(1)}, bf16[256,512]{1,0:T(8,128)(2,1)S(1)}) conditional(s32[]{:T(128)} %convert_element_type.63, () %tuple.31, (bf16[4,256,512]{2,1,0:T(8,128)(2,1)S(1)}, bf16[4,256,512]{2,1,0:T(8,128)(2,1)S(1)}, ...), branch_computations={%region_4.5_spmd, %region_5.6_spmd} | conditional | flops 3145728 | bytes 17301616 | solution.py:458
  89.6 11.3 %collective-permute-start.3 = (bf16[4,256,512]{2,1,0:T(8,128)(2,1)S(1)}, bf16[4,256,512]{2,1,0:T(8,128)(2,1)S(1)}, u32[]{:S(2)}, u32[]{:S(2)}) collective-permute-start(bf16[4,256,512]{2,1,0:T(8,128)(2,1)S(1)} %get-tuple-element.23), channel_id=1, source_target_pairs={{0,2},{1,3},{2,4},{3,5},{4,6},{5,7},{6,0},{7,1},{8,10},{9,11},{10,... | collective-permute-start | bytes 3145736 | tf_op jit(solution)/shard_map/cond/branch_1_fun/ppermute | solution.py:37
  102.2 22.8 %collective-permute-done.3 = bf16[4,256,512]{2,1,0:T(8,128)(2,1)S(1)} collective-permute-done((bf16[4,256,512]{2,1,0:T(8,128)(2,1)S(1)}, bf16[4,256,512]{2,1,0:T(8,128)(2,1)S(1)}, u32[]{:S(2)}, u32[]{:S(2)}) %collective-permute-start.3) | collective-permute-done | bytes 1048608 | tf_op jit(solution)/shard_map/cond/branch_1_fun/ppermute | solution.py:37
  126.2 23.6 %collective-permute-done.10.refs_0_ = bf16[64,8192]{1,0:T(8,128)(2,1)S(1)} collective-permute-done((bf16[64,8192]{1,0:T(8,128)(2,1)}, bf16[64,8192]{1,0:T(8,128)(2,1)S(1)}, u32[]{:S(2)}, u32[]{:S(2)}) %collective-permute-start.10) | collective-permute-done | bytes 1048608 | tf_op jit(solution)/shard_map/ppermute | solution.py:37
  154.8 8.2 %collective-permute-done.14.second = bf16[256,512]{1,0:T(8,128)(2,1)S(1)} collective-permute-done((bf16[256,512]{1,0:T(8,128)(2,1)S(1)}, bf16[256,512]{1,0:T(8,128)(2,1)S(1)}, u32[]{:S(2)}, u32[]{:S(2)}) %collective-permute-start.14) | collective-permute-done | bytes 262176 | tf_op jit(solution)/shard_map/ppermute | solution.py:37
  163.0 10.7 %collective-permute-done.15.third = bf16[256,512]{1,0:T(8,128)(2,1)S(1)} collective-permute-done((bf16[256,512]{1,0:T(8,128)(2,1)S(1)}, bf16[256,512]{1,0:T(8,128)(2,1)S(1)}, u32[]{:S(2)}, u32[]{:S(2)}) %collective-permute-start.15) | collective-permute-done | bytes 262176 | tf_op jit(solution)/shard_map/ppermute | solution.py:37
  173.7 2.6 %collective-permute-start.16 = (bf16[256,512]{1,0:T(8,128)(2,1)}, bf16[256,512]{1,0:T(8,128)(2,1)S(1)}, u32[]{:S(2)}, u32[]{:S(2)}) collective-permute-start(bf16[256,512]{1,0:T(8,128)(2,1)} %copy-done.11), channel_id=1, source_target_pairs={{0,24},{1,25},{2,26},{3,27},{4,28},{5,29},{6,30},{7,31},{8,0},{9,1... | collective-permute-start | bytes 786440 | tf_op jit(solution)/shard_map/ppermute | solution.py:37
  176.4 2.6 %shard_map.98.scale.coefs = f32[8,128]{1,0:T(8,128)} custom-call(s32[4]{0:T(128)S(1)} %pad_add_fusion.place.spot, s32[4]{0:T(128)} %bitcast.48, bf16[32,272,512]{2,1,0:T(8,128)(2,1)} %bitcast.38), custom_call_target="tpu_custom_call" | custom-call | tf_op jit(solution)/shard_map/pallas_call | solution.py:170
  179.0 9.3 %shard_map.99.slopes = bf16[256,8192]{1,0:T(8,128)(2,1)} custom-call(bf16[528,512]{1,0:T(8,128)(2,1)} %shard_map.96.payload, bf16[32,272,512]{2,1,0:T(8,128)(2,1)} %bitcast.39), custom_call_target="tpu_custom_call" | custom-call | tf_op jit(solution)/shard_map/pallas_call | solution.py:318
  189.1 2.3 %shard_map.104 = (bf16[256,512]{1,0:T(8,128)(2,1)}, f32[256,1]{1,0:T(8,128)}) custom-call(f32[8,128]{1,0:T(8,128)} %shard_map.98.scale.coefs, f32[256,512]{1,0:T(8,128)S(1)} %get-tuple-element.56.refs_1_.first, bf16[256,512]{1,0:T(8,128)(2,1)} %copy-done.8, bf16[256,512]{1,0:T(8,128)(2,1)} %copy-done.9, bf16[256,512]{1,0:T(8,128)(2,1)} %copy-done.10, ...), custom_call_target="tpu_custom_call" | custom-call | tf_op jit(solution)/shard_map/pallas_call | solution.py:194
  193.0 10.2 %collective-permute-done.11.refs_1_ = bf16[64,8192]{1,0:T(8,128)(2,1)S(1)} collective-permute-done((bf16[64,8192]{1,0:T(8,128)(2,1)}, bf16[64,8192]{1,0:T(8,128)(2,1)S(1)}, u32[]{:S(2)}, u32[]{:S(2)}) %collective-permute-start.11) | collective-permute-done | bytes 1048608 | tf_op jit(solution)/shard_map/ppermute | solution.py:37
  204.6 8.9 %shard_map.103 = bf16[256,8192]{1,0:T(8,128)(2,1)} custom-call(f32[8,128]{1,0:T(8,128)} %shard_map.98.scale.coefs, s32[1]{0:T(128)} %bitcast.24.is_far, bf16[256,8192]{1,0:T(8,128)(2,1)} %shard_map.99.slopes, bf16[256,8192]{1,0:T(8,128)(2,1)} %collective-permute-done.6.refs_0_, bf16[64,8192]{1,0:T(8,128)(2,1)} %copy-done.6, bf16[64,8192]{1,0:T(8,128)(2,1)} %copy-done.7, ...), custom_call_target="tpu_custom_call" | custom-call | tf_op jit(solution)/shard_map/pallas_call | solution.py:400
  (65 shorter events, 23.2 us)
Async XLA Ops:
  7.2 169.2 %all-gather.2.cloned.1.call-start = ((), (), s32[]{:S(2)}) async-start(), calls=%async_computation | async-start | bytes 9191424 | tf_op jit(solution)/shard_map/all_gather | solution.py:431
  10.8 33.7 %collective-permute-start.5 = (bf16[528,512]{1,0:T(8,128)(2,1)}, bf16[528,512]{1,0:T(8,128)(2,1)S(1)}, u32[]{:S(2)}, u32[]{:S(2)}) collective-permute-start(bf16[528,512]{1,0:T(8,128)(2,1)} %get-tuple-element.45.payload), channel_id=1, source_target_pairs={{32,0},{33,1},{34,2},{35,3},{36,4},{37,5},{38,6},{39,7},{40,8},{41... | collective-permute-start | bytes 1622024 | tf_op jit(solution)/shard_map/ppermute | solution.py:37
  47.1 19.2 %collective-permute-start.7 = (bf16[64,8192]{1,0:T(8,128)(2,1)}, bf16[64,8192]{1,0:T(8,128)(2,1)S(1)}, u32[]{:S(2)}, u32[]{:S(2)}) collective-permute-start(bf16[64,8192]{1,0:T(8,128)(2,1)} %get-tuple-element.49), channel_id=1, source_target_pairs={{128,160},{129,161},{130,162},{131,163},{132,164},{133,165},{134,1... | collective-permute-start | bytes 3145736 | tf_op jit(solution)/shard_map/ppermute | solution.py:37
  47.8 18.5 %collective-permute-start.8 = (bf16[64,8192]{1,0:T(8,128)(2,1)}, bf16[64,8192]{1,0:T(8,128)(2,1)S(1)}, u32[]{:S(2)}, u32[]{:S(2)}) collective-permute-start(bf16[64,8192]{1,0:T(8,128)(2,1)} %get-tuple-element.50), channel_id=1, source_target_pairs={{128,192},{129,193},{130,194},{131,195},{132,196},{133,197},{134,1... | collective-permute-start | bytes 3145736 | tf_op jit(solution)/shard_map/ppermute | solution.py:37
  48.5 17.7 %collective-permute-start.9 = (bf16[64,8192]{1,0:T(8,128)(2,1)}, bf16[64,8192]{1,0:T(8,128)(2,1)S(1)}, u32[]{:S(2)}, u32[]{:S(2)}) collective-permute-start(bf16[64,8192]{1,0:T(8,128)(2,1)} %get-tuple-element.51), channel_id=1, source_target_pairs={{128,224},{129,225},{130,226},{131,227},{132,228},{133,229},{134,2... | collective-permute-start | bytes 3145736 | tf_op jit(solution)/shard_map/ppermute | solution.py:37
  49.3 153.9 %collective-permute-start.6 = (bf16[256,8192]{1,0:T(8,128)(2,1)}, bf16[256,8192]{1,0:T(8,128)(2,1)}, u32[]{:S(2)}, u32[]{:S(2)}) collective-permute-start(bf16[256,8192]{1,0:T(8,128)(2,1)} %bitcast.41), channel_id=1, source_target_pairs={{32,0},{33,1},{34,2},{35,3},{36,4},{37,5},{38,6},{39,7},{40,8},{41... | collective-permute-start | bytes 12582920 | tf_op jit(solution)/shard_map/ppermute | solution.py:37
  52.7 7.9 %collective-permute-start = (bf16[4,4,256,512]{3,2,1,0:T(8,128)(2,1)}, bf16[4,4,256,512]{3,2,1,0:T(8,128)(2,1)S(1)}, u32[]{:S(2)}, u32[]{:S(2)}) collective-permute-start(bf16[4,4,256,512]{3,2,1,0:T(8,128)(2,1)} %get-tuple-element.21), channel_id=1, source_target_pairs={{0,1},{1,0},{2,3},{3,2},{4,5},{5,4},{6,7},{7,6},{8,9},{9,8},{10,11... | collective-permute-start | bytes 12582920 | tf_op jit(solution)/shard_map/cond/branch_1_fun/ppermute | solution.py:37
  66.3 1.3 copy-start.4
  68.6 4.5 %copy-start = (bf16[4,4,256,512]{3,2,1,0:T(8,128)(2,1)S(1)}, bf16[4,4,256,512]{3,2,1,0:T(8,128)(2,1)}, u32[]{:S(2)}) copy-start(bf16[4,4,256,512]{3,2,1,0:T(8,128)(2,1)} %get-tuple-element.89.refs_3_) | copy-start | bytes 12582916
  71.8 78.0 %collective-permute-start.10 = (bf16[64,8192]{1,0:T(8,128)(2,1)}, bf16[64,8192]{1,0:T(8,128)(2,1)S(1)}, u32[]{:S(2)}, u32[]{:S(2)}) collective-permute-start(bf16[64,8192]{1,0:T(8,128)(2,1)} %add_select_fusion), channel_id=1, source_target_pairs={{128,0},{129,1},{130,2},{131,3},{132,4},{133,5},{134,6},{135,7},{1... | collective-permute-start | bytes 3145736 | tf_op jit(solution)/shard_map/ppermute | solution.py:37
  73.3 15.8 %collective-permute-start.1 = (bf16[2,256,512]{2,1,0:T(8,128)(2,1)S(1)}, bf16[2,256,512]{2,1,0:T(8,128)(2,1)S(1)}, u32[]{:S(2)}, u32[]{:S(2)}) collective-permute-start(bf16[2,256,512]{2,1,0:T(8,128)(2,1)S(1)} %get-tuple-element.67), channel_id=1, source_target_pairs={{0,2},{1,3},{2,4},{3,5},{4,6},{5,7},{6,0},{7,1},{8,10},{9,11},{10,... | collective-permute-start | bytes 1572872 | tf_op jit(solution)/shard_map/cond/branch_1_fun/ppermute | solution.py:37
  75.0 14.2 %collective-permute-start.2 = (bf16[2,256,512]{2,1,0:T(8,128)(2,1)S(1)}, bf16[2,256,512]{2,1,0:T(8,128)(2,1)S(1)}, u32[]{:S(2)}, u32[]{:S(2)}) collective-permute-start(bf16[2,256,512]{2,1,0:T(8,128)(2,1)S(1)} %get-tuple-element.65), channel_id=1, source_target_pairs={{0,6},{1,7},{2,0},{3,1},{4,2},{5,3},{6,4},{7,5},{8,14},{9,15},{10,... | collective-permute-start | bytes 1572872 | tf_op jit(solution)/shard_map/cond/branch_1_fun/ppermute | solution.py:37
  89.6 35.3 %collective-permute-start.3 = (bf16[4,256,512]{2,1,0:T(8,128)(2,1)S(1)}, bf16[4,256,512]{2,1,0:T(8,128)(2,1)S(1)}, u32[]{:S(2)}, u32[]{:S(2)}) collective-permute-start(bf16[4,256,512]{2,1,0:T(8,128)(2,1)S(1)} %get-tuple-element.23), channel_id=1, source_target_pairs={{0,2},{1,3},{2,4},{3,5},{4,6},{5,7},{6,0},{7,1},{8,10},{9,11},{10,... | collective-permute-start | bytes 3145736 | tf_op jit(solution)/shard_map/cond/branch_1_fun/ppermute | solution.py:37
  101.0 24.7 %collective-permute-start.4 = (bf16[4,256,512]{2,1,0:T(8,128)(2,1)S(1)}, bf16[4,256,512]{2,1,0:T(8,128)(2,1)S(1)}, u32[]{:S(2)}, u32[]{:S(2)}) collective-permute-start(bf16[4,256,512]{2,1,0:T(8,128)(2,1)S(1)} %get-tuple-element.24), channel_id=1, source_target_pairs={{0,6},{1,7},{2,0},{3,1},{4,2},{5,3},{6,4},{7,5},{8,14},{9,15},{10,... | collective-permute-start | bytes 3145736 | tf_op jit(solution)/shard_map/cond/branch_1_fun/ppermute | solution.py:37
  126.2 28.4 %copy-start.11 = (bf16[256,512]{1,0:T(8,128)(2,1)}, bf16[256,512]{1,0:T(8,128)(2,1)S(1)}, u32[]{:S(2)}) copy-start(bf16[256,512]{1,0:T(8,128)(2,1)S(1)} %get-tuple-element.59) | copy-start | bytes 786436
  150.8 52.4 %collective-permute-start.11 = (bf16[64,8192]{1,0:T(8,128)(2,1)}, bf16[64,8192]{1,0:T(8,128)(2,1)S(1)}, u32[]{:S(2)}, u32[]{:S(2)}) collective-permute-start(bf16[64,8192]{1,0:T(8,128)(2,1)} %shard_map.102.refs_4_), channel_id=1, source_target_pairs={{0,96},{1,97},{2,98},{3,99},{4,100},{5,101},{6,102},{7,103},{8,104... | collective-permute-start | bytes 3145736 | tf_op jit(solution)/shard_map/ppermute | solution.py:37
  152.1 51.1 %collective-permute-start.12 = (bf16[64,8192]{1,0:T(8,128)(2,1)}, bf16[64,8192]{1,0:T(8,128)(2,1)S(1)}, u32[]{:S(2)}, u32[]{:S(2)}) collective-permute-start(bf16[64,8192]{1,0:T(8,128)(2,1)} %shard_map.102.refs_4_), channel_id=1, source_target_pairs={{32,96},{33,97},{34,98},{35,99},{36,100},{37,101},{38,102},{39,103... | collective-permute-start | bytes 3145736 | tf_op jit(solution)/shard_map/ppermute | solution.py:37
  153.4 49.8 %collective-permute-start.13 = (bf16[64,8192]{1,0:T(8,128)(2,1)}, bf16[64,8192]{1,0:T(8,128)(2,1)}, u32[]{:S(2)}, u32[]{:S(2)}) collective-permute-start(bf16[64,8192]{1,0:T(8,128)(2,1)} %shard_map.102.refs_4_), channel_id=1, source_target_pairs={{64,96},{65,97},{66,98},{67,99},{68,100},{69,101},{70,102},{71,103... | collective-permute-start | bytes 3145736 | tf_op jit(solution)/shard_map/ppermute | solution.py:37
  154.7 8.3 %collective-permute-start.14 = (bf16[256,512]{1,0:T(8,128)(2,1)S(1)}, bf16[256,512]{1,0:T(8,128)(2,1)S(1)}, u32[]{:S(2)}, u32[]{:S(2)}) collective-permute-start(bf16[256,512]{1,0:T(8,128)(2,1)S(1)} %get-tuple-element.57), channel_id=1, source_target_pairs={{0,8},{1,9},{2,10},{3,11},{4,12},{5,13},{6,14},{7,15},{8,16},{9,17... | collective-permute-start | bytes 786440 | tf_op jit(solution)/shard_map/ppermute | solution.py:37
  163.0 16.0 %copy-start.8 = (bf16[256,512]{1,0:T(8,128)(2,1)}, bf16[256,512]{1,0:T(8,128)(2,1)S(1)}, u32[]{:S(2)}) copy-start(bf16[256,512]{1,0:T(8,128)(2,1)S(1)} %collective-permute-done.14.second) | copy-start | bytes 786436
  163.0 10.7 %collective-permute-start.15 = (bf16[256,512]{1,0:T(8,128)(2,1)S(1)}, bf16[256,512]{1,0:T(8,128)(2,1)S(1)}, u32[]{:S(2)}, u32[]{:S(2)}) collective-permute-start(bf16[256,512]{1,0:T(8,128)(2,1)S(1)} %get-tuple-element.58), channel_id=1, source_target_pairs={{0,16},{1,17},{2,18},{3,19},{4,20},{5,21},{6,22},{7,23},{8,24},{9,... | collective-permute-start | bytes 786440 | tf_op jit(solution)/shard_map/ppermute | solution.py:37
  173.7 5.3 %copy-start.9 = (bf16[256,512]{1,0:T(8,128)(2,1)}, bf16[256,512]{1,0:T(8,128)(2,1)S(1)}, u32[]{:S(2)}) copy-start(bf16[256,512]{1,0:T(8,128)(2,1)S(1)} %collective-permute-done.15.third) | copy-start | bytes 786436
  173.7 14.7 %collective-permute-start.16 = (bf16[256,512]{1,0:T(8,128)(2,1)}, bf16[256,512]{1,0:T(8,128)(2,1)S(1)}, u32[]{:S(2)}, u32[]{:S(2)}) collective-permute-start(bf16[256,512]{1,0:T(8,128)(2,1)} %copy-done.11), channel_id=1, source_target_pairs={{0,24},{1,25},{2,26},{3,27},{4,28},{5,29},{6,30},{7,31},{8,0},{9,1... | collective-permute-start | bytes 786440 | tf_op jit(solution)/shard_map/ppermute | solution.py:37
  203.2 1.4 copy-start.7
  (6 other events, 5.4 us)
Sparse Core Ops, SparseCore 0:
  47.2 92.4 all-gather.1

commit v3 on v2

--- a/solution.py
+++ b/solution.py
@@ -71,6 +71,31 @@
     return moved(
         value, lambda z_hi, x, z_lo, y, core: (z_hi, x - 1, z_lo, y, core) if x else None
     )
+
+
+def picked_kernel(section, *refs):
+    *sources, out, held, sem = refs
+    for i, source in enumerate(sources):
+
+        @pl.when(section[0] == 5 + i)
+        def _():
+            for start, end in ((source, held), (held, out)):
+                copy = pltpu.make_async_copy(start, end, sem)
+                copy.start()
+                copy.wait()
+
+
+def picked(section, sources):
+    shape = sources[0].shape
+    return pl.pallas_call(
+        picked_kernel,
+        in_specs=[pl.BlockSpec(memory_space=pltpu.SMEM)] + [ANYWHERE] * 3,
+        out_specs=ANYWHERE,
+        out_shape=jax.ShapeDtypeStruct(shape, BF),
+        scratch_shapes=[pltpu.VMEM(shape, BF), pltpu.SemaphoreType.DMA],
+        compiler_params=pltpu.CompilerParams(vmem_limit_bytes=VMEM_LIMIT),
+        cost_estimate=FREE,
+    )(section[None], *sources)
 
 
 def prepare_kernel(place, limits, pairs, weights, gains, keys, ratios, out, mark):
@@ -143,7 +168,7 @@
 
 def coef_kernel(place, pairs, gathered, out, notes, sem):
     copy = pltpu.make_async_copy(
-        gathered.at[:, pl.ds(gathered.shape[1] - EXTRA, EXTRA)], notes, sem
+        gathered.at[:, pl.ds(gathered.shape[1] - EXTRA, EXTRA), pl.ds(0, 128)], notes, sem
     )
     copy.start()
     copy.wait()
@@ -173,7 +198,7 @@
         out_specs=pl.BlockSpec(memory_space=pltpu.VMEM),
         out_shape=jax.ShapeDtypeStruct((8, 128), F32),
         scratch_shapes=[
-            pltpu.VMEM((gathered.shape[0], EXTRA, gathered.shape[2]), BF),
+            pltpu.VMEM((gathered.shape[0], EXTRA, 128), BF),
             pltpu.SemaphoreType.DMA,
         ],
         cost_estimate=FREE,
@@ -185,7 +210,8 @@
     for i, wave in enumerate((second, third, fourth)):
         total += wave[...].astype(F32) * coefs[:1, i + 1 : i + 2]
     out[...] = (total * gains[...].astype(F32)).astype(BF)
-    sums[...] = jnp.sum(total * weights[...].astype(F32), axis=1, keepdims=True)
+    found = jnp.sum(total * weights[...].astype(F32), axis=1, keepdims=True)
+    sums[...] = jnp.broadcast_to(found, (found.shape[0], 128)).T[:1].astype(BF)
 
 
 def finished(coefs, waves, gains, weights):
@@ -195,7 +221,7 @@
         finish_kernel,
         in_specs=[whole] * 7,
         out_specs=[whole] * 2,
-        out_shape=[jax.ShapeDtypeStruct((rows, kw), BF), jax.ShapeDtypeStruct((rows, 1), F32)],
+        out_shape=[jax.ShapeDtypeStruct((rows, kw), BF), jax.ShapeDtypeStruct((1, rows), BF)],
         cost_estimate=FREE,
     )(coefs, *waves, gains, weights)
 
@@ -263,30 +289,30 @@
 
 
 def keep_kernel(spot, keys, hidden, *refs):
-    out, states, terms, in_sem, out_sem = refs
+    out, states, terms, in_sem, out_sem, _ = refs
     for copy in load(hidden, states, in_sem, 4):
         copy.wait()
     block_products(spot, False, states, keys, terms, out, out_sem)
 
 
-def term_call(kernel, operands, more):
+def term_call(kernel, operands, sending):
     tokens, width = operands[2].shape
     kw = operands[1].shape[1]
     whole = pl.BlockSpec(memory_space=pltpu.VMEM)
-    rows = [jax.ShapeDtypeStruct((QUARTER, width), BF)] * 4
-    keys = jax.ShapeDtypeStruct((tokens, kw), BF)
+    more = [jax.ShapeDtypeStruct((QUARTER, width), BF)] * 4 if sending else []
+    keys = [jax.ShapeDtypeStruct((tokens, kw), BF)] if sending else []
     return pl.pallas_call(
         kernel,
         in_specs=[pl.BlockSpec(memory_space=pltpu.SMEM), whole, ANYWHERE],
-        out_specs=[ANYWHERE] + ([ANYWHERE] * 4 + [whole] if more else []),
-        out_shape=[jax.ShapeDtypeStruct((4, 4, BLK, kw), BF)] + ([*rows, keys] if more else []),
+        out_specs=[ANYWHERE] * (1 + len(more)) + [whole] * len(keys),
+        out_shape=[jax.ShapeDtypeStruct((4, 4, BLK, kw), BF), *more, *keys],
         scratch_shapes=[
             pltpu.VMEM((tokens, width), BF),
             pltpu.VMEM((4, 4, BLK, kw), BF),
             pltpu.SemaphoreType.DMA((4,)),
             pltpu.SemaphoreType.DMA((4,)),
-        ]
-        + ([pltpu.SemaphoreType.DMA((4,))] if more else []),
+            pltpu.SemaphoreType.DMA((4,)),
+        ],
         compiler_params=pltpu.CompilerParams(vmem_limit_bytes=VMEM_LIMIT),
         cost_estimate=FREE,
     )(*operands)
@@ -432,25 +458,27 @@
     gathered = gathered.reshape(-1, tokens + EXTRA, kw)
     near = lowered(states)
     up = (1, 0)
-    spread = [stepped(quarter, up, (1, x + 1)) for x, quarter in enumerate(quarters[1:])]
+    direct = stepped(quarters[0], up, (0, 3))
+    spread = {x: stepped(quarters[x], up, (1, x)) for x in (2, 3, 1)}
 
     def over_cores(operands):
         states, keys, place, send = operands
         swapped = moved(send, lambda z_hi, x, z_lo, y, core: (z_hi, x, z_lo, y, 1 - core))
-        keep = term_call(keep_kernel, (place, keys, states), False)[0]
-        return added(keep, swapped).astype(BF)
+        return swapped, *term_call(keep_kernel, (place, keys, states), False)
 
     def over_far_chips(operands):
-        sums = operands
-        far_up, far_down = around(sums[2, :2], 1), around(sums[2, 2:], -1)
-        up_terms = jnp.concatenate([added(sums[1, :2], far_up).astype(BF), sums[1, 2:]])
-        down_terms = jnp.concatenate([sums[3, :2], added(sums[3, 2:], far_down).astype(BF)])
-        return sums[0], up_terms, down_terms
+        swapped, keep = operands
+        sums = lambda r, *more: added(keep[r], swapped[r], *more)
+        far = sums(2).astype(BF)
+        far_up, far_down = around(far[:2], 1), around(far[2:], -1)
+        up_terms = jnp.concatenate([far_up.astype(F32), jnp.zeros(far_up.shape, F32)])
+        down_terms = jnp.concatenate([jnp.zeros(far_down.shape, F32), far_down.astype(F32)])
+        return sums(0).astype(BF), sums(1, up_terms).astype(BF), sums(3, down_terms).astype(BF)
 
     def over_chips(operands):
         here, up_terms, down_terms = operands
         plane = added(here, around(up_terms, 1), around(down_terms, -1))
-        return plane[0], plane[1].astype(BF), plane[2].astype(BF), plane[3].astype(BF)
+        return plane[0], *[plane[i].astype(BF) for i in (1, 2, 3)]
 
     def staged(step, operands):
         shapes = jax.eval_shape(step, operands)
@@ -458,24 +486,23 @@
         return lax.cond(dp < tokens, step, blank, operands)
 
     sums = staged(over_cores, (states, keys, place, send))
-    spread = gated(spread, [sums])
-    crossing = jnp.where(section == 4, quarters[0], sum(spread))
+    second, third, first = gated([spread[x] for x in (2, 3, 1)], sums[:1])
+    crossing = picked(section, [first, second, third])
     crossed = moved(
-        crossing, lambda z_hi, x, z_lo, y, core: (0, x, z_lo, y, core) if z_hi else None
+        crossing, lambda z_hi, x, z_lo, y, core: (0, x, z_lo, y, core) if z_hi and x else None
     )
     plane = staged(over_chips, staged(over_far_chips, sums))
-    waves = [plane[0], *[along(wave, i + 1) for i, wave in enumerate(plane[1:])]]
-
     crossed = gated([crossed], plane[:1])[0]
-    far = [stepped(crossed, (0, x), (0, 3)) for x in range(3)] + [crossed]
-
+    far = [direct, *[stepped(crossed, (0, x), (0, 3)) for x in (1, 2)], crossed]
+    slopes = unit_grads(following, gathered, tokens)
     coefs = coef_table(place, pair_of_row[0], gathered)
+    later = gated(plane[1:], [near])
+    waves = [plane[0], *[along(wave, i + 1) for i, wave in enumerate(later)]]
     weight_grad, gain_grad = finished(coefs, waves, gains, weights)
 
-    slopes = unit_grads(following, gathered, tokens)
     is_far = (section == 3).astype(jnp.int32)[None]
     out = section_grads(coefs, is_far, slopes, [near], far)
-    return out[None], weight_grad[None], gain_grad.astype(BF).reshape(1, -1)
+    return out[None], weight_grad[None], gain_grad
 
 
 def solution(mesh):

time: 221 us -> 210 us (0.950)
  the two profiles are of different devices: /device:TPU:38 before, /device:TPU:100 now
where the time goes in v3:
time: 210 us; the launch traced here: 209 us
  waiting for transfers between devices  75.7 us (36%)
  starting transfers between devices  62 us (30%)
  Pallas kernels  42.9 us (20%)
  between operations  14.3 us (7%)
  local copies, waits for them, and re-layouts  7.71 us (4%)
  other arithmetic  6.37 us (3%)
    ppermute x17, waiting for transfers between devices, moved(): return lax.ppermute(value, AXES, pairs)  75.7 us
    ppermute x17, starting transfers between devices, moved(): return lax.ppermute(value, AXES, pairs)  61.9 us
    pallas_call x2, Pallas kernels, term_call(): pl.pallas_call(kernel, in_specs=[pl.BlockSpec(memory_space=pltpu.SMEM), w...  17.4 us
    pallas_call x1, Pallas kernels, unit_grads(): pl.pallas_call(grad_kernel, grid=(count // step,), in_specs=[pl.BlockSpec...  9.31 us
    pallas_call x1, Pallas kernels, section_grads(): pl.pallas_call(functools.partial(section_kernel, near_rows, far_rows), in...  7.68 us
    unnamed x18, local copies, waits for them, and re-layouts  6.14 us
  transfers between devices with their start and end apart: 18, of which 6 were waited for; matrix products, arithmetic and copies ran while one was open for 3% of the time, Pallas kernels for 15%

profile of v3, /device:TPU:100, one launch (start us, length us, event | category | flops | bytes accessed | tf_op | source)
XLA Modules:
  0.0 209.1 jit_solution(12063166527019357713)
XLA Ops:
  8.7 2.0 shard_map.94
  10.8 2.4 %collective-permute-start.5 = (bf16[528,512]{1,0:T(8,128)(2,1)}, bf16[528,512]{1,0:T(8,128)(2,1)S(1)}, u32[]{:S(2)}, u32[]{:S(2)}) collective-permute-start(bf16[528,512]{1,0:T(8,128)(2,1)} %get-tuple-element.52.payload), channel_id=1, source_target_pairs={{32,0},{33,1},{34,2},{35,3},{36,4},{37,5},{38,6},{39,7},{40,8},{41... | collective-permute-start | bytes 1622024 | tf_op jit(solution)/shard_map/ppermute | solution.py:37
  13.2 9.4 %shard_map.95 = (bf16[4,4,256,512]{3,2,1,0:T(8,128)(2,1)}, bf16[64,8192]{1,0:T(8,128)(2,1)}, bf16[64,8192]{1,0:T(8,128)(2,1)}, bf16[64,8192]{1,0:T(8,128)(2,1)},...) custom-call(s32[4]{0:T(128)S(1)} %pad_add_fusion.place.spot, bf16[528,512]{1,0:T(8,128)(2,1)} %get-tuple-element.52.payload, ...), custom_call_target="tpu_custom_call" | custom-call | tf_op jit(solution)/shard_map/pallas_call | solution.py:304
  22.6 4.3 %collective-permute-done.5.refs_0_ = bf16[528,512]{1,0:T(8,128)(2,1)S(1)} collective-permute-done((bf16[528,512]{1,0:T(8,128)(2,1)}, bf16[528,512]{1,0:T(8,128)(2,1)S(1)}, u32[]{:S(2)}, u32[]{:S(2)}) %collective-permute-start.5) | collective-permute-done | bytes 540704 | tf_op jit(solution)/shard_map/ppermute | solution.py:37
  27.7 1.8 shard_map.97.refs_1_
  29.5 2.4 %collective-permute-start.6 = (bf16[256,8192]{1,0:T(8,128)(2,1)}, bf16[256,8192]{1,0:T(8,128)(2,1)}, u32[]{:S(2)}, u32[]{:S(2)}) collective-permute-start(bf16[256,8192]{1,0:T(8,128)(2,1)} %bitcast.40), channel_id=1, source_target_pairs={{32,0},{33,1},{34,2},{35,3},{36,4},{37,5},{38,6},{39,7},{40,8},{41... | collective-permute-start | bytes 12582920 | tf_op jit(solution)/shard_map/ppermute | solution.py:37
  34.2 8.1 %conditional.3 = (bf16[4,4,256,512]{3,2,1,0:T(8,128)(2,1)}, bf16[4,4,256,512]{3,2,1,0:T(8,128)(2,1)}) conditional(s32[]{:T(128)} %convert_element_type.77, () %tuple.31, (bf16[4,4,256,512]{3,2,1,0:T(8,128)(2,1)}, s32[4]{0:T(128)S(1)}, bf16[256,512]{1,0:T(8,128)(2,1)S(1)}, bf16[256,8192]{1,0:T(8,128)(2,1)}) %tuple.51), branch_computations={%region_0.1_spmd, %region_1.2_spmd} | conditional | bytes 16777272 | solution.py:486
  34.3 8.0 %branch_1_fun.1 = bf16[4,4,256,512]{3,2,1,0:T(8,128)(2,1)} custom-call(s32[4]{0:T(128)S(1)} %get-tuple-element.19.spot, bf16[256,512]{1,0:T(8,128)(2,1)S(1)} %get-tuple-element.20.keys, bf16[256,8192]{1,0:T(8,128)(2,1)} %get-tuple-element.21.hidden), custom_call_target="tpu_custom_call" | custom-call | tf_op jit(solution)/shard_map/cond/branch_1_fun/pallas_call | solution.py:304
  47.0 30.2 %conditional.4 = (bf16[4,256,512]{2,1,0:T(8,128)(2,1)S(1)}, bf16[4,256,512]{2,1,0:T(8,128)(2,1)S(1)}, bf16[4,256,512]{2,1,0:T(8,128)(2,1)S(1)}) conditional(s32[]{:T(128)} %convert_element_type.77, () %tuple.34, (bf16[4,4,256,512]{3,2,1,0:T(8,128)(2,1)}, bf16[4,4,256,512]{3,2,1,0:T(8,128)(2,1)}) %tuple.35), branch_computations={%region_2.3_spmd, %region_3.4_spmd} | conditional | flops 10485760 | bytes 19923048 | solution.py:486
  47.0 2.8 %add_convert_fusion = (bf16[1,4,256,512]{3,2,1,0:T(8,128)(2,1)S(1)}, bf16[4,256,512]{2,1,0:T(8,128)(2,1)S(1)}) fusion(bf16[4,4,256,512]{3,2,1,0:T(8,128)(2,1)} %get-tuple-element.23, bf16[4,4,256,512]{3,2,1,0:T(8,128)(2,1)} %get-tuple-element.22), kind=kLoop, calls=%fused_computation.4 | loop fusion | flops 4194304 | bytes 6291456 | tf_op jit(solution)/shard_map/cond/branch_1_fun/convert_element_type | solution.py:472
  53.1 18.3 %collective-permute-done.1 = bf16[2,256,512]{2,1,0:T(8,128)(2,1)S(1)} collective-permute-done((bf16[2,256,512]{2,1,0:T(8,128)(2,1)S(1)}, bf16[2,256,512]{2,1,0:T(8,128)(2,1)S(1)}, u32[]{:S(2)}, u32[]{:S(2)}) %collective-permute-start.1) | collective-permute-done | bytes 524320 | tf_op jit(solution)/shard_map/cond/branch_1_fun/ppermute | solution.py:37
  71.5 2.7 %collective-permute-done.2 = bf16[2,256,512]{2,1,0:T(8,128)(2,1)S(1)} collective-permute-done((bf16[2,256,512]{2,1,0:T(8,128)(2,1)S(1)}, bf16[2,256,512]{2,1,0:T(8,128)(2,1)S(1)}, u32[]{:S(2)}, u32[]{:S(2)}) %collective-permute-start.2) | collective-permute-done | bytes 524320 | tf_op jit(solution)/shard_map/cond/branch_1_fun/ppermute | solution.py:37
  74.1 3.0 %fusion = (bf16[4,256,512]{2,1,0:T(8,128)(2,1)S(1)}, bf16[4,256,512]{2,1,0:T(8,128)(2,1)S(1)}) fusion(bf16[2,256,512]{2,1,0:T(8,128)(2,1)S(1)} %collective-permute-done.2, bf16[4,4,256,512]{3,2,1,0:T(8,128)(2,1)} %get-tuple-element.23, bf16[4,4,256,512]{3,2,1,0:T(8,128)(2,1)} %get-tuple-element.22, bf16[2,256,512]{2,1,0:T(8,128)(2,1)S(1)} %collective-permute-done.1), kind=kLoop, calls=%fused_computation.1 | loop fusion | flops 6291456 | bytes 7340032 | tf_op jit(solution)/shard_map/cond/branch_1_fun/convert_element_type | solution.py:476
  77.2 49.5 %conditional.5 = (f32[256,512]{1,0:T(8,128)S(1)}, bf16[256,512]{1,0:T(8,128)(2,1)S(1)}, bf16[256,512]{1,0:T(8,128)(2,1)S(1)}, bf16[256,512]{1,0:T(8,128)(2,1)S(1)}) conditional(s32[]{:T(128)} %convert_element_type.77, () %tuple.33, (bf16[4,256,512]{2,1,0:T(8,128)(2,1)S(1)}, bf16[4,256,512]{2,1,0:T(8,128)(2,1)S(1)}, ...), branch_computations={%region_4.5_spmd, %region_5.6_spmd} | conditional | flops 3145728 | bytes 17301616 | solution.py:486
  80.5 43.3 %collective-permute-done.3 = bf16[4,256,512]{2,1,0:T(8,128)(2,1)S(1)} collective-permute-done((bf16[4,256,512]{2,1,0:T(8,128)(2,1)S(1)}, bf16[4,256,512]{2,1,0:T(8,128)(2,1)S(1)}, u32[]{:S(2)}, u32[]{:S(2)}) %collective-permute-start.3) | collective-permute-done | bytes 1048608 | tf_op jit(solution)/shard_map/cond/branch_1_fun/ppermute | solution.py:37
  123.8 2.2 %collective-permute-done.4 = bf16[4,256,512]{2,1,0:T(8,128)(2,1)S(1)} collective-permute-done((bf16[4,256,512]{2,1,0:T(8,128)(2,1)S(1)}, bf16[4,256,512]{2,1,0:T(8,128)(2,1)S(1)}, u32[]{:S(2)}, u32[]{:S(2)}) %collective-permute-start.4) | collective-permute-done | bytes 1048608 | tf_op jit(solution)/shard_map/cond/branch_1_fun/ppermute | solution.py:37
  128.4 12.7 %collective-permute-start.13 = (bf16[64,8192]{1,0:T(8,128)(2,1)}, bf16[64,8192]{1,0:T(8,128)(2,1)S(1)}, u32[]{:S(2)}, u32[]{:S(2)}) collective-permute-start(bf16[64,8192]{1,0:T(8,128)(2,1)} %shard_map.103.refs_4_), channel_id=1, source_target_pairs={{64,96},{65,97},{66,98},{67,99},{68,100},{69,101},{70,102},{71,103... | collective-permute-start | bytes 3145736 | tf_op jit(solution)/shard_map/ppermute | solution.py:37
  141.4 17.3 %collective-permute-start.15 = (bf16[256,512]{1,0:T(8,128)(2,1)S(1)}, bf16[256,512]{1,0:T(8,128)(2,1)}, u32[]{:S(2)}, u32[]{:S(2)}) collective-permute-start(bf16[256,512]{1,0:T(8,128)(2,1)S(1)} %get-tuple-element.70), channel_id=1, source_target_pairs={{0,16},{1,17},{2,18},{3,19},{4,20},{5,21},{6,22},{7,23},{8,24},{9,... | collective-permute-start | bytes 786440 | tf_op jit(solution)/shard_map/ppermute | solution.py:37
  158.7 4.8 %collective-permute-done.14.second = bf16[256,512]{1,0:T(8,128)(2,1)S(1)} collective-permute-done((bf16[256,512]{1,0:T(8,128)(2,1)S(1)}, bf16[256,512]{1,0:T(8,128)(2,1)S(1)}, u32[]{:S(2)}, u32[]{:S(2)}) %collective-permute-start.14) | collective-permute-done | bytes 262176 | tf_op jit(solution)/shard_map/ppermute | solution.py:37
  164.3 14.1 %collective-permute-start.16 = (bf16[256,512]{1,0:T(8,128)(2,1)S(1)}, bf16[256,512]{1,0:T(8,128)(2,1)S(1)}, u32[]{:S(2)}, u32[]{:S(2)}) collective-permute-start(bf16[256,512]{1,0:T(8,128)(2,1)S(1)} %get-tuple-element.71), channel_id=1, source_target_pairs={{0,24},{1,25},{2,26},{3,27},{4,28},{5,29},{6,30},{7,31},{8,0},{9,1... | collective-permute-start | bytes 786440 | tf_op jit(solution)/shard_map/ppermute | solution.py:37
  178.4 2.5 %shard_map.98.scale.coefs = f32[8,128]{1,0:T(8,128)} custom-call(s32[4]{0:T(128)S(1)} %pad_add_fusion.place.spot, s32[4]{0:T(128)} %bitcast.47, bf16[32,272,512]{2,1,0:T(8,128)(2,1)} %bitcast.37), custom_call_target="tpu_custom_call" | custom-call | tf_op jit(solution)/shard_map/pallas_call | solution.py:195
  180.9 9.3 %shard_map.99.slopes = bf16[256,8192]{1,0:T(8,128)(2,1)} custom-call(bf16[528,512]{1,0:T(8,128)(2,1)} %shard_map.96.payload, bf16[32,272,512]{2,1,0:T(8,128)(2,1)} %bitcast.38), custom_call_target="tpu_custom_call" | custom-call | tf_op jit(solution)/shard_map/pallas_call | solution.py:344
  191.0 2.3 %shard_map.106 = (bf16[256,512]{1,0:T(8,128)(2,1)}, bf16[1,256]{1,0:T(2,128)(2,1)}) custom-call(f32[8,128]{1,0:T(8,128)} %shard_map.98.scale.coefs, f32[256,512]{1,0:T(8,128)S(1)} %get-tuple-element.65.refs_1_.first, bf16[256,512]{1,0:T(8,128)(2,1)} %copy-done.7, bf16[256,512]{1,0:T(8,128)(2,1)} %collective-permute-done.15.third, ...), custom_call_target="tpu_custom_call" | custom-call | tf_op jit(solution)/shard_map/pallas_call | solution.py:220
  194.5 7.7 %shard_map.104 = bf16[256,8192]{1,0:T(8,128)(2,1)} custom-call(f32[8,128]{1,0:T(8,128)} %shard_map.98.scale.coefs, s32[1]{0:T(128)} %bitcast.20.is_far, bf16[256,8192]{1,0:T(8,128)(2,1)} %shard_map.99.slopes, bf16[256,8192]{1,0:T(8,128)(2,1)} %collective-permute-done.6.refs_0_.refs_3_, bf16[64,8192]{1,0:T(8,128)(2,1)} %collective-permute-done.7.refs_1_, ...), custom_call_target="tpu_custom_call" | custom-call | tf_op jit(solution)/shard_map/pallas_call | solution.py:426
  (56 shorter events, 21.2 us)
Async XLA Ops:
  7.2 171.3 %all-gather.2.cloned.1.call-start = ((), (), s32[]{:S(2)}) async-start(), calls=%async_computation | async-start | bytes 9191424 | tf_op jit(solution)/shard_map/all_gather | solution.py:457
  10.8 16.1 %collective-permute-start.5 = (bf16[528,512]{1,0:T(8,128)(2,1)}, bf16[528,512]{1,0:T(8,128)(2,1)S(1)}, u32[]{:S(2)}, u32[]{:S(2)}) collective-permute-start(bf16[528,512]{1,0:T(8,128)(2,1)} %get-tuple-element.52.payload), channel_id=1, source_target_pairs={{32,0},{33,1},{34,2},{35,3},{36,4},{37,5},{38,6},{39,7},{40,8},{41... | collective-permute-start | bytes 1622024 | tf_op jit(solution)/shard_map/ppermute | solution.py:37
  29.5 111.7 %collective-permute-start.6 = (bf16[256,8192]{1,0:T(8,128)(2,1)}, bf16[256,8192]{1,0:T(8,128)(2,1)}, u32[]{:S(2)}, u32[]{:S(2)}) collective-permute-start(bf16[256,8192]{1,0:T(8,128)(2,1)} %bitcast.40), channel_id=1, source_target_pairs={{32,0},{33,1},{34,2},{35,3},{36,4},{37,5},{38,6},{39,7},{40,8},{41... | collective-permute-start | bytes 12582920 | tf_op jit(solution)/shard_map/ppermute | solution.py:37
  31.9 10.4 %collective-permute-start.10 = (bf16[64,8192]{1,0:T(8,128)(2,1)}, bf16[64,8192]{1,0:T(8,128)(2,1)S(1)}, u32[]{:S(2)}, u32[]{:S(2)}) collective-permute-start(bf16[64,8192]{1,0:T(8,128)(2,1)} %get-tuple-element.58), channel_id=1, source_target_pairs={{128,160},{129,161},{130,162},{131,163},{132,164},{133,165},{134,1... | collective-permute-start | bytes 3145736 | tf_op jit(solution)/shard_map/ppermute | solution.py:37
  32.7 9.6 %collective-permute-start.8 = (bf16[64,8192]{1,0:T(8,128)(2,1)}, bf16[64,8192]{1,0:T(8,128)(2,1)S(1)}, u32[]{:S(2)}, u32[]{:S(2)}) collective-permute-start(bf16[64,8192]{1,0:T(8,128)(2,1)} %get-tuple-element.56), channel_id=1, source_target_pairs={{128,192},{129,193},{130,194},{131,195},{132,196},{133,197},{134,1... | collective-permute-start | bytes 3145736 | tf_op jit(solution)/shard_map/ppermute | solution.py:37
  33.4 8.9 %collective-permute-start.9 = (bf16[64,8192]{1,0:T(8,128)(2,1)}, bf16[64,8192]{1,0:T(8,128)(2,1)S(1)}, u32[]{:S(2)}, u32[]{:S(2)}) collective-permute-start(bf16[64,8192]{1,0:T(8,128)(2,1)} %get-tuple-element.57), channel_id=1, source_target_pairs={{128,224},{129,225},{130,226},{131,227},{132,228},{133,229},{134,2... | collective-permute-start | bytes 3145736 | tf_op jit(solution)/shard_map/ppermute | solution.py:37
  34.2 8.1 %collective-permute-start = (bf16[4,4,256,512]{3,2,1,0:T(8,128)(2,1)}, bf16[4,4,256,512]{3,2,1,0:T(8,128)(2,1)}, u32[]{:S(2)}, u32[]{:S(2)}) collective-permute-start(bf16[4,4,256,512]{3,2,1,0:T(8,128)(2,1)} %get-tuple-element.18), channel_id=1, source_target_pairs={{0,1},{1,0},{2,3},{3,2},{4,5},{5,4},{6,7},{7,6},{8,9},{9,8},{10,11... | collective-permute-start | bytes 12582920 | tf_op jit(solution)/shard_map/cond/branch_1_fun/ppermute | solution.py:37
  42.3 1.1 copy-start.1
  42.3 1.3 copy-start.2
  42.3 1.6 copy-start.3
  44.0 82.7 %collective-permute-start.11 = (bf16[64,8192]{1,0:T(8,128)(2,1)}, bf16[64,8192]{1,0:T(8,128)(2,1)S(1)}, u32[]{:S(2)}, u32[]{:S(2)}) collective-permute-start(bf16[64,8192]{1,0:T(8,128)(2,1)} %shard_map.102), channel_id=1, source_target_pairs={{160,32},{161,33},{162,34},{163,35},{164,36},{165,37},{166,38},{16... | collective-permute-start | bytes 3145736 | tf_op jit(solution)/shard_map/ppermute | solution.py:37
  45.3 147.9 %collective-permute-start.7 = (bf16[64,8192]{1,0:T(8,128)(2,1)}, bf16[64,8192]{1,0:T(8,128)(2,1)}, u32[]{:S(2)}, u32[]{:S(2)}) collective-permute-start(bf16[64,8192]{1,0:T(8,128)(2,1)} %get-tuple-element.55), channel_id=1, source_target_pairs={{128,96},{129,97},{130,98},{131,99},{132,100},{133,101},{134,102},... | collective-permute-start | bytes 3145736 | tf_op jit(solution)/shard_map/ppermute | solution.py:37
  49.8 21.6 %collective-permute-start.1 = (bf16[2,256,512]{2,1,0:T(8,128)(2,1)S(1)}, bf16[2,256,512]{2,1,0:T(8,128)(2,1)S(1)}, u32[]{:S(2)}, u32[]{:S(2)}) collective-permute-start(bf16[2,256,512]{2,1,0:T(8,128)(2,1)S(1)} %get-tuple-element.81), channel_id=1, source_target_pairs={{0,2},{1,3},{2,4},{3,5},{4,6},{5,7},{6,0},{7,1},{8,10},{9,11},{10,... | collective-permute-start | bytes 1572872 | tf_op jit(solution)/shard_map/cond/branch_1_fun/ppermute | solution.py:37
  51.5 22.7 %collective-permute-start.2 = (bf16[2,256,512]{2,1,0:T(8,128)(2,1)S(1)}, bf16[2,256,512]{2,1,0:T(8,128)(2,1)S(1)}, u32[]{:S(2)}, u32[]{:S(2)}) collective-permute-start(bf16[2,256,512]{2,1,0:T(8,128)(2,1)S(1)} %get-tuple-element.80), channel_id=1, source_target_pairs={{0,6},{1,7},{2,0},{3,1},{4,2},{5,3},{6,4},{7,5},{8,14},{9,15},{10,... | collective-permute-start | bytes 1572872 | tf_op jit(solution)/shard_map/cond/branch_1_fun/ppermute | solution.py:37
  77.2 46.6 %collective-permute-start.3 = (bf16[4,256,512]{2,1,0:T(8,128)(2,1)S(1)}, bf16[4,256,512]{2,1,0:T(8,128)(2,1)S(1)}, u32[]{:S(2)}, u32[]{:S(2)}) collective-permute-start(bf16[4,256,512]{2,1,0:T(8,128)(2,1)S(1)} %get-tuple-element.25), channel_id=1, source_target_pairs={{0,2},{1,3},{2,4},{3,5},{4,6},{5,7},{6,0},{7,1},{8,10},{9,11},{10,... | collective-permute-start | bytes 3145736 | tf_op jit(solution)/shard_map/cond/branch_1_fun/ppermute | solution.py:37
  78.9 47.2 %collective-permute-start.4 = (bf16[4,256,512]{2,1,0:T(8,128)(2,1)S(1)}, bf16[4,256,512]{2,1,0:T(8,128)(2,1)S(1)}, u32[]{:S(2)}, u32[]{:S(2)}) collective-permute-start(bf16[4,256,512]{2,1,0:T(8,128)(2,1)S(1)} %get-tuple-element.26), channel_id=1, source_target_pairs={{0,6},{1,7},{2,0},{3,1},{4,2},{5,3},{6,4},{7,5},{8,14},{9,15},{10,... | collective-permute-start | bytes 3145736 | tf_op jit(solution)/shard_map/cond/branch_1_fun/ppermute | solution.py:37
  126.7 1.0 copy-start.4
  127.7 65.6 %collective-permute-start.12 = (bf16[64,8192]{1,0:T(8,128)(2,1)}, bf16[64,8192]{1,0:T(8,128)(2,1)S(1)}, u32[]{:S(2)}, u32[]{:S(2)}) collective-permute-start(bf16[64,8192]{1,0:T(8,128)(2,1)} %shard_map.103.refs_4_), channel_id=1, source_target_pairs={{32,96},{33,97},{34,98},{35,99},{36,100},{37,101},{38,102},{39,103... | collective-permute-start | bytes 3145736 | tf_op jit(solution)/shard_map/ppermute | solution.py:37
  128.4 64.8 %collective-permute-start.13 = (bf16[64,8192]{1,0:T(8,128)(2,1)}, bf16[64,8192]{1,0:T(8,128)(2,1)S(1)}, u32[]{:S(2)}, u32[]{:S(2)}) collective-permute-start(bf16[64,8192]{1,0:T(8,128)(2,1)} %shard_map.103.refs_4_), channel_id=1, source_target_pairs={{64,96},{65,97},{66,98},{67,99},{68,100},{69,101},{70,102},{71,103... | collective-permute-start | bytes 3145736 | tf_op jit(solution)/shard_map/ppermute | solution.py:37
  141.2 22.4 %collective-permute-start.14 = (bf16[256,512]{1,0:T(8,128)(2,1)S(1)}, bf16[256,512]{1,0:T(8,128)(2,1)S(1)}, u32[]{:S(2)}, u32[]{:S(2)}) collective-permute-start(bf16[256,512]{1,0:T(8,128)(2,1)S(1)} %get-tuple-element.69), channel_id=1, source_target_pairs={{0,8},{1,9},{2,10},{3,11},{4,12},{5,13},{6,14},{7,15},{8,16},{9,17... | collective-permute-start | bytes 786440 | tf_op jit(solution)/shard_map/ppermute | solution.py:37
  141.4 48.8 %collective-permute-start.15 = (bf16[256,512]{1,0:T(8,128)(2,1)S(1)}, bf16[256,512]{1,0:T(8,128)(2,1)}, u32[]{:S(2)}, u32[]{:S(2)}) collective-permute-start(bf16[256,512]{1,0:T(8,128)(2,1)S(1)} %get-tuple-element.70), channel_id=1, source_target_pairs={{0,16},{1,17},{2,18},{3,19},{4,20},{5,21},{6,22},{7,23},{8,24},{9,... | collective-permute-start | bytes 786440 | tf_op jit(solution)/shard_map/ppermute | solution.py:37
  164.3 26.0 %collective-permute-start.16 = (bf16[256,512]{1,0:T(8,128)(2,1)S(1)}, bf16[256,512]{1,0:T(8,128)(2,1)S(1)}, u32[]{:S(2)}, u32[]{:S(2)}) collective-permute-start(bf16[256,512]{1,0:T(8,128)(2,1)S(1)} %get-tuple-element.71), channel_id=1, source_target_pairs={{0,24},{1,25},{2,26},{3,27},{4,28},{5,29},{6,30},{7,31},{8,0},{9,1... | collective-permute-start | bytes 786440 | tf_op jit(solution)/shard_map/ppermute | solution.py:37
  193.2 1.0 copy-start.5
  193.3 1.3 copy-start.6
  (3 other events, 2.2 us)
Sparse Core Ops, SparseCore 0:
  29.6 111.0 all-gather.1

commit v4 on v3

--- a/solution.py
+++ b/solution.py
@@ -12,7 +12,7 @@
 AXES = ("section", "dp")
 BF, F32 = jnp.bfloat16, jnp.float32
 BLK = 256
-PIECE = 16
+PIECE = 64
 FREE = pl.CostEstimate(flops=0, bytes_accessed=0, transcendentals=0)
 EXTRA = 16
 QUARTER = 64
@@ -98,9 +98,13 @@
     )(section[None], *sources)
 
 
+def as_column(row):
+    return jnp.broadcast_to(row.astype(F32), (128, row.shape[1])).T[:, :1]
+
+
 def prepare_kernel(place, limits, pairs, weights, gains, keys, ratios, out, mark):
     tokens, kw = keys.shape
-    out[:tokens, :] = (weights[...].astype(F32) * gains[...].astype(F32)).astype(BF)
+    out[:tokens, :] = (weights[...].astype(F32) * as_column(gains[...])).astype(BF)
     limit = limits[place[2]] - place[3]
     valid = lax.broadcasted_iota(jnp.int32, (tokens, kw), 0) < limit
     out[tokens + EXTRA :, :] = jnp.where(valid, keys[...], jnp.zeros_like(keys))
@@ -209,7 +213,7 @@
     total = first[...] * coefs[:1, :1]
     for i, wave in enumerate((second, third, fourth)):
         total += wave[...].astype(F32) * coefs[:1, i + 1 : i + 2]
-    out[...] = (total * gains[...].astype(F32)).astype(BF)
+    out[...] = (total * as_column(gains[...])).astype(BF)
     found = jnp.sum(total * weights[...].astype(F32), axis=1, keepdims=True)
     sums[...] = jnp.broadcast_to(found, (found.shape[0], 128)).T[:1].astype(BF)
 
@@ -330,26 +334,45 @@
     return sum(part.astype(F32) for part in parts)
 
 
-def grad_kernel(payload, weights, out):
-    keys = payload[payload.shape[0] - out.shape[0] :, :]
-    for i in range(weights.shape[0]):
-        out[:, i * BLK : (i + 1) * BLK] = lax.dot_general(
-            keys, weights[i, :BLK], (((1,), (1,)), ((), ())), preferred_element_type=F32
+def grad_kernel(payload, weights, out, held, slopes, in_sem, out_sem):
+    tokens, parts = out.shape[0], in_sem.shape[0]
+    count, rows, kw = held.shape
+    step = count // parts
+    keys = payload[payload.shape[0] - tokens :, :]
+    copies = []
+    for i in range(parts):
+        at = pl.ds(i * step, step)
+        copies.append(
+            pltpu.make_async_copy(weights.at[at, pl.ds(0, rows)], held.at[at], in_sem.at[i])
+        )
+        copies[-1].start()
+    for i in range(parts):
+        copies[i].wait()
+        block = held[i * step : (i + 1) * step].reshape(step * rows, kw)
+        span = pl.ds(i * step * rows, step * rows)
+        slopes[:, span] = lax.dot_general(
+            keys, block, (((1,), (1,)), ((), ())), preferred_element_type=F32
         ).astype(BF)
+        copies[i] = pltpu.make_async_copy(slopes.at[:, span], out.at[:, span], out_sem.at[i])
+        copies[i].start()
+    for copy in copies:
+        copy.wait()
 
 
 def unit_grads(payload, gathered, tokens):
-    count, rows, kw = gathered.shape
-    step = 4
+    count, _, kw = gathered.shape
+    parts = 4
     return pl.pallas_call(
         grad_kernel,
-        grid=(count // step,),
-        in_specs=[
-            pl.BlockSpec(payload.shape, lambda i: (0, 0)),
-            pl.BlockSpec((step, rows, kw), lambda i: (i, 0, 0)),
+        in_specs=[pl.BlockSpec(memory_space=pltpu.VMEM), ANYWHERE],
+        out_specs=ANYWHERE,
+        out_shape=jax.ShapeDtypeStruct((tokens, count * BLK), BF),
+        scratch_shapes=[
+            pltpu.VMEM((count, BLK, kw), BF),
+            pltpu.VMEM((tokens, count * BLK), BF),
+            pltpu.SemaphoreType.DMA((parts,)),
+            pltpu.SemaphoreType.DMA((parts,)),
         ],
-        out_specs=pl.BlockSpec((tokens, step * BLK), lambda i: (0, i)),
-        out_shape=jax.ShapeDtypeStruct((tokens, count * BLK), BF),
         compiler_params=pltpu.CompilerParams(vmem_limit_bytes=VMEM_LIMIT),
         cost_estimate=FREE,
     )(payload, gathered)
@@ -443,10 +466,9 @@
     section, dp = lax.axis_index("section"), lax.axis_index("dp")
     core, y, z = dp % 2, (dp // 2) % 4, dp // 8
     place = jnp.stack([core, y, z, (dp * tokens) % ROW_LEN]).astype(jnp.int32)
-    gains = norm_gain[0][:, None]
 
     payload, mark = prepared(
-        place, lengths[0], pair_of_row[0], weights, gains, key_cotangent[0], token_logratio
+        place, lengths[0], pair_of_row[0], weights, norm_gain, key_cotangent[0], token_logratio
     )
     following = to_previous(payload)
 
@@ -498,7 +520,7 @@
     coefs = coef_table(place, pair_of_row[0], gathered)
     later = gated(plane[1:], [near])
     waves = [plane[0], *[along(wave, i + 1) for i, wave in enumerate(later)]]
-    weight_grad, gain_grad = finished(coefs, waves, gains, weights)
+    weight_grad, gain_grad = finished(coefs, waves, norm_gain, weights)
 
     is_far = (section == 3).astype(jnp.int32)[None]
     out = section_grads(coefs, is_far, slopes, [near], far)

time: 210 us -> 204 us (0.971)
  Pallas kernels: 42.9 us -> 39.1 us
    pallas_call x1, Pallas kernels: 9.31 us -> 6.66 us  [unit_grads(): pl.pallas_call(grad_kernel, in_specs=[pl.BlockSpec(memory_space=pltpu.VME...]
  transfers between devices with their start and end apart: 18 -> 18, of which waited for: 6 -> 6; matrix products, arithmetic and copies ran while one was open for 3% -> 3% of each run, Pallas kernels for 15% -> 14%
where the time goes in v4:
time: 204 us
  waiting for transfers between devices  75.7 us (37%)
  starting transfers between devices  62 us (30%)
  Pallas kernels  39.1 us (19%)
  between operations  14.4 us (7%)
  other arithmetic  6.37 us (3%)
  local copies, waits for them, and re-layouts  6.3 us (3%)
    ppermute x17, waiting for transfers between devices, moved(): return lax.ppermute(value, AXES, pairs)  75.7 us
    ppermute x17, starting transfers between devices, moved(): return lax.ppermute(value, AXES, pairs)  61.9 us
    pallas_call x2, Pallas kernels, term_call(): pl.pallas_call(kernel, in_specs=[pl.BlockSpec(memory_space=pltpu.SMEM), w...  17.4 us
    pallas_call x1, Pallas kernels, unit_grads(): pl.pallas_call(grad_kernel, in_specs=[pl.BlockSpec(memory_space=pltpu.VME...  6.66 us
    pallas_call x1, Pallas kernels, section_grads(): pl.pallas_call(functools.partial(section_kernel, near_rows, far_rows), in...  6.41 us
    unnamed x18, local copies, waits for them, and re-layouts  6.14 us
  transfers between devices with their start and end apart: 18, of which 6 were waited for; matrix products, arithmetic and copies ran while one was open for 3% of the time, Pallas kernels for 14%

profile of v4, /device:TPU:100, one launch (start us, length us, event | category | flops | bytes accessed | tf_op | source)
XLA Modules:
  0.0 203.9 jit_solution(18246440267963100161)
XLA Ops:
  7.3 2.1 %shard_map.94 = (bf16[528,512]{1,0:T(8,128)(2,1)}, bf16[16,512]{1,0:T(8,128)(2,1)}) custom-call(s32[4]{0:T(128)S(1)} %pad_add_fusion.place.spot, s32[4]{0:T(128)} %bitcast.47, s32[4]{0:T(128)} %bitcast.45, bf16[256,512]{1,0:T(8,128)(2,1)} %bitcast.42, bf16[1,256]{1,0:T(2,128)(2,1)} %gains.3, bf16[256,512]{1,0:T(8,128)(2,1)} %bitcast.44, f32[1,256]{1,0:T(1,128)} %ratios.1), custom_call_target="tpu_custom_call" | custom-call | tf_op jit(solution)/shard_map/pallas_call | solution.py:133
  9.4 2.4 %collective-permute-start.5 = (bf16[528,512]{1,0:T(8,128)(2,1)}, bf16[528,512]{1,0:T(8,128)(2,1)S(1)}, u32[]{:S(2)}, u32[]{:S(2)}) collective-permute-start(bf16[528,512]{1,0:T(8,128)(2,1)} %get-tuple-element.52.payload), channel_id=1, source_target_pairs={{32,0},{33,1},{34,2},{35,3},{36,4},{37,5},{38,6},{39,7},{40,8},{41... | collective-permute-start | bytes 1622024 | tf_op jit(solution)/shard_map/ppermute | solution.py:37
  11.8 9.4 %shard_map.95 = (bf16[4,4,256,512]{3,2,1,0:T(8,128)(2,1)}, bf16[64,8192]{1,0:T(8,128)(2,1)}, bf16[64,8192]{1,0:T(8,128)(2,1)}, bf16[64,8192]{1,0:T(8,128)(2,1)},...) custom-call(s32[4]{0:T(128)S(1)} %pad_add_fusion.place.spot, bf16[528,512]{1,0:T(8,128)(2,1)} %get-tuple-element.52.payload, ...), custom_call_target="tpu_custom_call" | custom-call | tf_op jit(solution)/shard_map/pallas_call | solution.py:308
  21.2 4.3 %collective-permute-done.5.refs_0_ = bf16[528,512]{1,0:T(8,128)(2,1)S(1)} collective-permute-done((bf16[528,512]{1,0:T(8,128)(2,1)}, bf16[528,512]{1,0:T(8,128)(2,1)S(1)}, u32[]{:S(2)}, u32[]{:S(2)}) %collective-permute-start.5) | collective-permute-done | bytes 540704 | tf_op jit(solution)/shard_map/ppermute | solution.py:37
  26.3 1.8 shard_map.97.refs_1_
  28.1 2.4 %collective-permute-start.6 = (bf16[256,8192]{1,0:T(8,128)(2,1)}, bf16[256,8192]{1,0:T(8,128)(2,1)}, u32[]{:S(2)}, u32[]{:S(2)}) collective-permute-start(bf16[256,8192]{1,0:T(8,128)(2,1)} %bitcast.39), channel_id=1, source_target_pairs={{32,0},{33,1},{34,2},{35,3},{36,4},{37,5},{38,6},{39,7},{40,8},{41... | collective-permute-start | bytes 12582920 | tf_op jit(solution)/shard_map/ppermute | solution.py:37
  32.8 8.1 %conditional.3 = (bf16[4,4,256,512]{3,2,1,0:T(8,128)(2,1)}, bf16[4,4,256,512]{3,2,1,0:T(8,128)(2,1)}) conditional(s32[]{:T(128)} %convert_element_type.77, () %tuple.31, (bf16[4,4,256,512]{3,2,1,0:T(8,128)(2,1)}, s32[4]{0:T(128)S(1)}, bf16[256,512]{1,0:T(8,128)(2,1)S(1)}, bf16[256,8192]{1,0:T(8,128)(2,1)}) %tuple.51), branch_computations={%region_0.1_spmd, %region_1.2_spmd} | conditional | bytes 16777272 | solution.py:508
  32.9 8.0 %branch_1_fun.1 = bf16[4,4,256,512]{3,2,1,0:T(8,128)(2,1)} custom-call(s32[4]{0:T(128)S(1)} %get-tuple-element.19.spot, bf16[256,512]{1,0:T(8,128)(2,1)S(1)} %get-tuple-element.20.keys, bf16[256,8192]{1,0:T(8,128)(2,1)} %get-tuple-element.21.hidden), custom_call_target="tpu_custom_call" | custom-call | tf_op jit(solution)/shard_map/cond/branch_1_fun/pallas_call | solution.py:308
  45.6 30.2 %conditional.4 = (bf16[4,256,512]{2,1,0:T(8,128)(2,1)S(1)}, bf16[4,256,512]{2,1,0:T(8,128)(2,1)S(1)}, bf16[4,256,512]{2,1,0:T(8,128)(2,1)S(1)}) conditional(s32[]{:T(128)} %convert_element_type.77, () %tuple.34, (bf16[4,4,256,512]{3,2,1,0:T(8,128)(2,1)}, bf16[4,4,256,512]{3,2,1,0:T(8,128)(2,1)}) %tuple.35), branch_computations={%region_2.3_spmd, %region_3.4_spmd} | conditional | flops 10485760 | bytes 19923048 | solution.py:508
  45.6 2.8 %add_convert_fusion = (bf16[1,4,256,512]{3,2,1,0:T(8,128)(2,1)S(1)}, bf16[4,256,512]{2,1,0:T(8,128)(2,1)S(1)}) fusion(bf16[4,4,256,512]{3,2,1,0:T(8,128)(2,1)} %get-tuple-element.23, bf16[4,4,256,512]{3,2,1,0:T(8,128)(2,1)} %get-tuple-element.22), kind=kLoop, calls=%fused_computation.4 | loop fusion | flops 4194304 | bytes 6291456 | tf_op jit(solution)/shard_map/cond/branch_1_fun/convert_element_type | solution.py:494
  51.8 18.2 %collective-permute-done.1 = bf16[2,256,512]{2,1,0:T(8,128)(2,1)S(1)} collective-permute-done((bf16[2,256,512]{2,1,0:T(8,128)(2,1)S(1)}, bf16[2,256,512]{2,1,0:T(8,128)(2,1)S(1)}, u32[]{:S(2)}, u32[]{:S(2)}) %collective-permute-start.1) | collective-permute-done | bytes 524320 | tf_op jit(solution)/shard_map/cond/branch_1_fun/ppermute | solution.py:37
  70.0 2.8 %collective-permute-done.2 = bf16[2,256,512]{2,1,0:T(8,128)(2,1)S(1)} collective-permute-done((bf16[2,256,512]{2,1,0:T(8,128)(2,1)S(1)}, bf16[2,256,512]{2,1,0:T(8,128)(2,1)S(1)}, u32[]{:S(2)}, u32[]{:S(2)}) %collective-permute-start.2) | collective-permute-done | bytes 524320 | tf_op jit(solution)/shard_map/cond/branch_1_fun/ppermute | solution.py:37
  72.8 3.0 %fusion = (bf16[4,256,512]{2,1,0:T(8,128)(2,1)S(1)}, bf16[4,256,512]{2,1,0:T(8,128)(2,1)S(1)}) fusion(bf16[2,256,512]{2,1,0:T(8,128)(2,1)S(1)} %collective-permute-done.2, bf16[4,4,256,512]{3,2,1,0:T(8,128)(2,1)} %get-tuple-element.23, bf16[4,4,256,512]{3,2,1,0:T(8,128)(2,1)} %get-tuple-element.22, bf16[2,256,512]{2,1,0:T(8,128)(2,1)S(1)} %collective-permute-done.1), kind=kLoop, calls=%fused_computation.1 | loop fusion | flops 6291456 | bytes 7340032 | tf_op jit(solution)/shard_map/cond/branch_1_fun/convert_element_type | solution.py:498
  75.8 49.5 %conditional.5 = (f32[256,512]{1,0:T(8,128)S(1)}, bf16[256,512]{1,0:T(8,128)(2,1)S(1)}, bf16[256,512]{1,0:T(8,128)(2,1)S(1)}, bf16[256,512]{1,0:T(8,128)(2,1)S(1)}) conditional(s32[]{:T(128)} %convert_element_type.77, () %tuple.33, (bf16[4,256,512]{2,1,0:T(8,128)(2,1)S(1)}, bf16[4,256,512]{2,1,0:T(8,128)(2,1)S(1)}, ...), branch_computations={%region_4.5_spmd, %region_5.6_spmd} | conditional | flops 3145728 | bytes 17301616 | solution.py:508
  79.1 43.3 %collective-permute-done.3 = bf16[4,256,512]{2,1,0:T(8,128)(2,1)S(1)} collective-permute-done((bf16[4,256,512]{2,1,0:T(8,128)(2,1)S(1)}, bf16[4,256,512]{2,1,0:T(8,128)(2,1)S(1)}, u32[]{:S(2)}, u32[]{:S(2)}) %collective-permute-start.3) | collective-permute-done | bytes 1048608 | tf_op jit(solution)/shard_map/cond/branch_1_fun/ppermute | solution.py:37
  122.5 2.2 %collective-permute-done.4 = bf16[4,256,512]{2,1,0:T(8,128)(2,1)S(1)} collective-permute-done((bf16[4,256,512]{2,1,0:T(8,128)(2,1)S(1)}, bf16[4,256,512]{2,1,0:T(8,128)(2,1)S(1)}, u32[]{:S(2)}, u32[]{:S(2)}) %collective-permute-start.4) | collective-permute-done | bytes 1048608 | tf_op jit(solution)/shard_map/cond/branch_1_fun/ppermute | solution.py:37
  127.0 12.8 %collective-permute-start.13 = (bf16[64,8192]{1,0:T(8,128)(2,1)}, bf16[64,8192]{1,0:T(8,128)(2,1)S(1)}, u32[]{:S(2)}, u32[]{:S(2)}) collective-permute-start(bf16[64,8192]{1,0:T(8,128)(2,1)} %shard_map.103.refs_4_), channel_id=1, source_target_pairs={{64,96},{65,97},{66,98},{67,99},{68,100},{69,101},{70,102},{71,103... | collective-permute-start | bytes 3145736 | tf_op jit(solution)/shard_map/ppermute | solution.py:37
  140.1 17.3 %collective-permute-start.15 = (bf16[256,512]{1,0:T(8,128)(2,1)S(1)}, bf16[256,512]{1,0:T(8,128)(2,1)}, u32[]{:S(2)}, u32[]{:S(2)}) collective-permute-start(bf16[256,512]{1,0:T(8,128)(2,1)S(1)} %get-tuple-element.70), channel_id=1, source_target_pairs={{0,16},{1,17},{2,18},{3,19},{4,20},{5,21},{6,22},{7,23},{8,24},{9,... | collective-permute-start | bytes 786440 | tf_op jit(solution)/shard_map/ppermute | solution.py:37
  157.4 4.8 %collective-permute-done.14.second = bf16[256,512]{1,0:T(8,128)(2,1)S(1)} collective-permute-done((bf16[256,512]{1,0:T(8,128)(2,1)S(1)}, bf16[256,512]{1,0:T(8,128)(2,1)S(1)}, u32[]{:S(2)}, u32[]{:S(2)}) %collective-permute-start.14) | collective-permute-done | bytes 262176 | tf_op jit(solution)/shard_map/ppermute | solution.py:37
  162.9 14.2 %collective-permute-start.16 = (bf16[256,512]{1,0:T(8,128)(2,1)S(1)}, bf16[256,512]{1,0:T(8,128)(2,1)S(1)}, u32[]{:S(2)}, u32[]{:S(2)}) collective-permute-start(bf16[256,512]{1,0:T(8,128)(2,1)S(1)} %get-tuple-element.71), channel_id=1, source_target_pairs={{0,24},{1,25},{2,26},{3,27},{4,28},{5,29},{6,30},{7,31},{8,0},{9,1... | collective-permute-start | bytes 786440 | tf_op jit(solution)/shard_map/ppermute | solution.py:37
  177.1 2.5 %shard_map.98.scale.coefs = f32[8,128]{1,0:T(8,128)} custom-call(s32[4]{0:T(128)S(1)} %pad_add_fusion.place.spot, s32[4]{0:T(128)} %bitcast.46, bf16[32,272,512]{2,1,0:T(8,128)(2,1)} %bitcast.36), custom_call_target="tpu_custom_call" | custom-call | tf_op jit(solution)/shard_map/pallas_call | solution.py:199
  179.6 6.7 %shard_map.99.slopes = bf16[256,8192]{1,0:T(8,128)(2,1)} custom-call(bf16[528,512]{1,0:T(8,128)(2,1)} %shard_map.96.payload, bf16[32,272,512]{2,1,0:T(8,128)(2,1)} %bitcast.37), custom_call_target="tpu_custom_call" | custom-call | tf_op jit(solution)/shard_map/pallas_call | solution.py:365
  187.0 2.3 %shard_map.106 = (bf16[256,512]{1,0:T(8,128)(2,1)}, bf16[1,256]{1,0:T(2,128)(2,1)}) custom-call(f32[8,128]{1,0:T(8,128)} %shard_map.98.scale.coefs, f32[256,512]{1,0:T(8,128)S(1)} %get-tuple-element.65.refs_1_.first, bf16[256,512]{1,0:T(8,128)(2,1)} %copy-done.7, bf16[256,512]{1,0:T(8,128)(2,1)} %collective-permute-done.15.third, ...), custom_call_target="tpu_custom_call" | custom-call | tf_op jit(solution)/shard_map/pallas_call | solution.py:224
  190.6 6.4 %shard_map.104 = bf16[256,8192]{1,0:T(8,128)(2,1)} custom-call(f32[8,128]{1,0:T(8,128)} %shard_map.98.scale.coefs, s32[1]{0:T(128)} %bitcast.19.is_far, bf16[256,8192]{1,0:T(8,128)(2,1)} %shard_map.99.slopes, bf16[256,8192]{1,0:T(8,128)(2,1)} %collective-permute-done.6.refs_0_.refs_3_, bf16[64,8192]{1,0:T(8,128)(2,1)} %collective-permute-done.7.refs_1_, ...), custom_call_target="tpu_custom_call" | custom-call | tf_op jit(solution)/shard_map/pallas_call | solution.py:449
  (55 shorter events, 19.8 us)
Async XLA Ops:
  7.2 169.9 %all-gather.2.cloned.1.call-start = ((), (), s32[]{:S(2)}) async-start(), calls=%async_computation | async-start | bytes 9191424 | tf_op jit(solution)/shard_map/all_gather | solution.py:479
  9.4 16.1 %collective-permute-start.5 = (bf16[528,512]{1,0:T(8,128)(2,1)}, bf16[528,512]{1,0:T(8,128)(2,1)S(1)}, u32[]{:S(2)}, u32[]{:S(2)}) collective-permute-start(bf16[528,512]{1,0:T(8,128)(2,1)} %get-tuple-element.52.payload), channel_id=1, source_target_pairs={{32,0},{33,1},{34,2},{35,3},{36,4},{37,5},{38,6},{39,7},{40,8},{41... | collective-permute-start | bytes 1622024 | tf_op jit(solution)/shard_map/ppermute | solution.py:37
  28.1 111.7 %collective-permute-start.6 = (bf16[256,8192]{1,0:T(8,128)(2,1)}, bf16[256,8192]{1,0:T(8,128)(2,1)}, u32[]{:S(2)}, u32[]{:S(2)}) collective-permute-start(bf16[256,8192]{1,0:T(8,128)(2,1)} %bitcast.39), channel_id=1, source_target_pairs={{32,0},{33,1},{34,2},{35,3},{36,4},{37,5},{38,6},{39,7},{40,8},{41... | collective-permute-start | bytes 12582920 | tf_op jit(solution)/shard_map/ppermute | solution.py:37
  30.6 10.4 %collective-permute-start.10 = (bf16[64,8192]{1,0:T(8,128)(2,1)}, bf16[64,8192]{1,0:T(8,128)(2,1)S(1)}, u32[]{:S(2)}, u32[]{:S(2)}) collective-permute-start(bf16[64,8192]{1,0:T(8,128)(2,1)} %get-tuple-element.58), channel_id=1, source_target_pairs={{128,160},{129,161},{130,162},{131,163},{132,164},{133,165},{134,1... | collective-permute-start | bytes 3145736 | tf_op jit(solution)/shard_map/ppermute | solution.py:37
  31.3 9.6 %collective-permute-start.8 = (bf16[64,8192]{1,0:T(8,128)(2,1)}, bf16[64,8192]{1,0:T(8,128)(2,1)S(1)}, u32[]{:S(2)}, u32[]{:S(2)}) collective-permute-start(bf16[64,8192]{1,0:T(8,128)(2,1)} %get-tuple-element.56), channel_id=1, source_target_pairs={{128,192},{129,193},{130,194},{131,195},{132,196},{133,197},{134,1... | collective-permute-start | bytes 3145736 | tf_op jit(solution)/shard_map/ppermute | solution.py:37
  32.0 8.9 %collective-permute-start.9 = (bf16[64,8192]{1,0:T(8,128)(2,1)}, bf16[64,8192]{1,0:T(8,128)(2,1)S(1)}, u32[]{:S(2)}, u32[]{:S(2)}) collective-permute-start(bf16[64,8192]{1,0:T(8,128)(2,1)} %get-tuple-element.57), channel_id=1, source_target_pairs={{128,224},{129,225},{130,226},{131,227},{132,228},{133,229},{134,2... | collective-permute-start | bytes 3145736 | tf_op jit(solution)/shard_map/ppermute | solution.py:37
  32.8 8.1 %collective-permute-start = (bf16[4,4,256,512]{3,2,1,0:T(8,128)(2,1)}, bf16[4,4,256,512]{3,2,1,0:T(8,128)(2,1)}, u32[]{:S(2)}, u32[]{:S(2)}) collective-permute-start(bf16[4,4,256,512]{3,2,1,0:T(8,128)(2,1)} %get-tuple-element.18), channel_id=1, source_target_pairs={{0,1},{1,0},{2,3},{3,2},{4,5},{5,4},{6,7},{7,6},{8,9},{9,8},{10,11... | collective-permute-start | bytes 12582920 | tf_op jit(solution)/shard_map/cond/branch_1_fun/ppermute | solution.py:37
  40.9 1.1 copy-start.1
  41.0 1.3 copy-start.2
  41.0 1.6 copy-start.3
  42.6 82.7 %collective-permute-start.11 = (bf16[64,8192]{1,0:T(8,128)(2,1)}, bf16[64,8192]{1,0:T(8,128)(2,1)S(1)}, u32[]{:S(2)}, u32[]{:S(2)}) collective-permute-start(bf16[64,8192]{1,0:T(8,128)(2,1)} %shard_map.102), channel_id=1, source_target_pairs={{160,32},{161,33},{162,34},{163,35},{164,36},{165,37},{166,38},{16... | collective-permute-start | bytes 3145736 | tf_op jit(solution)/shard_map/ppermute | solution.py:37
  43.9 145.4 %collective-permute-start.7 = (bf16[64,8192]{1,0:T(8,128)(2,1)}, bf16[64,8192]{1,0:T(8,128)(2,1)}, u32[]{:S(2)}, u32[]{:S(2)}) collective-permute-start(bf16[64,8192]{1,0:T(8,128)(2,1)} %get-tuple-element.55), channel_id=1, source_target_pairs={{128,96},{129,97},{130,98},{131,99},{132,100},{133,101},{134,102},... | collective-permute-start | bytes 3145736 | tf_op jit(solution)/shard_map/ppermute | solution.py:37
  48.5 21.5 %collective-permute-start.1 = (bf16[2,256,512]{2,1,0:T(8,128)(2,1)S(1)}, bf16[2,256,512]{2,1,0:T(8,128)(2,1)S(1)}, u32[]{:S(2)}, u32[]{:S(2)}) collective-permute-start(bf16[2,256,512]{2,1,0:T(8,128)(2,1)S(1)} %get-tuple-element.81), channel_id=1, source_target_pairs={{0,2},{1,3},{2,4},{3,5},{4,6},{5,7},{6,0},{7,1},{8,10},{9,11},{10,... | collective-permute-start | bytes 1572872 | tf_op jit(solution)/shard_map/cond/branch_1_fun/ppermute | solution.py:37
  50.1 22.7 %collective-permute-start.2 = (bf16[2,256,512]{2,1,0:T(8,128)(2,1)S(1)}, bf16[2,256,512]{2,1,0:T(8,128)(2,1)S(1)}, u32[]{:S(2)}, u32[]{:S(2)}) collective-permute-start(bf16[2,256,512]{2,1,0:T(8,128)(2,1)S(1)} %get-tuple-element.80), channel_id=1, source_target_pairs={{0,6},{1,7},{2,0},{3,1},{4,2},{5,3},{6,4},{7,5},{8,14},{9,15},{10,... | collective-permute-start | bytes 1572872 | tf_op jit(solution)/shard_map/cond/branch_1_fun/ppermute | solution.py:37
  75.8 46.6 %collective-permute-start.3 = (bf16[4,256,512]{2,1,0:T(8,128)(2,1)S(1)}, bf16[4,256,512]{2,1,0:T(8,128)(2,1)S(1)}, u32[]{:S(2)}, u32[]{:S(2)}) collective-permute-start(bf16[4,256,512]{2,1,0:T(8,128)(2,1)S(1)} %get-tuple-element.25), channel_id=1, source_target_pairs={{0,2},{1,3},{2,4},{3,5},{4,6},{5,7},{6,0},{7,1},{8,10},{9,11},{10,... | collective-permute-start | bytes 3145736 | tf_op jit(solution)/shard_map/cond/branch_1_fun/ppermute | solution.py:37
  77.5 47.1 %collective-permute-start.4 = (bf16[4,256,512]{2,1,0:T(8,128)(2,1)S(1)}, bf16[4,256,512]{2,1,0:T(8,128)(2,1)S(1)}, u32[]{:S(2)}, u32[]{:S(2)}) collective-permute-start(bf16[4,256,512]{2,1,0:T(8,128)(2,1)S(1)} %get-tuple-element.26), channel_id=1, source_target_pairs={{0,6},{1,7},{2,0},{3,1},{4,2},{5,3},{6,4},{7,5},{8,14},{9,15},{10,... | collective-permute-start | bytes 3145736 | tf_op jit(solution)/shard_map/cond/branch_1_fun/ppermute | solution.py:37
  125.3 1.0 copy-start.4
  126.3 63.0 %collective-permute-start.12 = (bf16[64,8192]{1,0:T(8,128)(2,1)}, bf16[64,8192]{1,0:T(8,128)(2,1)S(1)}, u32[]{:S(2)}, u32[]{:S(2)}) collective-permute-start(bf16[64,8192]{1,0:T(8,128)(2,1)} %shard_map.103.refs_4_), channel_id=1, source_target_pairs={{32,96},{33,97},{34,98},{35,99},{36,100},{37,101},{38,102},{39,103... | collective-permute-start | bytes 3145736 | tf_op jit(solution)/shard_map/ppermute | solution.py:37
  127.0 62.3 %collective-permute-start.13 = (bf16[64,8192]{1,0:T(8,128)(2,1)}, bf16[64,8192]{1,0:T(8,128)(2,1)S(1)}, u32[]{:S(2)}, u32[]{:S(2)}) collective-permute-start(bf16[64,8192]{1,0:T(8,128)(2,1)} %shard_map.103.refs_4_), channel_id=1, source_target_pairs={{64,96},{65,97},{66,98},{67,99},{68,100},{69,101},{70,102},{71,103... | collective-permute-start | bytes 3145736 | tf_op jit(solution)/shard_map/ppermute | solution.py:37
  139.8 22.4 %collective-permute-start.14 = (bf16[256,512]{1,0:T(8,128)(2,1)S(1)}, bf16[256,512]{1,0:T(8,128)(2,1)S(1)}, u32[]{:S(2)}, u32[]{:S(2)}) collective-permute-start(bf16[256,512]{1,0:T(8,128)(2,1)S(1)} %get-tuple-element.69), channel_id=1, source_target_pairs={{0,8},{1,9},{2,10},{3,11},{4,12},{5,13},{6,14},{7,15},{8,16},{9,17... | collective-permute-start | bytes 786440 | tf_op jit(solution)/shard_map/ppermute | solution.py:37
  140.1 46.2 %collective-permute-start.15 = (bf16[256,512]{1,0:T(8,128)(2,1)S(1)}, bf16[256,512]{1,0:T(8,128)(2,1)}, u32[]{:S(2)}, u32[]{:S(2)}) collective-permute-start(bf16[256,512]{1,0:T(8,128)(2,1)S(1)} %get-tuple-element.70), channel_id=1, source_target_pairs={{0,16},{1,17},{2,18},{3,19},{4,20},{5,21},{6,22},{7,23},{8,24},{9,... | collective-permute-start | bytes 786440 | tf_op jit(solution)/shard_map/ppermute | solution.py:37
  162.9 23.4 %collective-permute-start.16 = (bf16[256,512]{1,0:T(8,128)(2,1)S(1)}, bf16[256,512]{1,0:T(8,128)(2,1)S(1)}, u32[]{:S(2)}, u32[]{:S(2)}) collective-permute-start(bf16[256,512]{1,0:T(8,128)(2,1)S(1)} %get-tuple-element.71), channel_id=1, source_target_pairs={{0,24},{1,25},{2,26},{3,27},{4,28},{5,29},{6,30},{7,31},{8,0},{9,1... | collective-permute-start | bytes 786440 | tf_op jit(solution)/shard_map/ppermute | solution.py:37
  189.3 1.0 copy-start.5
  189.3 1.3 copy-start.6
  (3 other events, 2.2 us)
Sparse Core Ops, SparseCore 0:
  28.2 111.0 all-gather.1

commit v5 on v4

--- a/solution.py
+++ b/solution.py
@@ -519,7 +519,10 @@
     slopes = unit_grads(following, gathered, tokens)
     coefs = coef_table(place, pair_of_row[0], gathered)
     later = gated(plane[1:], [near])
-    waves = [plane[0], *[along(wave, i + 1) for i, wave in enumerate(later)]]
+    slopes = gated([slopes], [coefs])[0]
+    first, last = along(later[0], 1), along(later[2], 3)
+    middle = along(gated([later[1]], [slopes])[0], 2)
+    waves = [plane[0], first, middle, last]
     weight_grad, gain_grad = finished(coefs, waves, norm_gain, weights)
 
     is_far = (section == 3).astype(jnp.int32)[None]

time: 204 us -> 198 us (0.971)
  the two profiles are of different devices: /device:TPU:100 before, /device:TPU:38 now
where the time goes in v5:
time: 198 us; the launch traced here: 197 us
  waiting for transfers between devices  101 us (51%)
  Pallas kernels  39.6 us (20%)
  starting transfers between devices  31.2 us (16%)
  between operations  14.4 us (7%)
  other arithmetic  6.4 us (3%)
  local copies, waits for them, and re-layouts  4.57 us (2%)
    ppermute x17, waiting for transfers between devices, moved(): return lax.ppermute(value, AXES, pairs)  101 us
    ppermute x17, starting transfers between devices, moved(): return lax.ppermute(value, AXES, pairs)  31.2 us
    pallas_call x2, Pallas kernels, term_call(): pl.pallas_call(kernel, in_specs=[pl.BlockSpec(memory_space=pltpu.SMEM), w...  17.4 us
    pallas_call x1, Pallas kernels, section_grads(): pl.pallas_call(functools.partial(section_kernel, near_rows, far_rows), in...  6.88 us
    pallas_call x1, Pallas kernels, unit_grads(): pl.pallas_call(grad_kernel, in_specs=[pl.BlockSpec(memory_space=pltpu.VME...  6.67 us
    unnamed x14, local copies, waits for them, and re-layouts  4.41 us
  transfers between devices with their start and end apart: 18, of which 8 were waited for; matrix products, arithmetic and copies ran while one was open for 3% of the time, Pallas kernels for 17%

profile of v5, /device:TPU:38, one launch (start us, length us, event | category | flops | bytes accessed | tf_op | source)
XLA Modules:
  0.0 197.1 jit_solution(8069434227792422659)
XLA Ops:
  7.3 2.0 %shard_map.94 = (bf16[528,512]{1,0:T(8,128)(2,1)}, bf16[16,512]{1,0:T(8,128)(2,1)}) custom-call(s32[4]{0:T(128)S(1)} %pad_add_fusion.place.spot, s32[4]{0:T(128)} %bitcast.47, s32[4]{0:T(128)} %bitcast.45, bf16[256,512]{1,0:T(8,128)(2,1)} %bitcast.42, bf16[1,256]{1,0:T(2,128)(2,1)} %gains.3, bf16[256,512]{1,0:T(8,128)(2,1)} %bitcast.44, f32[1,256]{1,0:T(1,128)} %ratios.1), custom_call_target="tpu_custom_call" | custom-call | tf_op jit(solution)/shard_map/pallas_call | solution.py:133
  9.4 2.7 %collective-permute-start.5 = (bf16[528,512]{1,0:T(8,128)(2,1)}, bf16[528,512]{1,0:T(8,128)(2,1)S(1)}, u32[]{:S(2)}, u32[]{:S(2)}) collective-permute-start(bf16[528,512]{1,0:T(8,128)(2,1)} %get-tuple-element.52.payload), channel_id=1, source_target_pairs={{32,0},{33,1},{34,2},{35,3},{36,4},{37,5},{38,6},{39,7},{40,8},{41... | collective-permute-start | bytes 1622024 | tf_op jit(solution)/shard_map/ppermute | solution.py:37
  12.1 9.4 %shard_map.95 = (bf16[4,4,256,512]{3,2,1,0:T(8,128)(2,1)}, bf16[64,8192]{1,0:T(8,128)(2,1)}, bf16[64,8192]{1,0:T(8,128)(2,1)}, bf16[64,8192]{1,0:T(8,128)(2,1)},...) custom-call(s32[4]{0:T(128)S(1)} %pad_add_fusion.place.spot, bf16[528,512]{1,0:T(8,128)(2,1)} %get-tuple-element.52.payload, ...), custom_call_target="tpu_custom_call" | custom-call | tf_op jit(solution)/shard_map/pallas_call | solution.py:308
  21.5 21.6 %collective-permute-done.5.refs_0_ = bf16[528,512]{1,0:T(8,128)(2,1)S(1)} collective-permute-done((bf16[528,512]{1,0:T(8,128)(2,1)}, bf16[528,512]{1,0:T(8,128)(2,1)S(1)}, u32[]{:S(2)}, u32[]{:S(2)}) %collective-permute-start.5) | collective-permute-done | bytes 540704 | tf_op jit(solution)/shard_map/ppermute | solution.py:37
  43.9 1.8 shard_map.97.refs_1_
  45.7 3.4 %collective-permute-start.6 = (bf16[256,8192]{1,0:T(8,128)(2,1)}, bf16[256,8192]{1,0:T(8,128)(2,1)}, u32[]{:S(2)}, u32[]{:S(2)}) collective-permute-start(bf16[256,8192]{1,0:T(8,128)(2,1)} %bitcast.39), channel_id=1, source_target_pairs={{32,0},{33,1},{34,2},{35,3},{36,4},{37,5},{38,6},{39,7},{40,8},{41... | collective-permute-start | bytes 12582920 | tf_op jit(solution)/shard_map/ppermute | solution.py:37
  51.3 8.1 %conditional.3 = (bf16[4,4,256,512]{3,2,1,0:T(8,128)(2,1)}, bf16[4,4,256,512]{3,2,1,0:T(8,128)(2,1)}) conditional(s32[]{:T(128)} %convert_element_type.77, () %tuple.31, (bf16[4,4,256,512]{3,2,1,0:T(8,128)(2,1)}, s32[4]{0:T(128)S(1)}, bf16[256,512]{1,0:T(8,128)(2,1)S(1)}, bf16[256,8192]{1,0:T(8,128)(2,1)}) %tuple.51), branch_computations={%region_0.1_spmd, %region_1.2_spmd} | conditional | bytes 16777272 | solution.py:508
  51.4 8.0 %branch_1_fun.1 = bf16[4,4,256,512]{3,2,1,0:T(8,128)(2,1)} custom-call(s32[4]{0:T(128)S(1)} %get-tuple-element.19.spot, bf16[256,512]{1,0:T(8,128)(2,1)S(1)} %get-tuple-element.20.keys, bf16[256,8192]{1,0:T(8,128)(2,1)} %get-tuple-element.21.hidden), custom_call_target="tpu_custom_call" | custom-call | tf_op jit(solution)/shard_map/cond/branch_1_fun/pallas_call | solution.py:308
  63.7 21.7 %conditional.4 = (bf16[4,256,512]{2,1,0:T(8,128)(2,1)S(1)}, bf16[4,256,512]{2,1,0:T(8,128)(2,1)S(1)}, bf16[4,256,512]{2,1,0:T(8,128)(2,1)S(1)}) conditional(s32[]{:T(128)} %convert_element_type.77, () %tuple.34, (bf16[4,4,256,512]{3,2,1,0:T(8,128)(2,1)}, bf16[4,4,256,512]{3,2,1,0:T(8,128)(2,1)}) %tuple.35), branch_computations={%region_2.3_spmd, %region_3.4_spmd} | conditional | flops 10485760 | bytes 19923048 | solution.py:508
  63.7 2.9 %add_convert_fusion = (bf16[1,4,256,512]{3,2,1,0:T(8,128)(2,1)S(1)}, bf16[4,256,512]{2,1,0:T(8,128)(2,1)S(1)}) fusion(bf16[4,4,256,512]{3,2,1,0:T(8,128)(2,1)} %get-tuple-element.23, bf16[4,4,256,512]{3,2,1,0:T(8,128)(2,1)} %get-tuple-element.22), kind=kLoop, calls=%fused_computation.4 | loop fusion | flops 4194304 | bytes 6291456 | tf_op jit(solution)/shard_map/cond/branch_1_fun/convert_element_type | solution.py:494
  70.0 12.4 %collective-permute-done.1 = bf16[2,256,512]{2,1,0:T(8,128)(2,1)S(1)} collective-permute-done((bf16[2,256,512]{2,1,0:T(8,128)(2,1)S(1)}, bf16[2,256,512]{2,1,0:T(8,128)(2,1)S(1)}, u32[]{:S(2)}, u32[]{:S(2)}) %collective-permute-start.1) | collective-permute-done | bytes 524320 | tf_op jit(solution)/shard_map/cond/branch_1_fun/ppermute | solution.py:37
  82.5 3.0 %fusion = (bf16[4,256,512]{2,1,0:T(8,128)(2,1)S(1)}, bf16[4,256,512]{2,1,0:T(8,128)(2,1)S(1)}) fusion(bf16[2,256,512]{2,1,0:T(8,128)(2,1)S(1)} %collective-permute-done.2, bf16[4,4,256,512]{3,2,1,0:T(8,128)(2,1)} %get-tuple-element.23, bf16[4,4,256,512]{3,2,1,0:T(8,128)(2,1)} %get-tuple-element.22, bf16[2,256,512]{2,1,0:T(8,128)(2,1)S(1)} %collective-permute-done.1), kind=kLoop, calls=%fused_computation.1 | loop fusion | flops 6291456 | bytes 7340032 | tf_op jit(solution)/shard_map/cond/branch_1_fun/convert_element_type | solution.py:498
  85.5 37.3 %conditional.5 = (f32[256,512]{1,0:T(8,128)S(1)}, bf16[256,512]{1,0:T(8,128)(2,1)S(1)}, bf16[256,512]{1,0:T(8,128)(2,1)S(1)}, bf16[256,512]{1,0:T(8,128)(2,1)S(1)}) conditional(s32[]{:T(128)} %convert_element_type.77, () %tuple.33, (bf16[4,256,512]{2,1,0:T(8,128)(2,1)S(1)}, bf16[4,256,512]{2,1,0:T(8,128)(2,1)S(1)}, ...), branch_computations={%region_4.5_spmd, %region_5.6_spmd} | conditional | flops 3145728 | bytes 17301616 | solution.py:508
  85.5 11.6 %collective-permute-start.3 = (bf16[4,256,512]{2,1,0:T(8,128)(2,1)S(1)}, bf16[4,256,512]{2,1,0:T(8,128)(2,1)S(1)}, u32[]{:S(2)}, u32[]{:S(2)}) collective-permute-start(bf16[4,256,512]{2,1,0:T(8,128)(2,1)S(1)} %get-tuple-element.25), channel_id=1, source_target_pairs={{0,2},{1,3},{2,4},{3,5},{4,6},{5,7},{6,0},{7,1},{8,10},{9,11},{10,... | collective-permute-start | bytes 3145736 | tf_op jit(solution)/shard_map/cond/branch_1_fun/ppermute | solution.py:37
  97.7 22.8 %collective-permute-done.3 = bf16[4,256,512]{2,1,0:T(8,128)(2,1)S(1)} collective-permute-done((bf16[4,256,512]{2,1,0:T(8,128)(2,1)S(1)}, bf16[4,256,512]{2,1,0:T(8,128)(2,1)S(1)}, u32[]{:S(2)}, u32[]{:S(2)}) %collective-permute-start.3) | collective-permute-done | bytes 1048608 | tf_op jit(solution)/shard_map/cond/branch_1_fun/ppermute | solution.py:37
  120.5 1.7 collective-permute-done.4
  122.8 26.5 %collective-permute-done.11.refs_0_ = bf16[64,8192]{1,0:T(8,128)(2,1)S(1)} collective-permute-done((bf16[64,8192]{1,0:T(8,128)(2,1)}, bf16[64,8192]{1,0:T(8,128)(2,1)S(1)}, u32[]{:S(2)}, u32[]{:S(2)}) %collective-permute-start.11) | collective-permute-done | bytes 1048608 | tf_op jit(solution)/shard_map/ppermute | solution.py:37
  153.0 2.0 %collective-permute-start.16 = (bf16[256,512]{1,0:T(8,128)(2,1)S(1)}, bf16[256,512]{1,0:T(8,128)(2,1)}, u32[]{:S(2)}, u32[]{:S(2)}) collective-permute-start(bf16[256,512]{1,0:T(8,128)(2,1)S(1)} %get-tuple-element.71), channel_id=1, source_target_pairs={{0,24},{1,25},{2,26},{3,27},{4,28},{5,29},{6,30},{7,31},{8,0},{9,1... | collective-permute-start | bytes 786440 | tf_op jit(solution)/shard_map/ppermute | solution.py:37
  155.0 6.7 %shard_map.99.refs_0_ = bf16[256,8192]{1,0:T(8,128)(2,1)} custom-call(bf16[528,512]{1,0:T(8,128)(2,1)} %shard_map.96.payload, bf16[32,272,512]{2,1,0:T(8,128)(2,1)} %bitcast.36), custom_call_target="tpu_custom_call" | custom-call | tf_op jit(solution)/shard_map/pallas_call | solution.py:365
  161.7 2.5 %shard_map.98.refs_1_.scale.coefs = f32[8,128]{1,0:T(8,128)} custom-call(s32[4]{0:T(128)S(1)} %pad_add_fusion.place.spot, s32[4]{0:T(128)} %bitcast.46, bf16[32,272,512]{2,1,0:T(8,128)(2,1)} %bitcast.37), custom_call_target="tpu_custom_call" | custom-call | tf_op jit(solution)/shard_map/pallas_call | solution.py:199
  164.3 12.8 %collective-permute-done.12.refs_2_ = bf16[64,8192]{1,0:T(8,128)(2,1)S(1)} collective-permute-done((bf16[64,8192]{1,0:T(8,128)(2,1)}, bf16[64,8192]{1,0:T(8,128)(2,1)S(1)}, u32[]{:S(2)}, u32[]{:S(2)}) %collective-permute-start.12) | collective-permute-done | bytes 1048608 | tf_op jit(solution)/shard_map/ppermute | solution.py:37
  177.1 2.9 %collective-permute-done.13.refs_3_ = bf16[64,8192]{1,0:T(8,128)(2,1)S(1)} collective-permute-done((bf16[64,8192]{1,0:T(8,128)(2,1)}, bf16[64,8192]{1,0:T(8,128)(2,1)S(1)}, u32[]{:S(2)}, u32[]{:S(2)}) %collective-permute-start.13) | collective-permute-done | bytes 1048608 | tf_op jit(solution)/shard_map/ppermute | solution.py:37
  181.0 6.9 %shard_map.105 = bf16[256,8192]{1,0:T(8,128)(2,1)} custom-call(f32[8,128]{1,0:T(8,128)} %shard_map.98.refs_1_.scale.coefs, s32[1]{0:T(128)} %bitcast.19.is_far, bf16[256,8192]{1,0:T(8,128)(2,1)} %shard_map.100.slopes.refs_1_, bf16[256,8192]{1,0:T(8,128)(2,1)} %collective-permute-done.6.refs_0_.refs_3_, bf16[64,8192]{1,0:T(8,128)(2,1)} %collective-permute-done.7.refs_1_, ...), custom_call_target="tpu_custom_call" | custom-call | tf_op jit(solution)/shard_map/pallas_call | solution.py:449
  188.0 2.3 %shard_map.108 = (bf16[256,512]{1,0:T(8,128)(2,1)}, bf16[1,256]{1,0:T(2,128)(2,1)}) custom-call(f32[8,128]{1,0:T(8,128)} %shard_map.98.refs_1_.scale.coefs, f32[256,512]{1,0:T(8,128)S(1)} %get-tuple-element.65.refs_1_.first, bf16[256,512]{1,0:T(8,128)(2,1)} %collective-permute-done.14.second, bf16[256,512]{1,0:T(8,128)(2,1)} %collective-permute-done.15.third, ...), custom_call_target="tpu_custom_call" | custom-call | tf_op jit(solution)/shard_map/pallas_call | solution.py:224
  (53 shorter events, 16.8 us)
Async XLA Ops:
  7.2 147.8 %all-gather.2.cloned.1.call-start = ((), (), s32[]{:S(2)}) async-start(), calls=%async_computation | async-start | bytes 9191424 | tf_op jit(solution)/shard_map/all_gather | solution.py:479
  9.4 33.7 %collective-permute-start.5 = (bf16[528,512]{1,0:T(8,128)(2,1)}, bf16[528,512]{1,0:T(8,128)(2,1)S(1)}, u32[]{:S(2)}, u32[]{:S(2)}) collective-permute-start(bf16[528,512]{1,0:T(8,128)(2,1)} %get-tuple-element.52.payload), channel_id=1, source_target_pairs={{32,0},{33,1},{34,2},{35,3},{36,4},{37,5},{38,6},{39,7},{40,8},{41... | collective-permute-start | bytes 1622024 | tf_op jit(solution)/shard_map/ppermute | solution.py:37
  45.7 107.2 %collective-permute-start.6 = (bf16[256,8192]{1,0:T(8,128)(2,1)}, bf16[256,8192]{1,0:T(8,128)(2,1)}, u32[]{:S(2)}, u32[]{:S(2)}) collective-permute-start(bf16[256,8192]{1,0:T(8,128)(2,1)} %bitcast.39), channel_id=1, source_target_pairs={{32,0},{33,1},{34,2},{35,3},{36,4},{37,5},{38,6},{39,7},{40,8},{41... | collective-permute-start | bytes 12582920 | tf_op jit(solution)/shard_map/ppermute | solution.py:37
  49.1 10.4 %collective-permute-start.10 = (bf16[64,8192]{1,0:T(8,128)(2,1)}, bf16[64,8192]{1,0:T(8,128)(2,1)S(1)}, u32[]{:S(2)}, u32[]{:S(2)}) collective-permute-start(bf16[64,8192]{1,0:T(8,128)(2,1)} %get-tuple-element.58), channel_id=1, source_target_pairs={{128,160},{129,161},{130,162},{131,163},{132,164},{133,165},{134,1... | collective-permute-start | bytes 3145736 | tf_op jit(solution)/shard_map/ppermute | solution.py:37
  49.8 9.7 %collective-permute-start.8 = (bf16[64,8192]{1,0:T(8,128)(2,1)}, bf16[64,8192]{1,0:T(8,128)(2,1)S(1)}, u32[]{:S(2)}, u32[]{:S(2)}) collective-permute-start(bf16[64,8192]{1,0:T(8,128)(2,1)} %get-tuple-element.56), channel_id=1, source_target_pairs={{128,192},{129,193},{130,194},{131,195},{132,196},{133,197},{134,1... | collective-permute-start | bytes 3145736 | tf_op jit(solution)/shard_map/ppermute | solution.py:37
  50.5 8.9 %collective-permute-start.9 = (bf16[64,8192]{1,0:T(8,128)(2,1)}, bf16[64,8192]{1,0:T(8,128)(2,1)S(1)}, u32[]{:S(2)}, u32[]{:S(2)}) collective-permute-start(bf16[64,8192]{1,0:T(8,128)(2,1)} %get-tuple-element.57), channel_id=1, source_target_pairs={{128,224},{129,225},{130,226},{131,227},{132,228},{133,229},{134,2... | collective-permute-start | bytes 3145736 | tf_op jit(solution)/shard_map/ppermute | solution.py:37
  51.3 8.1 %collective-permute-start = (bf16[4,4,256,512]{3,2,1,0:T(8,128)(2,1)}, bf16[4,4,256,512]{3,2,1,0:T(8,128)(2,1)}, u32[]{:S(2)}, u32[]{:S(2)}) collective-permute-start(bf16[4,4,256,512]{3,2,1,0:T(8,128)(2,1)} %get-tuple-element.18), channel_id=1, source_target_pairs={{0,1},{1,0},{2,3},{3,2},{4,5},{5,4},{6,7},{7,6},{8,9},{9,8},{10,11... | collective-permute-start | bytes 12582920 | tf_op jit(solution)/shard_map/cond/branch_1_fun/ppermute | solution.py:37
  59.4 1.1 copy-start.1
  59.5 1.3 copy-start.2
  59.5 1.6 copy-start.3
  61.1 88.1 %collective-permute-start.11 = (bf16[64,8192]{1,0:T(8,128)(2,1)}, bf16[64,8192]{1,0:T(8,128)(2,1)S(1)}, u32[]{:S(2)}, u32[]{:S(2)}) collective-permute-start(bf16[64,8192]{1,0:T(8,128)(2,1)} %shard_map.103), channel_id=1, source_target_pairs={{160,32},{161,33},{162,34},{163,35},{164,36},{165,37},{166,38},{16... | collective-permute-start | bytes 3145736 | tf_op jit(solution)/shard_map/ppermute | solution.py:37
  62.4 101.8 %collective-permute-start.7 = (bf16[64,8192]{1,0:T(8,128)(2,1)}, bf16[64,8192]{1,0:T(8,128)(2,1)}, u32[]{:S(2)}, u32[]{:S(2)}) collective-permute-start(bf16[64,8192]{1,0:T(8,128)(2,1)} %get-tuple-element.55), channel_id=1, source_target_pairs={{128,96},{129,97},{130,98},{131,99},{132,100},{133,101},{134,102},... | collective-permute-start | bytes 3145736 | tf_op jit(solution)/shard_map/ppermute | solution.py:37
  66.7 15.8 %collective-permute-start.1 = (bf16[2,256,512]{2,1,0:T(8,128)(2,1)S(1)}, bf16[2,256,512]{2,1,0:T(8,128)(2,1)S(1)}, u32[]{:S(2)}, u32[]{:S(2)}) collective-permute-start(bf16[2,256,512]{2,1,0:T(8,128)(2,1)S(1)} %get-tuple-element.81), channel_id=1, source_target_pairs={{0,2},{1,3},{2,4},{3,5},{4,6},{5,7},{6,0},{7,1},{8,10},{9,11},{10,... | collective-permute-start | bytes 1572872 | tf_op jit(solution)/shard_map/cond/branch_1_fun/ppermute | solution.py:37
  68.3 14.2 %collective-permute-start.2 = (bf16[2,256,512]{2,1,0:T(8,128)(2,1)S(1)}, bf16[2,256,512]{2,1,0:T(8,128)(2,1)S(1)}, u32[]{:S(2)}, u32[]{:S(2)}) collective-permute-start(bf16[2,256,512]{2,1,0:T(8,128)(2,1)S(1)} %get-tuple-element.80), channel_id=1, source_target_pairs={{0,6},{1,7},{2,0},{3,1},{4,2},{5,3},{6,4},{7,5},{8,14},{9,15},{10,... | collective-permute-start | bytes 1572872 | tf_op jit(solution)/shard_map/cond/branch_1_fun/ppermute | solution.py:37
  85.5 35.0 %collective-permute-start.3 = (bf16[4,256,512]{2,1,0:T(8,128)(2,1)S(1)}, bf16[4,256,512]{2,1,0:T(8,128)(2,1)S(1)}, u32[]{:S(2)}, u32[]{:S(2)}) collective-permute-start(bf16[4,256,512]{2,1,0:T(8,128)(2,1)S(1)} %get-tuple-element.25), channel_id=1, source_target_pairs={{0,2},{1,3},{2,4},{3,5},{4,6},{5,7},{6,0},{7,1},{8,10},{9,11},{10,... | collective-permute-start | bytes 3145736 | tf_op jit(solution)/shard_map/cond/branch_1_fun/ppermute | solution.py:37
  97.1 25.0 %collective-permute-start.4 = (bf16[4,256,512]{2,1,0:T(8,128)(2,1)S(1)}, bf16[4,256,512]{2,1,0:T(8,128)(2,1)S(1)}, u32[]{:S(2)}, u32[]{:S(2)}) collective-permute-start(bf16[4,256,512]{2,1,0:T(8,128)(2,1)S(1)} %get-tuple-element.26), channel_id=1, source_target_pairs={{0,6},{1,7},{2,0},{3,1},{4,2},{5,3},{6,4},{7,5},{8,14},{9,15},{10,... | collective-permute-start | bytes 3145736 | tf_op jit(solution)/shard_map/cond/branch_1_fun/ppermute | solution.py:37
  149.3 1.0 copy-start.4
  150.3 26.9 %collective-permute-start.12 = (bf16[64,8192]{1,0:T(8,128)(2,1)}, bf16[64,8192]{1,0:T(8,128)(2,1)S(1)}, u32[]{:S(2)}, u32[]{:S(2)}) collective-permute-start(bf16[64,8192]{1,0:T(8,128)(2,1)} %shard_map.104.refs_4_), channel_id=1, source_target_pairs={{32,96},{33,97},{34,98},{35,99},{36,100},{37,101},{38,102},{39,103... | collective-permute-start | bytes 3145736 | tf_op jit(solution)/shard_map/ppermute | solution.py:37
  151.6 28.5 %collective-permute-start.13 = (bf16[64,8192]{1,0:T(8,128)(2,1)}, bf16[64,8192]{1,0:T(8,128)(2,1)S(1)}, u32[]{:S(2)}, u32[]{:S(2)}) collective-permute-start(bf16[64,8192]{1,0:T(8,128)(2,1)} %shard_map.104.refs_4_), channel_id=1, source_target_pairs={{64,96},{65,97},{66,98},{67,99},{68,100},{69,101},{70,102},{71,103... | collective-permute-start | bytes 3145736 | tf_op jit(solution)/shard_map/ppermute | solution.py:37
  152.9 35.1 %collective-permute-start.14 = (bf16[256,512]{1,0:T(8,128)(2,1)S(1)}, bf16[256,512]{1,0:T(8,128)(2,1)}, u32[]{:S(2)}, u32[]{:S(2)}) collective-permute-start(bf16[256,512]{1,0:T(8,128)(2,1)S(1)} %get-tuple-element.69), channel_id=1, source_target_pairs={{0,8},{1,9},{2,10},{3,11},{4,12},{5,13},{6,14},{7,15},{8,16},{9,17... | collective-permute-start | bytes 786440 | tf_op jit(solution)/shard_map/ppermute | solution.py:37
  153.0 35.0 %collective-permute-start.16 = (bf16[256,512]{1,0:T(8,128)(2,1)S(1)}, bf16[256,512]{1,0:T(8,128)(2,1)}, u32[]{:S(2)}, u32[]{:S(2)}) collective-permute-start(bf16[256,512]{1,0:T(8,128)(2,1)S(1)} %get-tuple-element.71), channel_id=1, source_target_pairs={{0,24},{1,25},{2,26},{3,27},{4,28},{5,29},{6,30},{7,31},{8,0},{9,1... | collective-permute-start | bytes 786440 | tf_op jit(solution)/shard_map/ppermute | solution.py:37
  164.2 23.7 %collective-permute-start.15 = (bf16[256,512]{1,0:T(8,128)(2,1)S(1)}, bf16[256,512]{1,0:T(8,128)(2,1)}, u32[]{:S(2)}, u32[]{:S(2)}) collective-permute-start(bf16[256,512]{1,0:T(8,128)(2,1)S(1)} %shard_map.107), channel_id=1, source_target_pairs={{0,16},{1,17},{2,18},{3,19},{4,20},{5,21},{6,22},{7,23},{8,24},{9,... | collective-permute-start | bytes 786440 | tf_op jit(solution)/shard_map/ppermute | solution.py:37
  177.1 2.9 %copy-start.5 = (bf16[64,8192]{1,0:T(8,128)(2,1)}, bf16[64,8192]{1,0:T(8,128)(2,1)S(1)}, u32[]{:S(2)}) copy-start(bf16[64,8192]{1,0:T(8,128)(2,1)S(1)} %collective-permute-done.12.refs_2_) | copy-start | bytes 3145732
  180.1 1.0 copy-start.6
  (1 other events, 0.8 us)
Sparse Core Ops, SparseCore 0:
  45.8 98.3 all-gather.1

commit v6 on v5

--- a/solution.py
+++ b/solution.py
@@ -523,10 +523,11 @@
     first, last = along(later[0], 1), along(later[2], 3)
     middle = along(gated([later[1]], [slopes])[0], 2)
     waves = [plane[0], first, middle, last]
-    weight_grad, gain_grad = finished(coefs, waves, norm_gain, weights)
 
     is_far = (section == 3).astype(jnp.int32)[None]
     out = section_grads(coefs, is_far, slopes, [near], far)
+    waves[2] = gated([waves[2]], [out])[0]
+    weight_grad, gain_grad = finished(coefs, waves, norm_gain, weights)
     return out[None], weight_grad[None], gain_grad
 
 

time: 198 us -> 198 us (level)
  no operation moved by 1% of the time
where the time goes in v6:
time: 198 us; the launch traced here: 197 us
  waiting for transfers between devices  101 us (51%)
  Pallas kernels  39.6 us (20%)
  starting transfers between devices  31.3 us (16%)
  between operations  14.4 us (7%)
  other arithmetic  6.4 us (3%)
  local copies, waits for them, and re-layouts  4.57 us (2%)
    ppermute x17, waiting for transfers between devices, moved(): return lax.ppermute(value, AXES, pairs)  101 us
    ppermute x17, starting transfers between devices, moved(): return lax.ppermute(value, AXES, pairs)  31.2 us
    pallas_call x2, Pallas kernels, term_call(): pl.pallas_call(kernel, in_specs=[pl.BlockSpec(memory_space=pltpu.SMEM), w...  17.4 us
    pallas_call x1, Pallas kernels, section_grads(): pl.pallas_call(functools.partial(section_kernel, near_rows, far_rows), in...  6.88 us
    pallas_call x1, Pallas kernels, unit_grads(): pl.pallas_call(grad_kernel, in_specs=[pl.BlockSpec(memory_space=pltpu.VME...  6.68 us
    unnamed x14, local copies, waits for them, and re-layouts  4.41 us
  transfers between devices with their start and end apart: 18, of which 8 were waited for; matrix products, arithmetic and copies ran while one was open for 3% of the time, Pallas kernels for 17%

profile of v6, /device:TPU:38, one launch (start us, length us, event | category | flops | bytes accessed | tf_op | source)
XLA Modules:
  0.0 197.1 jit_solution(11569992238352877755)
XLA Ops:
  7.3 2.0 %shard_map.94 = (bf16[528,512]{1,0:T(8,128)(2,1)}, bf16[16,512]{1,0:T(8,128)(2,1)}) custom-call(s32[4]{0:T(128)S(1)} %pad_add_fusion.place.spot, s32[4]{0:T(128)} %bitcast.47, s32[4]{0:T(128)} %bitcast.45, bf16[256,512]{1,0:T(8,128)(2,1)} %bitcast.42, bf16[1,256]{1,0:T(2,128)(2,1)} %gains.3, bf16[256,512]{1,0:T(8,128)(2,1)} %bitcast.44, f32[1,256]{1,0:T(1,128)} %ratios.1), custom_call_target="tpu_custom_call" | custom-call | tf_op jit(solution)/shard_map/pallas_call | solution.py:133
  9.4 2.7 %collective-permute-start.5 = (bf16[528,512]{1,0:T(8,128)(2,1)}, bf16[528,512]{1,0:T(8,128)(2,1)S(1)}, u32[]{:S(2)}, u32[]{:S(2)}) collective-permute-start(bf16[528,512]{1,0:T(8,128)(2,1)} %get-tuple-element.52.payload), channel_id=1, source_target_pairs={{32,0},{33,1},{34,2},{35,3},{36,4},{37,5},{38,6},{39,7},{40,8},{41... | collective-permute-start | bytes 1622024 | tf_op jit(solution)/shard_map/ppermute | solution.py:37
  12.1 9.4 %shard_map.95 = (bf16[4,4,256,512]{3,2,1,0:T(8,128)(2,1)}, bf16[64,8192]{1,0:T(8,128)(2,1)}, bf16[64,8192]{1,0:T(8,128)(2,1)}, bf16[64,8192]{1,0:T(8,128)(2,1)},...) custom-call(s32[4]{0:T(128)S(1)} %pad_add_fusion.place.spot, bf16[528,512]{1,0:T(8,128)(2,1)} %get-tuple-element.52.payload, ...), custom_call_target="tpu_custom_call" | custom-call | tf_op jit(solution)/shard_map/pallas_call | solution.py:308
  21.5 21.6 %collective-permute-done.5.refs_0_ = bf16[528,512]{1,0:T(8,128)(2,1)S(1)} collective-permute-done((bf16[528,512]{1,0:T(8,128)(2,1)}, bf16[528,512]{1,0:T(8,128)(2,1)S(1)}, u32[]{:S(2)}, u32[]{:S(2)}) %collective-permute-start.5) | collective-permute-done | bytes 540704 | tf_op jit(solution)/shard_map/ppermute | solution.py:37
  43.9 1.8 shard_map.97.refs_1_
  45.7 3.4 %collective-permute-start.6 = (bf16[256,8192]{1,0:T(8,128)(2,1)}, bf16[256,8192]{1,0:T(8,128)(2,1)}, u32[]{:S(2)}, u32[]{:S(2)}) collective-permute-start(bf16[256,8192]{1,0:T(8,128)(2,1)} %bitcast.39), channel_id=1, source_target_pairs={{32,0},{33,1},{34,2},{35,3},{36,4},{37,5},{38,6},{39,7},{40,8},{41... | collective-permute-start | bytes 12582920 | tf_op jit(solution)/shard_map/ppermute | solution.py:37
  51.3 8.1 %conditional.3 = (bf16[4,4,256,512]{3,2,1,0:T(8,128)(2,1)}, bf16[4,4,256,512]{3,2,1,0:T(8,128)(2,1)}) conditional(s32[]{:T(128)} %convert_element_type.77, () %tuple.31, (bf16[4,4,256,512]{3,2,1,0:T(8,128)(2,1)}, s32[4]{0:T(128)S(1)}, bf16[256,512]{1,0:T(8,128)(2,1)S(1)}, bf16[256,8192]{1,0:T(8,128)(2,1)}) %tuple.51), branch_computations={%region_0.1_spmd, %region_1.2_spmd} | conditional | bytes 16777272 | solution.py:508
  51.4 8.0 %branch_1_fun.1 = bf16[4,4,256,512]{3,2,1,0:T(8,128)(2,1)} custom-call(s32[4]{0:T(128)S(1)} %get-tuple-element.19.spot, bf16[256,512]{1,0:T(8,128)(2,1)S(1)} %get-tuple-element.20.keys, bf16[256,8192]{1,0:T(8,128)(2,1)} %get-tuple-element.21.hidden), custom_call_target="tpu_custom_call" | custom-call | tf_op jit(solution)/shard_map/cond/branch_1_fun/pallas_call | solution.py:308
  63.7 21.7 %conditional.4 = (bf16[4,256,512]{2,1,0:T(8,128)(2,1)S(1)}, bf16[4,256,512]{2,1,0:T(8,128)(2,1)S(1)}, bf16[4,256,512]{2,1,0:T(8,128)(2,1)S(1)}) conditional(s32[]{:T(128)} %convert_element_type.77, () %tuple.34, (bf16[4,4,256,512]{3,2,1,0:T(8,128)(2,1)}, bf16[4,4,256,512]{3,2,1,0:T(8,128)(2,1)}) %tuple.35), branch_computations={%region_2.3_spmd, %region_3.4_spmd} | conditional | flops 10485760 | bytes 19923048 | solution.py:508
  63.8 2.9 %add_convert_fusion = (bf16[1,4,256,512]{3,2,1,0:T(8,128)(2,1)S(1)}, bf16[4,256,512]{2,1,0:T(8,128)(2,1)S(1)}) fusion(bf16[4,4,256,512]{3,2,1,0:T(8,128)(2,1)} %get-tuple-element.23, bf16[4,4,256,512]{3,2,1,0:T(8,128)(2,1)} %get-tuple-element.22), kind=kLoop, calls=%fused_computation.4 | loop fusion | flops 4194304 | bytes 6291456 | tf_op jit(solution)/shard_map/cond/branch_1_fun/convert_element_type | solution.py:494
  68.3 1.7 collective-permute-start.2
  70.0 12.4 %collective-permute-done.1 = bf16[2,256,512]{2,1,0:T(8,128)(2,1)S(1)} collective-permute-done((bf16[2,256,512]{2,1,0:T(8,128)(2,1)S(1)}, bf16[2,256,512]{2,1,0:T(8,128)(2,1)S(1)}, u32[]{:S(2)}, u32[]{:S(2)}) %collective-permute-start.1) | collective-permute-done | bytes 524320 | tf_op jit(solution)/shard_map/cond/branch_1_fun/ppermute | solution.py:37
  82.5 2.9 %fusion = (bf16[4,256,512]{2,1,0:T(8,128)(2,1)S(1)}, bf16[4,256,512]{2,1,0:T(8,128)(2,1)S(1)}) fusion(bf16[2,256,512]{2,1,0:T(8,128)(2,1)S(1)} %collective-permute-done.2, bf16[4,4,256,512]{3,2,1,0:T(8,128)(2,1)} %get-tuple-element.23, bf16[4,4,256,512]{3,2,1,0:T(8,128)(2,1)} %get-tuple-element.22, bf16[2,256,512]{2,1,0:T(8,128)(2,1)S(1)} %collective-permute-done.1), kind=kLoop, calls=%fused_computation.1 | loop fusion | flops 6291456 | bytes 7340032 | tf_op jit(solution)/shard_map/cond/branch_1_fun/convert_element_type | solution.py:498
  85.5 37.3 %conditional.5 = (f32[256,512]{1,0:T(8,128)S(1)}, bf16[256,512]{1,0:T(8,128)(2,1)S(1)}, bf16[256,512]{1,0:T(8,128)(2,1)S(1)}, bf16[256,512]{1,0:T(8,128)(2,1)S(1)}) conditional(s32[]{:T(128)} %convert_element_type.77, () %tuple.33, (bf16[4,256,512]{2,1,0:T(8,128)(2,1)S(1)}, bf16[4,256,512]{2,1,0:T(8,128)(2,1)S(1)}, ...), branch_computations={%region_4.5_spmd, %region_5.6_spmd} | conditional | flops 3145728 | bytes 17301616 | solution.py:508
  85.5 11.6 %collective-permute-start.3 = (bf16[4,256,512]{2,1,0:T(8,128)(2,1)S(1)}, bf16[4,256,512]{2,1,0:T(8,128)(2,1)S(1)}, u32[]{:S(2)}, u32[]{:S(2)}) collective-permute-start(bf16[4,256,512]{2,1,0:T(8,128)(2,1)S(1)} %get-tuple-element.25), channel_id=1, source_target_pairs={{0,2},{1,3},{2,4},{3,5},{4,6},{5,7},{6,0},{7,1},{8,10},{9,11},{10,... | collective-permute-start | bytes 3145736 | tf_op jit(solution)/shard_map/cond/branch_1_fun/ppermute | solution.py:37
  97.7 22.8 %collective-permute-done.3 = bf16[4,256,512]{2,1,0:T(8,128)(2,1)S(1)} collective-permute-done((bf16[4,256,512]{2,1,0:T(8,128)(2,1)S(1)}, bf16[4,256,512]{2,1,0:T(8,128)(2,1)S(1)}, u32[]{:S(2)}, u32[]{:S(2)}) %collective-permute-start.3) | collective-permute-done | bytes 1048608 | tf_op jit(solution)/shard_map/cond/branch_1_fun/ppermute | solution.py:37
  122.8 26.5 %collective-permute-done.11.refs_0_ = bf16[64,8192]{1,0:T(8,128)(2,1)S(1)} collective-permute-done((bf16[64,8192]{1,0:T(8,128)(2,1)}, bf16[64,8192]{1,0:T(8,128)(2,1)S(1)}, u32[]{:S(2)}, u32[]{:S(2)}) %collective-permute-start.11) | collective-permute-done | bytes 1048608 | tf_op jit(solution)/shard_map/ppermute | solution.py:37
  153.0 6.7 %shard_map.99.refs_0_ = bf16[256,8192]{1,0:T(8,128)(2,1)} custom-call(bf16[528,512]{1,0:T(8,128)(2,1)} %shard_map.96.payload, bf16[32,272,512]{2,1,0:T(8,128)(2,1)} %bitcast.36), custom_call_target="tpu_custom_call" | custom-call | tf_op jit(solution)/shard_map/pallas_call | solution.py:365
  159.7 2.5 %shard_map.98.refs_1_.scale.coefs = f32[8,128]{1,0:T(8,128)} custom-call(s32[4]{0:T(128)S(1)} %pad_add_fusion.place.spot, s32[4]{0:T(128)} %bitcast.46, bf16[32,272,512]{2,1,0:T(8,128)(2,1)} %bitcast.37), custom_call_target="tpu_custom_call" | custom-call | tf_op jit(solution)/shard_map/pallas_call | solution.py:199
  162.3 2.1 %collective-permute-start.16 = (bf16[256,512]{1,0:T(8,128)(2,1)S(1)}, bf16[256,512]{1,0:T(8,128)(2,1)}, u32[]{:S(2)}, u32[]{:S(2)}) collective-permute-start(bf16[256,512]{1,0:T(8,128)(2,1)S(1)} %get-tuple-element.71), channel_id=1, source_target_pairs={{0,24},{1,25},{2,26},{3,27},{4,28},{5,29},{6,30},{7,31},{8,0},{9,1... | collective-permute-start | bytes 786440 | tf_op jit(solution)/shard_map/ppermute | solution.py:37
  164.4 12.4 %collective-permute-done.12.refs_2_ = bf16[64,8192]{1,0:T(8,128)(2,1)S(1)} collective-permute-done((bf16[64,8192]{1,0:T(8,128)(2,1)}, bf16[64,8192]{1,0:T(8,128)(2,1)S(1)}, u32[]{:S(2)}, u32[]{:S(2)}) %collective-permute-start.12) | collective-permute-done | bytes 1048608 | tf_op jit(solution)/shard_map/ppermute | solution.py:37
  176.8 3.2 %collective-permute-done.13.refs_3_ = bf16[64,8192]{1,0:T(8,128)(2,1)S(1)} collective-permute-done((bf16[64,8192]{1,0:T(8,128)(2,1)}, bf16[64,8192]{1,0:T(8,128)(2,1)S(1)}, u32[]{:S(2)}, u32[]{:S(2)}) %collective-permute-start.13) | collective-permute-done | bytes 1048608 | tf_op jit(solution)/shard_map/ppermute | solution.py:37
  181.0 6.9 %shard_map.105.refs_1_ = bf16[256,8192]{1,0:T(8,128)(2,1)} custom-call(f32[8,128]{1,0:T(8,128)} %shard_map.98.refs_1_.scale.coefs, s32[1]{0:T(128)} %bitcast.19.is_far, bf16[256,8192]{1,0:T(8,128)(2,1)} %shard_map.100.slopes.refs_1_, bf16[256,8192]{1,0:T(8,128)(2,1)} %collective-permute-done.6.refs_0_.refs_3_, ...), custom_call_target="tpu_custom_call" | custom-call | tf_op jit(solution)/shard_map/pallas_call | solution.py:449
  188.0 2.3 %shard_map.109 = (bf16[256,512]{1,0:T(8,128)(2,1)}, bf16[1,256]{1,0:T(2,128)(2,1)}) custom-call(f32[8,128]{1,0:T(8,128)} %shard_map.98.refs_1_.scale.coefs, f32[256,512]{1,0:T(8,128)S(1)} %get-tuple-element.65.refs_1_.first, bf16[256,512]{1,0:T(8,128)(2,1)} %collective-permute-done.14.second, bf16[256,512]{1,0:T(8,128)(2,1)} %shard_map.108.third, ...), custom_call_target="tpu_custom_call" | custom-call | tf_op jit(solution)/shard_map/pallas_call | solution.py:224
  (54 shorter events, 16.9 us)
Async XLA Ops:
  7.2 145.8 %all-gather.2.cloned.1.call-start = ((), (), s32[]{:S(2)}) async-start(), calls=%async_computation | async-start | bytes 9191424 | tf_op jit(solution)/shard_map/all_gather | solution.py:479
  9.4 33.7 %collective-permute-start.5 = (bf16[528,512]{1,0:T(8,128)(2,1)}, bf16[528,512]{1,0:T(8,128)(2,1)S(1)}, u32[]{:S(2)}, u32[]{:S(2)}) collective-permute-start(bf16[528,512]{1,0:T(8,128)(2,1)} %get-tuple-element.52.payload), channel_id=1, source_target_pairs={{32,0},{33,1},{34,2},{35,3},{36,4},{37,5},{38,6},{39,7},{40,8},{41... | collective-permute-start | bytes 1622024 | tf_op jit(solution)/shard_map/ppermute | solution.py:37
  45.7 107.2 %collective-permute-start.6 = (bf16[256,8192]{1,0:T(8,128)(2,1)}, bf16[256,8192]{1,0:T(8,128)(2,1)}, u32[]{:S(2)}, u32[]{:S(2)}) collective-permute-start(bf16[256,8192]{1,0:T(8,128)(2,1)} %bitcast.39), channel_id=1, source_target_pairs={{32,0},{33,1},{34,2},{35,3},{36,4},{37,5},{38,6},{39,7},{40,8},{41... | collective-permute-start | bytes 12582920 | tf_op jit(solution)/shard_map/ppermute | solution.py:37
  49.1 10.4 %collective-permute-start.10 = (bf16[64,8192]{1,0:T(8,128)(2,1)}, bf16[64,8192]{1,0:T(8,128)(2,1)S(1)}, u32[]{:S(2)}, u32[]{:S(2)}) collective-permute-start(bf16[64,8192]{1,0:T(8,128)(2,1)} %get-tuple-element.58), channel_id=1, source_target_pairs={{128,160},{129,161},{130,162},{131,163},{132,164},{133,165},{134,1... | collective-permute-start | bytes 3145736 | tf_op jit(solution)/shard_map/ppermute | solution.py:37
  49.8 9.7 %collective-permute-start.8 = (bf16[64,8192]{1,0:T(8,128)(2,1)}, bf16[64,8192]{1,0:T(8,128)(2,1)S(1)}, u32[]{:S(2)}, u32[]{:S(2)}) collective-permute-start(bf16[64,8192]{1,0:T(8,128)(2,1)} %get-tuple-element.56), channel_id=1, source_target_pairs={{128,192},{129,193},{130,194},{131,195},{132,196},{133,197},{134,1... | collective-permute-start | bytes 3145736 | tf_op jit(solution)/shard_map/ppermute | solution.py:37
  50.5 8.9 %collective-permute-start.9 = (bf16[64,8192]{1,0:T(8,128)(2,1)}, bf16[64,8192]{1,0:T(8,128)(2,1)S(1)}, u32[]{:S(2)}, u32[]{:S(2)}) collective-permute-start(bf16[64,8192]{1,0:T(8,128)(2,1)} %get-tuple-element.57), channel_id=1, source_target_pairs={{128,224},{129,225},{130,226},{131,227},{132,228},{133,229},{134,2... | collective-permute-start | bytes 3145736 | tf_op jit(solution)/shard_map/ppermute | solution.py:37
  51.3 8.1 %collective-permute-start = (bf16[4,4,256,512]{3,2,1,0:T(8,128)(2,1)}, bf16[4,4,256,512]{3,2,1,0:T(8,128)(2,1)}, u32[]{:S(2)}, u32[]{:S(2)}) collective-permute-start(bf16[4,4,256,512]{3,2,1,0:T(8,128)(2,1)} %get-tuple-element.18), channel_id=1, source_target_pairs={{0,1},{1,0},{2,3},{3,2},{4,5},{5,4},{6,7},{7,6},{8,9},{9,8},{10,11... | collective-permute-start | bytes 12582920 | tf_op jit(solution)/shard_map/cond/branch_1_fun/ppermute | solution.py:37
  59.4 1.1 copy-start.1
  59.5 1.3 copy-start.2
  59.5 1.6 copy-start.3
  61.1 88.1 %collective-permute-start.11 = (bf16[64,8192]{1,0:T(8,128)(2,1)}, bf16[64,8192]{1,0:T(8,128)(2,1)S(1)}, u32[]{:S(2)}, u32[]{:S(2)}) collective-permute-start(bf16[64,8192]{1,0:T(8,128)(2,1)} %shard_map.103), channel_id=1, source_target_pairs={{160,32},{161,33},{162,34},{163,35},{164,36},{165,37},{166,38},{16... | collective-permute-start | bytes 3145736 | tf_op jit(solution)/shard_map/ppermute | solution.py:37
  62.4 99.9 %collective-permute-start.7 = (bf16[64,8192]{1,0:T(8,128)(2,1)}, bf16[64,8192]{1,0:T(8,128)(2,1)}, u32[]{:S(2)}, u32[]{:S(2)}) collective-permute-start(bf16[64,8192]{1,0:T(8,128)(2,1)} %get-tuple-element.55), channel_id=1, source_target_pairs={{128,96},{129,97},{130,98},{131,99},{132,100},{133,101},{134,102},... | collective-permute-start | bytes 3145736 | tf_op jit(solution)/shard_map/ppermute | solution.py:37
  66.7 15.7 %collective-permute-start.1 = (bf16[2,256,512]{2,1,0:T(8,128)(2,1)S(1)}, bf16[2,256,512]{2,1,0:T(8,128)(2,1)S(1)}, u32[]{:S(2)}, u32[]{:S(2)}) collective-permute-start(bf16[2,256,512]{2,1,0:T(8,128)(2,1)S(1)} %get-tuple-element.81), channel_id=1, source_target_pairs={{0,2},{1,3},{2,4},{3,5},{4,6},{5,7},{6,0},{7,1},{8,10},{9,11},{10,... | collective-permute-start | bytes 1572872 | tf_op jit(solution)/shard_map/cond/branch_1_fun/ppermute | solution.py:37
  68.3 14.2 %collective-permute-start.2 = (bf16[2,256,512]{2,1,0:T(8,128)(2,1)S(1)}, bf16[2,256,512]{2,1,0:T(8,128)(2,1)S(1)}, u32[]{:S(2)}, u32[]{:S(2)}) collective-permute-start(bf16[2,256,512]{2,1,0:T(8,128)(2,1)S(1)} %get-tuple-element.80), channel_id=1, source_target_pairs={{0,6},{1,7},{2,0},{3,1},{4,2},{5,3},{6,4},{7,5},{8,14},{9,15},{10,... | collective-permute-start | bytes 1572872 | tf_op jit(solution)/shard_map/cond/branch_1_fun/ppermute | solution.py:37
  85.5 35.0 %collective-permute-start.3 = (bf16[4,256,512]{2,1,0:T(8,128)(2,1)S(1)}, bf16[4,256,512]{2,1,0:T(8,128)(2,1)S(1)}, u32[]{:S(2)}, u32[]{:S(2)}) collective-permute-start(bf16[4,256,512]{2,1,0:T(8,128)(2,1)S(1)} %get-tuple-element.25), channel_id=1, source_target_pairs={{0,2},{1,3},{2,4},{3,5},{4,6},{5,7},{6,0},{7,1},{8,10},{9,11},{10,... | collective-permute-start | bytes 3145736 | tf_op jit(solution)/shard_map/cond/branch_1_fun/ppermute | solution.py:37
  97.1 25.1 %collective-permute-start.4 = (bf16[4,256,512]{2,1,0:T(8,128)(2,1)S(1)}, bf16[4,256,512]{2,1,0:T(8,128)(2,1)S(1)}, u32[]{:S(2)}, u32[]{:S(2)}) collective-permute-start(bf16[4,256,512]{2,1,0:T(8,128)(2,1)S(1)} %get-tuple-element.26), channel_id=1, source_target_pairs={{0,6},{1,7},{2,0},{3,1},{4,2},{5,3},{6,4},{7,5},{8,14},{9,15},{10,... | collective-permute-start | bytes 3145736 | tf_op jit(solution)/shard_map/cond/branch_1_fun/ppermute | solution.py:37
  149.3 1.0 copy-start.4
  150.3 26.5 %collective-permute-start.12 = (bf16[64,8192]{1,0:T(8,128)(2,1)}, bf16[64,8192]{1,0:T(8,128)(2,1)S(1)}, u32[]{:S(2)}, u32[]{:S(2)}) collective-permute-start(bf16[64,8192]{1,0:T(8,128)(2,1)} %shard_map.104.refs_4_), channel_id=1, source_target_pairs={{32,96},{33,97},{34,98},{35,99},{36,100},{37,101},{38,102},{39,103... | collective-permute-start | bytes 3145736 | tf_op jit(solution)/shard_map/ppermute | solution.py:37
  151.6 28.5 %collective-permute-start.13 = (bf16[64,8192]{1,0:T(8,128)(2,1)}, bf16[64,8192]{1,0:T(8,128)(2,1)S(1)}, u32[]{:S(2)}, u32[]{:S(2)}) collective-permute-start(bf16[64,8192]{1,0:T(8,128)(2,1)} %shard_map.104.refs_4_), channel_id=1, source_target_pairs={{64,96},{65,97},{66,98},{67,99},{68,100},{69,101},{70,102},{71,103... | collective-permute-start | bytes 3145736 | tf_op jit(solution)/shard_map/ppermute | solution.py:37
  152.9 35.1 %collective-permute-start.14 = (bf16[256,512]{1,0:T(8,128)(2,1)S(1)}, bf16[256,512]{1,0:T(8,128)(2,1)}, u32[]{:S(2)}, u32[]{:S(2)}) collective-permute-start(bf16[256,512]{1,0:T(8,128)(2,1)S(1)} %get-tuple-element.69), channel_id=1, source_target_pairs={{0,8},{1,9},{2,10},{3,11},{4,12},{5,13},{6,14},{7,15},{8,16},{9,17... | collective-permute-start | bytes 786440 | tf_op jit(solution)/shard_map/ppermute | solution.py:37
  162.2 25.7 %collective-permute-start.15 = (bf16[256,512]{1,0:T(8,128)(2,1)S(1)}, bf16[256,512]{1,0:T(8,128)(2,1)}, u32[]{:S(2)}, u32[]{:S(2)}) collective-permute-start(bf16[256,512]{1,0:T(8,128)(2,1)S(1)} %shard_map.107), channel_id=1, source_target_pairs={{0,16},{1,17},{2,18},{3,19},{4,20},{5,21},{6,22},{7,23},{8,24},{9,... | collective-permute-start | bytes 786440 | tf_op jit(solution)/shard_map/ppermute | solution.py:37
  162.3 25.6 %collective-permute-start.16 = (bf16[256,512]{1,0:T(8,128)(2,1)S(1)}, bf16[256,512]{1,0:T(8,128)(2,1)}, u32[]{:S(2)}, u32[]{:S(2)}) collective-permute-start(bf16[256,512]{1,0:T(8,128)(2,1)S(1)} %get-tuple-element.71), channel_id=1, source_target_pairs={{0,24},{1,25},{2,26},{3,27},{4,28},{5,29},{6,30},{7,31},{8,0},{9,1... | collective-permute-start | bytes 786440 | tf_op jit(solution)/shard_map/ppermute | solution.py:37
  176.8 3.2 %copy-start.5 = (bf16[64,8192]{1,0:T(8,128)(2,1)}, bf16[64,8192]{1,0:T(8,128)(2,1)S(1)}, u32[]{:S(2)}) copy-start(bf16[64,8192]{1,0:T(8,128)(2,1)S(1)} %collective-permute-done.12.refs_2_) | copy-start | bytes 3145732
  180.1 1.0 copy-start.6
  (1 other events, 0.8 us)
Sparse Core Ops, SparseCore 0:
  45.8 98.4 all-gather.1
